TPU v7x, 32 devices: a whole 2x2x4 slice. The times are simulated.
32 devices in a mesh: dp: 16 (over z, x, core), tensor: 2 (over y).
Axes of the slice: x: 2, y: 2, z: 4, core: 2. Of those that a mesh axis runs over, the one named last changes fastest.
Arguments:
- inputs: float32 [512, 64, 768], P('tensor', 'dp'), may hold values from -6 to 6
- lengths: int32 [64], P('dp'), may hold values from 128 to 512, as said below
- query_weight: bfloat16 [768, 768], P('dp', 'tensor'), may hold values from -0.21875 to 0.21875
- key_weight: bfloat16 [768, 768], P('dp', 'tensor'), may hold values from -0.21875 to 0.21875
- value_weight: bfloat16 [768, 768], P('dp', 'tensor'), may hold values from -0.21875 to 0.21875
- query_bias: float32 [768], replicated, may hold values from -3 to 3
- value_bias: float32 [768], replicated, may hold values from -3 to 3
- out_weight: bfloat16 [768, 768], P('tensor', 'dp'), may hold values from -1.75 to 1.75
- out_bias: float32 [768], replicated, may hold values from -3 to 3
- first_gain: float32 [768], replicated, may hold values from 0.25 to 1.75
- first_shift: float32 [768], replicated, may hold values from -2 to 2
- input_projection_weight: bfloat16 [768, 3072], P('dp', 'tensor'), may hold values from -0.21875 to 0.21875
- input_projection_bias: float32 [3072], replicated, may hold values from -3 to 3
- output_projection_weight: bfloat16 [3072, 768], P('tensor', 'dp'), may hold values from -0.109375 to 0.109375
- output_projection_bias: float32 [768], replicated, may hold values from -3 to 3
- second_gain: float32 [768], replicated, may hold values from 0.25 to 1.75
- second_shift: float32 [768], replicated, may hold values from -2 to 2
- out_cotangent: float32 [512, 64, 768], P('tensor', 'dp'), may hold values from -6 to 6
Outputs:
- outputs: float32 [512, 64, 768], P('tensor', 'dp')
- input_grad: float32 [512, 64, 768], P('tensor', 'dp')
- query_weight_grad: float32 [768, 768], P('dp', 'tensor')
- key_weight_grad: float32 [768, 768], P('dp', 'tensor')
- value_weight_grad: float32 [768, 768], P('dp', 'tensor')
- query_bias_grad: float32 [768], replicated
- value_bias_grad: float32 [768], replicated
- out_weight_grad: float32 [768, 768], P('tensor', 'dp')
- out_bias_grad: float32 [768], replicated
- first_gain_grad: float32 [768], replicated
- first_shift_grad: float32 [768], replicated
- up_weight_grad: float32 [768, 3072], P('dp', 'tensor')
- up_bias_grad: float32 [3072], replicated
- down_weight_grad: float32 [3072, 768], P('tensor', 'dp')
- down_bias_grad: float32 [768], replicated
- second_gain_grad: float32 [768], replicated
- second_shift_grad: float32 [768], replicated
Inputs may be any that keep to these rules, and one draw needn't show every extreme that they name: `lengths`: valid positions of each sequence. In every aligned block of 4 sequences one, at a drawn place, has more than 448 valid positions; one sequence of all, at a drawn place, has exactly 512.
All inputs are finite; a program needn't handle non-finite values.
Results may differ from a plain program's by a relative error of at most 0.017.
Values may be sent and summed in bfloat16 or wider, within the bound.
No kernel may reach another device: no remote copies, remote signals or barrier semaphores. Data moves between devices by JAX's collectives and lax.ppermute only.
A program may use at most 192 MiB of HBM per device.

v0:
```python
import jax
import jax.numpy as jnp
from jax import lax
from jax.sharding import PartitionSpec as P

D = 768
H = 12
HD = 64
FF = 3072


NORM_EPSILON = 1e-12


def layer_norm(resid, gain_vec, shift_vec):
    mean_value = jnp.mean(resid, -1, keepdims=True)
    centred = resid - mean_value
    variance = jnp.mean(centred * centred, -1, keepdims=True)
    inv_std = lax.rsqrt(variance + NORM_EPSILON)
    normed = centred * inv_std
    return (normed * gain_vec + shift_vec, normed, inv_std)


def norm_back(grad_in, normed, inv_std, gain_vec):
    scaled = grad_in * gain_vec
    return inv_std * (
        scaled
        - jnp.mean(scaled, -1, keepdims=True)
        - normed * jnp.mean(scaled * normed, -1, keepdims=True)
    )


def gelu_exact(values_in):
    return jax.nn.gelu(values_in, approximate=False)


def masked_scores(query_seq, key_seq, key_valid):
    scores = jnp.einsum(
        "qhd,khd->hqk", query_seq, key_seq, preferred_element_type=jnp.float32
    ) * HD ** (-0.5)
    return jnp.where(key_valid[None, None, :], scores, -1e30)


def attend_forward(packed):
    query_seq, key_seq, value_seq, key_valid = packed
    scores = masked_scores(query_seq, key_seq, key_valid)
    maxima = jnp.max(scores, -1, keepdims=True)
    exponent = jnp.exp(scores - maxima)
    denom_sum = jnp.sum(exponent, -1, keepdims=True)
    soft_weights = exponent / denom_sum
    context = jnp.einsum(
        "hqk,khd->qhd",
        soft_weights.astype(jnp.bfloat16),
        value_seq,
        preferred_element_type=jnp.float32,
    )
    return (
        context.reshape(context.shape[0], -1).astype(jnp.bfloat16),
        (maxima + jnp.log(denom_sum))[..., 0],
    )


def attend_backward(packed):
    query_seq, key_seq, value_seq, key_valid, log_sums, context_grad = packed
    scores = masked_scores(query_seq, key_seq, key_valid)
    soft_weights = jnp.exp(scores - log_sums[..., None])
    weight_grad = jnp.einsum(
        "qhd,khd->hqk", context_grad, value_seq, preferred_element_type=jnp.float32
    )
    row_dot = jnp.sum(soft_weights * weight_grad, -1, keepdims=True)
    score_grad = (soft_weights * (weight_grad - row_dot)).astype(jnp.bfloat16)
    query_grad = jnp.einsum(
        "hqk,khd->qhd", score_grad, key_seq, preferred_element_type=jnp.float32
    ) * HD ** (-0.5)
    key_grad = jnp.einsum(
        "hqk,qhd->khd", score_grad, query_seq, preferred_element_type=jnp.float32
    ) * HD ** (-0.5)
    value_grad = jnp.einsum(
        "hqk,qhd->khd",
        soft_weights.astype(jnp.bfloat16),
        context_grad,
        preferred_element_type=jnp.float32,
    )
    length = query_seq.shape[0]
    return (
        query_grad.reshape(length, -1).astype(jnp.bfloat16),
        key_grad.reshape(length, -1).astype(jnp.bfloat16),
        value_grad.reshape(length, -1).astype(jnp.bfloat16),
    )


def embed(part_vec, total, offset):
    return lax.dynamic_update_slice_in_dim(jnp.zeros((total,), jnp.float32), part_vec, offset, 0)


def shards(
    inputs,
    lengths,
    query_weight,
    key_weight,
    value_weight,
    query_bias,
    value_bias,
    out_weight,
    out_bias,
    first_gain,
    first_shift,
    input_projection_weight,
    input_projection_bias,
    output_projection_weight,
    output_projection_bias,
    second_gain,
    second_shift,
    out_cotangent,
):
    tensor_index = lax.axis_index("tensor")
    tensor_size = lax.axis_size("tensor")
    head_width = D // tensor_size
    hidden_width = FF // tensor_size
    heads_local = H // tensor_size
    half_rows = inputs.shape[0]
    seq_count = inputs.shape[1]
    length = half_rows * tensor_size
    head_shape = (seq_count, length, heads_local, HD)
    query_full, key_full, value_full, out_full, up_projection_gathered, down_projection_gathered = (
        lax.all_gather(query_weight, "dp", axis=0, tiled=True),
        lax.all_gather(key_weight, "dp", axis=0, tiled=True),
        lax.all_gather(value_weight, "dp", axis=0, tiled=True),
        lax.all_gather(out_weight, "dp", axis=1, tiled=True),
        lax.all_gather(input_projection_weight, "dp", axis=0, tiled=True),
        lax.all_gather(output_projection_weight, "dp", axis=1, tiled=True),
    )
    query_slice = lax.dynamic_slice_in_dim(query_bias, tensor_index * head_width, head_width)
    value_slice = lax.dynamic_slice_in_dim(value_bias, tensor_index * head_width, head_width)
    up_slice = lax.dynamic_slice_in_dim(
        input_projection_bias, tensor_index * hidden_width, hidden_width
    )
    rows_low = inputs.astype(jnp.bfloat16)
    rows_all = lax.all_gather(rows_low, "tensor", axis=0, tiled=True)
    queries = (
        jnp.einsum("lsd,dc->slc", rows_all, query_full, preferred_element_type=jnp.float32)
        + query_slice
    ).astype(jnp.bfloat16)
    keys_low = jnp.einsum(
        "lsd,dc->slc", rows_all, key_full, preferred_element_type=jnp.float32
    ).astype(jnp.bfloat16)
    values_low = (
        jnp.einsum("lsd,dc->slc", rows_all, value_full, preferred_element_type=jnp.float32)
        + value_slice
    ).astype(jnp.bfloat16)
    query_heads = queries.reshape(head_shape)
    key_heads = keys_low.reshape(head_shape)
    value_heads = values_low.reshape(head_shape)
    key_valid = jnp.arange(length, dtype=jnp.int32)[None, :] < lengths[:, None]
    context, log_sums = lax.map(attend_forward, (query_heads, key_heads, value_heads, key_valid))
    block_row_span = context
    attention = lax.psum_scatter(
        jnp.einsum(
            "slc,cd->lsd", block_row_span, out_full, preferred_element_type=jnp.float32
        ).astype(jnp.bfloat16),
        "tensor",
        scatter_dimension=0,
        tiled=True,
    ).astype(jnp.float32)
    hidden, normed_one, inv_one = layer_norm(inputs + attention + out_bias, first_gain, first_shift)
    hidden_reduced_precision = hidden.astype(jnp.bfloat16)
    hidden_gathered = lax.all_gather(hidden_reduced_precision, "tensor", axis=0, tiled=True)
    hidden_preactivation = (
        jnp.einsum(
            "zhx,xm->zhm",
            hidden_gathered,
            up_projection_gathered,
            preferred_element_type=jnp.float32,
        )
        + up_slice
    )
    hidden_activation = gelu_exact(hidden_preactivation).astype(jnp.bfloat16)
    block_row_span = hidden_activation
    feedforward_branch = lax.psum_scatter(
        jnp.einsum(
            "kng,gw->knw",
            block_row_span,
            down_projection_gathered,
            preferred_element_type=jnp.float32,
        ).astype(jnp.bfloat16),
        "tensor",
        scatter_dimension=0,
        tiled=True,
    ).astype(jnp.float32)
    outputs, normed_two, inv_two = layer_norm(
        hidden + feedforward_branch + output_projection_bias, second_gain, second_shift
    )
    second_grad = norm_back(out_cotangent, normed_two, inv_two, second_gain)
    second_gain_part = jnp.sum(out_cotangent * normed_two, axis=(0, 1))
    second_shift_part = jnp.sum(out_cotangent, axis=(0, 1))
    down_bias_part = jnp.sum(second_grad, axis=(0, 1))
    query_back, key_back, value_back, out_back, up_projection_backward, down_projection_backward = (
        lax.all_gather(query_weight, "dp", axis=0, tiled=True),
        lax.all_gather(key_weight, "dp", axis=0, tiled=True),
        lax.all_gather(value_weight, "dp", axis=0, tiled=True),
        lax.all_gather(out_weight, "dp", axis=1, tiled=True),
        lax.all_gather(input_projection_weight, "dp", axis=0, tiled=True),
        lax.all_gather(output_projection_weight, "dp", axis=1, tiled=True),
    )
    second_low = second_grad.astype(jnp.bfloat16)
    second_norm_gathered = lax.all_gather(second_low, "tensor", axis=0, tiled=True)
    activation_gradient = jnp.einsum(
        "mkx,wx->mkw",
        second_norm_gathered,
        down_projection_backward,
        preferred_element_type=jnp.float32,
    )
    preactivation_gradient = jax.vjp(gelu_exact, hidden_preactivation)[1](activation_gradient)[
        0
    ].astype(jnp.bfloat16)
    down_weight_part = jnp.einsum(
        "ayw,ayv->wv", hidden_activation, second_norm_gathered, preferred_element_type=jnp.float32
    )
    up_weight_part = jnp.einsum(
        "irj,iro->jo", hidden_gathered, preactivation_gradient, preferred_element_type=jnp.float32
    )
    up_bias_part = jnp.sum(preactivation_gradient, axis=(0, 1), dtype=jnp.float32)
    block_row_span = preactivation_gradient
    hidden_grad = second_grad + lax.psum_scatter(
        jnp.einsum(
            "hky,ty->hkt",
            block_row_span,
            up_projection_backward,
            preferred_element_type=jnp.float32,
        ).astype(jnp.bfloat16),
        "tensor",
        scatter_dimension=0,
        tiled=True,
    ).astype(jnp.float32)
    first_grad = norm_back(hidden_grad, normed_one, inv_one, first_gain)
    first_gain_part = jnp.sum(hidden_grad * normed_one, axis=(0, 1))
    first_shift_part = jnp.sum(hidden_grad, axis=(0, 1))
    out_bias_part = jnp.sum(first_grad, axis=(0, 1))
    first_low = first_grad.astype(jnp.bfloat16)
    first_all = lax.all_gather(first_low, "tensor", axis=0, tiled=True)
    context_grad = jnp.einsum(
        "lsd,cd->slc", first_all, out_back, preferred_element_type=jnp.float32
    ).astype(jnp.bfloat16)
    out_weight_part = jnp.einsum(
        "slc,lsd->cd", context, first_all, preferred_element_type=jnp.float32
    )
    query_grad, key_grad, value_grad = lax.map(
        attend_backward,
        (
            query_heads,
            key_heads,
            value_heads,
            key_valid,
            log_sums,
            context_grad.reshape(head_shape),
        ),
    )
    query_weight_part = jnp.einsum(
        "lsd,slc->dc", rows_all, query_grad, preferred_element_type=jnp.float32
    )
    key_weight_part = jnp.einsum(
        "lsd,slc->dc", rows_all, key_grad, preferred_element_type=jnp.float32
    )
    value_weight_part = jnp.einsum(
        "lsd,slc->dc", rows_all, value_grad, preferred_element_type=jnp.float32
    )
    query_bias_part = jnp.sum(query_grad, axis=(0, 1), dtype=jnp.float32)
    value_bias_part = jnp.sum(value_grad, axis=(0, 1), dtype=jnp.float32)
    total = jnp.einsum("slc,dc->lsd", query_grad, query_back, preferred_element_type=jnp.float32)
    total = total + jnp.einsum(
        "slc,dc->lsd", key_grad, key_back, preferred_element_type=jnp.float32
    )
    input_grad = first_grad + lax.psum_scatter(
        (
            total
            + jnp.einsum("slc,dc->lsd", value_grad, value_back, preferred_element_type=jnp.float32)
        ).astype(jnp.bfloat16),
        "tensor",
        scatter_dimension=0,
        tiled=True,
    ).astype(jnp.float32)
    (
        query_weight_sum,
        key_weight_sum,
        value_weight_sum,
        out_weight_sum,
        up_weight_sum,
        down_weight_sum,
    ) = (
        lax.psum_scatter(query_weight_part, "dp", scatter_dimension=0, tiled=True),
        lax.psum_scatter(key_weight_part, "dp", scatter_dimension=0, tiled=True),
        lax.psum_scatter(value_weight_part, "dp", scatter_dimension=0, tiled=True),
        lax.psum_scatter(out_weight_part, "dp", scatter_dimension=1, tiled=True),
        lax.psum_scatter(up_weight_part, "dp", scatter_dimension=0, tiled=True),
        lax.psum_scatter(down_weight_part, "dp", scatter_dimension=1, tiled=True),
    )
    vector_sums = lax.psum(
        (
            embed(query_bias_part, D, tensor_index * head_width),
            embed(value_bias_part, D, tensor_index * head_width),
            out_bias_part,
            first_gain_part,
            first_shift_part,
            embed(up_bias_part, FF, tensor_index * hidden_width),
            down_bias_part,
            second_gain_part,
            second_shift_part,
        ),
        ("dp", "tensor"),
    )
    return (
        outputs,
        input_grad,
        query_weight_sum,
        key_weight_sum,
        value_weight_sum,
        vector_sums[0],
        vector_sums[1],
        out_weight_sum,
        vector_sums[2],
        vector_sums[3],
        vector_sums[4],
        up_weight_sum,
        vector_sums[5],
        down_weight_sum,
        vector_sums[6],
        vector_sums[7],
        vector_sums[8],
    )


def solution(mesh):
    in_specs = (
        P("tensor", "dp", None),
        P("dp"),
        P("dp", "tensor"),
        P("dp", "tensor"),
        P("dp", "tensor"),
        P(),
        P(),
        P("tensor", "dp"),
        P(),
        P(),
        P(),
        P("dp", "tensor"),
        P(),
        P("tensor", "dp"),
        P(),
        P(),
        P(),
        P("tensor", "dp", None),
    )
    out_specs = (
        P("tensor", "dp", None),
        P("tensor", "dp", None),
        P("dp", "tensor"),
        P("dp", "tensor"),
        P("dp", "tensor"),
        P(),
        P(),
        P("tensor", "dp"),
        P(),
        P(),
        P(),
        P("dp", "tensor"),
        P(),
        P("tensor", "dp"),
        P(),
        P(),
        P(),
    )
    return jax.shard_map(shards, mesh=mesh, in_specs=in_specs, out_specs=out_specs, check_vma=False)
```

profile of v0, /device:TPU:0, one launch (start us, length us, event | category | flops | bytes accessed | tf_op | source)
XLA Modules:
  0.0 1032.4 jit_solution(2957072023171445475)
XLA Ops:
  12.0 24.8 %all_gather.36 = bf16[768,384]{1,0:T(8,128)(2,1)S(1)} all-gather(bf16[48,384]{1,0:T(8,128)(2,1)S(1)} %copy-done.21), channel_id=1, replica_groups=mesh['dp'=16,'tensor'=2] {'dp'}, dimensions={0}, use_global_device_ids=true | all-gather | bytes 626688 | tf_op jit(solution)/shard_map/all_gather | solution.py:128
  36.8 20.4 %all_gather.38 = bf16[768,384]{1,0:T(8,128)(2,1)} all-gather(bf16[48,384]{1,0:T(8,128)(2,1)S(1)} %copy-done.22), channel_id=1, replica_groups=mesh['dp'=16,'tensor'=2] {'dp'}, dimensions={0}, use_global_device_ids=true | all-gather | bytes 626688 | tf_op jit(solution)/shard_map/all_gather | solution.py:126
  57.2 20.6 %all_gather.39 = bf16[768,384]{1,0:T(8,128)(2,1)S(1)} all-gather(bf16[48,384]{1,0:T(8,128)(2,1)S(1)} %copy-done.23), channel_id=1, replica_groups=mesh['dp'=16,'tensor'=2] {'dp'}, dimensions={0}, use_global_device_ids=true | all-gather | bytes 626688 | tf_op jit(solution)/shard_map/all_gather | solution.py:127
  77.9 20.4 %all_gather.40 = bf16[384,768]{0,1:T(8,128)(2,1)} all-gather(bf16[384,48]{0,1:T(8,128)(2,1)S(1)} %copy-done.24), channel_id=1, replica_groups=mesh['dp'=16,'tensor'=2] {'dp'}, dimensions={1}, use_global_device_ids=true | all-gather | bytes 626688 | tf_op jit(solution)/shard_map/all_gather | solution.py:129
  107.3 26.1 %while.26 = (s32[]{:T(128)}, bf16[4,512,384]{1,2,0:T(8,128)(2,1)}, f32[4,6,512]{2,1,0:T(8,128)S(1)}, bf16[4,512,6,64]{1,3,2,0:T(8,128)(2,1)}, pred[4,512]{1,0:T(...) while((s32[]{:T(128)}, bf16[4,512,384]{1,2,0:T(8,128)(2,1)}, ...), condition=%wide.region_3.4_spmd, body=%wide.region_0.3_spmd.sunk | while | flops 421721088 | bytes 21348956 | solution.py:155
  140.8 40.9 %reduce-scatter.17.cloned.1.call-done = bf16[256,4,768]{2,0,1:T(8,128)(2,1)} async-done(((bf16[512,4,768]{2,0,1:T(8,128)(2,1)}), bf16[256,4,768]{2,0,1:T(8,128)(2,1)}) %reduce-scatter.17.cloned.1.call-update) | async-done | bytes 1572880 | tf_op jit(solution)/shard_map/reduce_scatter | solution.py:157
  187.9 44.1 %all-gather.9.cloned.1.call-done = bf16[512,4,768]{2,0,1:T(8,128)(2,1)} async-done(((bf16[256,4,768]{2,0,1:T(8,128)(2,1)}), bf16[512,4,768]{2,0,1:T(8,128)(2,1)}) %all-gather.9.cloned.1.call-update) | async-done | bytes 3145744 | tf_op jit(solution)/shard_map/all_gather | solution.py:167
  232.0 11.1 %fusion.55 = (u8[512,1536]{1,0:T(8,128)(4,1)S(1)}, u8[512,1536]{1,0:T(8,128)(4,1)S(1)}, f32[512,4,1536]{2,0,1:T(8,128)S(1)}) fusion(f32[1536]{0:T(1024)S(1)} %dynamic_slice.44, bf16[512,4,768]{2,0,1:T(8,128)(2,1)} %all-gather.9.cloned.1.call-done, bf16[768,1536]{1,0:T(8,128)(2,1)} %all-gather.11.cloned.1.call-done), kind=kOutput, calls=%fused_computation.106 | convolution fusion | flops 4874305536 | bytes 19666944 | tf_op jit(solution)/shard_map/zhx,xm->zhm/dot_general | solution.py:169
  247.6 30.2 %multiply_convert_fusion.1 = (bf16[512,4,1536]{2,0,1:T(8,128)(2,1)}, f32[512,4,1536]{2,0,1:T(8,128)}) fusion(f32[512,4,1536]{2,0,1:T(8,128)S(1)} %get-tuple-element.218, f32[1536]{0:T(1024)S(1)} %dynamic_slice.44, u8[512,1536]{1,0:T(8,128)(4,1)S(1)} %get-tuple-element.149, u8[512,1536]{1,0:T(8,128)(4,1)S(1)} %get-tuple-element.148), kind=kLoop, calls=%fused_computation.69 | loop fusion | flops 223346688 | bytes 33036288 | tf_op jit(solution)/shard_map/convert_element_type | solution.py:177
  287.2 43.3 %reduce-scatter.19.cloned.1.call-done = bf16[256,4,768]{2,0,1:T(8,128)(2,1)} async-done(((bf16[512,4,768]{2,0,1:T(8,128)(2,1)}), bf16[256,4,768]{2,0,1:T(8,128)(2,1)}) %reduce-scatter.19.cloned.1.call-update) | async-done | bytes 1572880 | tf_op jit(solution)/shard_map/reduce_scatter | solution.py:179
  340.8 44.8 %all-gather.15.cloned.1.call-done = bf16[512,4,768]{2,0,1:T(8,128)(2,1)} async-done(((bf16[256,4,768]{2,0,1:T(8,128)(2,1)}), bf16[512,4,768]{2,0,1:T(8,128)(2,1)}) %all-gather.15.cloned.1.call-update) | async-done | bytes 3145744 | tf_op jit(solution)/shard_map/all_gather | solution.py:206
  385.7 17.0 %convert_reduce_fusion = (f32[1536]{0:T(1024)S(1)}, bf16[512,4,1536]{2,0,1:T(8,128)(2,1)S(1)}) fusion(f32[512,4,1536]{2,0,1:T(8,128)} %get-tuple-element.208, bf16[512,4,768]{2,0,1:T(8,128)(2,1)} %all-gather.15.cloned.1.call-done, bf16[1536,768]{0,1:T(8,128)(2,1)} %all-gather.13.cloned.1.call-done, f32[512,4,1536]{2,0,1:T(8,128)} %copy-done.11, ...), kind=kOutput, calls=%fused_computation.67 | convolution fusion | flops 4885314048 | bytes 36974592 | tf_op jit(solution)/shard_map/mkx,wx->mkw/dot_general | solution.py:207
  411.8 43.3 %reduce-scatter.21.cloned.1.call-done = bf16[256,4,768]{2,0,1:T(8,128)(2,1)} async-done(((bf16[512,4,768]{2,0,1:T(8,128)(2,1)}), bf16[256,4,768]{2,0,1:T(8,128)(2,1)}) %reduce-scatter.21.cloned.1.call-update) | async-done | bytes 1572880 | tf_op jit(solution)/shard_map/reduce_scatter | solution.py:224
  463.1 45.0 %all-gather.17.cloned.1.call-done = bf16[512,4,768]{2,0,1:T(8,128)(2,1)} async-done(((bf16[256,4,768]{2,0,1:T(8,128)(2,1)}), bf16[512,4,768]{2,0,1:T(8,128)(2,1)}) %all-gather.17.cloned.1.call-update) | async-done | bytes 3145744 | tf_op jit(solution)/shard_map/all_gather | solution.py:240
  515.3 51.6 %while.27 = (s32[]{:T(128)}, bf16[4,512,384]{1,2,0:T(8,128)(2,1)S(1)}, bf16[4,512,384]{1,2,0:T(8,128)(2,1)}, bf16[4,512,384]{1,2,0:T(8,128)(2,1)}, bf16[4,512,6,...) while((s32[]{:T(128)}, ...), condition=%wide.region_17.18_spmd, body=%wide.region_15.17_spmd.sunk | while | flops 1031205888 | bytes 59868828 | solution.py:247
  576.5 10.5 %convolution_bitcast_fusion = f32[1536,768]{0,1:T(8,128)} fusion(bf16[512,4,1536]{2,0,1:T(8,128)(2,1)} %get-tuple-element.207, bf16[512,4,768]{2,0,1:T(8,128)(2,1)} %all-gather.15.cloned.1.call-done), kind=kOutput, calls=%fused_computation.83 | convolution fusion | flops 4831838208 | bytes 14155776 | tf_op jit(solution)/shard_map/ayw,ayv->wv/dot_general | solution.py:216
  587.1 9.8 convolution_bitcast_fusion.1
  632.0 41.9 %all-reduce = (f32[768]{0:T(1024)}, f32[768]{0:T(1024)}, f32[768]{0:T(1024)}, f32[768]{0:T(1024)}, f32[768]{0:T(1024)}, /*index=5*/f32[3072]{0:T(1024)}, f32[768]{0:T(1024)}, f32[768]{0:T(1024)}, f32[768]{0:T(1024)}) all-reduce(f32[768]{0:T(1024)S(1)} %dynamic_update_slice.26, ...), channel_id=1, replica_groups=mesh['dp'=16,'tensor'=2] {'dp','tensor'}, use_global_device_ids=true, to_apply=%region_23.24 | all-reduce | flops 9216 | bytes 73728 | tf_op jit(solution)/shard_map/psum | solution.py:297
  679.4 20.6 %reduce-scatter.29.cloned.1.call-done = f32[1536,48]{0,1:T(8,128)} async-done(((f32[1536,768]{0,1:T(8,128)}), f32[1536,48]{0,1:T(8,128)}) %reduce-scatter.29.cloned.1.call-update) | async-done | bytes 294928 | tf_op jit(solution)/shard_map/reduce_scatter | solution.py:295
  700.0 79.6 %reduce-scatter.27.cloned.1.call-done = f32[48,1536]{1,0:T(8,128)} async-done(((f32[768,1536]{1,0:T(8,128)}), f32[48,1536]{1,0:T(8,128)}) %reduce-scatter.27.cloned.1.call-update) | async-done | bytes 294928 | tf_op jit(solution)/shard_map/reduce_scatter | solution.py:294
  779.6 61.4 %reduce-scatter.31.cloned.1.call-done = f32[48,384]{1,0:T(8,128)} async-done(((f32[768,384]{1,0:T(8,128)}), f32[48,384]{1,0:T(8,128)}) %reduce-scatter.31.cloned.1.call-update) | async-done | bytes 73744
  840.9 61.3 %reduce-scatter.33.cloned.1.call-done = f32[48,384]{1,0:T(8,128)} async-done(((f32[768,384]{1,0:T(8,128)}), f32[48,384]{1,0:T(8,128)}) %reduce-scatter.33.cloned.1.call-update) | async-done | bytes 73744
  902.3 61.2 %reduce-scatter.35.cloned.1.call-done = f32[48,384]{1,0:T(8,128)} async-done(((f32[768,384]{1,0:T(8,128)}), f32[48,384]{1,0:T(8,128)}) %reduce-scatter.35.cloned.1.call-update) | async-done | bytes 73744
  963.5 61.4 %reduce-scatter.25.cloned.1.call-done = f32[384,48]{0,1:T(8,128)} async-done(((f32[384,768]{0,1:T(8,128)}), f32[384,48]{0,1:T(8,128)}) %reduce-scatter.25.cloned.1.call-update) | async-done | bytes 73744 | tf_op jit(solution)/shard_map/reduce_scatter | solution.py:293
  (238 shorter events, 201.8 us)
Async XLA Ops:
  8.1 49.2 %copy-start.23 = (bf16[48,384]{1,0:T(8,128)(2,1)S(1)}, bf16[48,384]{1,0:T(8,128)(2,1)}, u32[]{:S(2)}) copy-start(bf16[48,384]{1,0:T(8,128)(2,1)} %param.25) | copy-start | bytes 110596
  8.1 69.8 %copy-start.24 = (bf16[384,48]{0,1:T(8,128)(2,1)S(1)}, bf16[384,48]{0,1:T(8,128)(2,1)}, u32[]{:S(2)}) copy-start(bf16[384,48]{0,1:T(8,128)(2,1)} %param.29) | copy-start | bytes 110596
  8.1 90.2 %all-gather.7.cloned.1.call-start = ((), (), s32[]{:S(2)}) async-start(), calls=%async_computation.10 | async-start | bytes 4718592 | tf_op jit(solution)/shard_map/all_gather | solution.py:139
  11.7 170.0 %reduce-scatter.17.cloned.1.call-start = ((), (), s32[]{:S(2)}) async-start(), calls=%async_computation.11 | async-start | bytes 4718592 | tf_op jit(solution)/shard_map/reduce_scatter | solution.py:157
  36.8 65.0 %copy-start.14 = (bf16[768,384]{1,0:T(8,128)(2,1)}, bf16[768,384]{1,0:T(8,128)(2,1)S(1)}, u32[]{:S(2)}) copy-start(bf16[768,384]{1,0:T(8,128)(2,1)S(1)} %all_gather.36) | copy-start | bytes 1769476
  133.4 48.3 %copy-start.29 = (f32[768]{0:T(1024)S(1)}, f32[768]{0:T(1024)}, u32[]{:S(2)}) copy-start(f32[768]{0:T(1024)} %param.30) | copy-start | bytes 9220
  139.7 48.3 %all-gather.11.cloned.1.call-start = ((), (), s32[]{:S(2)}) async-start(), calls=%async_computation.13 | async-start | bytes 2506752 | tf_op jit(solution)/shard_map/all_gather | solution.py:130
  140.3 91.8 %all-gather.9.cloned.1.call-start = ((), (), s32[]{:S(2)}) async-start(), calls=%async_computation.12 | async-start | bytes 4718592 | tf_op jit(solution)/shard_map/all_gather | solution.py:167
  187.2 90.6 %all-gather.13.cloned.1.call-start = ((), (), s32[]{:S(2)}) async-start(), calls=%async_computation.14 | async-start | bytes 2506752 | tf_op jit(solution)/shard_map/all_gather | solution.py:131
  187.8 142.6 %reduce-scatter.19.cloned.1.call-start = ((), (), s32[]{:S(2)}) async-start(), calls=%async_computation.15 | async-start | bytes 4718592 | tf_op jit(solution)/shard_map/reduce_scatter | solution.py:179
  286.9 43.5 %copy-start.30 = (f32[768]{0:T(1024)S(1)}, f32[768]{0:T(1024)}, u32[]{:S(2)}) copy-start(f32[768]{0:T(1024)} %param.36) | copy-start | bytes 9220
  286.9 98.7 %all-gather.15.cloned.1.call-start = ((), (), s32[]{:S(2)}) async-start(), calls=%async_computation.16 | async-start | bytes 4718592 | tf_op jit(solution)/shard_map/all_gather | solution.py:206
  340.8 114.3 %reduce-scatter.21.cloned.1.call-start = ((), (), s32[]{:S(2)}) async-start(), calls=%async_computation.17 | async-start | bytes 4718592 | tf_op jit(solution)/shard_map/reduce_scatter | solution.py:224
  411.7 96.4 %all-gather.17.cloned.1.call-start = ((), (), s32[]{:S(2)}) async-start(), calls=%async_computation.18 | async-start | bytes 4718592 | tf_op jit(solution)/shard_map/all_gather | solution.py:240
  461.7 46.4 %copy-start.19 = (bf16[384,768]{0,1:T(8,128)(2,1)S(1)}, bf16[384,768]{0,1:T(8,128)(2,1)}, u32[]{:S(2)}) copy-start(bf16[384,768]{0,1:T(8,128)(2,1)} %all_gather.40) | copy-start | bytes 1769476
  463.1 210.9 %reduce-scatter.23.cloned.1.call-start = ((), (), s32[]{:S(2)}) async-start(), calls=%async_computation.19 | async-start | bytes 4718592 | tf_op jit(solution)/shard_map/reduce_scatter | solution.py:273
  566.8 30.1 %copy-start.5 = (bf16[4,512,384]{1,2,0:T(8,128)(2,1)}, bf16[4,512,384]{1,2,0:T(8,128)(2,1)S(1)}, u32[]{:S(2)}) copy-start(bf16[4,512,384]{1,2,0:T(8,128)(2,1)S(1)} %get-tuple-element.111) | copy-start | bytes 4718596
  576.5 123.5 %reduce-scatter.29.cloned.1.call-start = ((), (), s32[]{:S(2)}) async-start(), calls=%async_computation.22 | async-start | bytes 5013504 | tf_op jit(solution)/shard_map/reduce_scatter | solution.py:295
  587.0 192.6 %reduce-scatter.27.cloned.1.call-start = ((), (), s32[]{:S(2)}) async-start(), calls=%async_computation.21 | async-start | bytes 5013504 | tf_op jit(solution)/shard_map/reduce_scatter | solution.py:294
  596.9 244.1 %reduce-scatter.31.cloned.1.call-start = ((), (), s32[]{:S(2)}) async-start(), calls=%async_computation.23 | async-start | bytes 1253376
  604.0 298.3 %reduce-scatter.33.cloned.1.call-start = ((), (), s32[]{:S(2)}) async-start(), calls=%async_computation.24 | async-start | bytes 1253376
  611.1 352.4 %reduce-scatter.35.cloned.1.call-start = ((), (), s32[]{:S(2)}) async-start(), calls=%async_computation.25 | async-start | bytes 1253376
  615.9 408.9 %reduce-scatter.25.cloned.1.call-start = ((), (), s32[]{:S(2)}) async-start(), calls=%async_computation.20 | async-start | bytes 1253376 | tf_op jit(solution)/shard_map/reduce_scatter | solution.py:293
  627.6 46.3 %copy-start.1 = (f32[256,4,768]{2,0,1:T(8,128)S(1)}, f32[256,4,768]{2,0,1:T(8,128)}, u32[]{:S(2)}) copy-start(f32[256,4,768]{2,0,1:T(8,128)} %copy-done) | copy-start | bytes 9437188
  (33 other events, 163.7 us)
Sparse Core Ops, SparseCore 0:
  11.8 47.6 all-gather.6
  139.8 41.8 reduce-scatter.16
  287.1 43.3 reduce-scatter.18
  463.2 44.9 all-gather.16
  576.6 43.3 reduce-scatter.22
  624.3 75.7 reduce-scatter.28
  704.9 74.5 reduce-scatter.26
  783.8 57.1 reduce-scatter.30
  845.1 57.1 reduce-scatter.32
  906.3 57.0 reduce-scatter.34
  967.7 57.1 reduce-scatter.24
Sparse Core Ops, SparseCore 1:
  142.7 41.0 all-gather.10
  187.3 44.7 all-gather.8
  234.5 42.7 all-gather.12
  340.9 44.7 all-gather.14
  411.8 43.2 reduce-scatter.20
where the time goes:
time: 1040 us; the launch traced here: 1030 us
  waiting for transfers between devices  608 us (58%)
  matrix products  164 us (16%)
  blocking collectives  128 us (12%)
  other arithmetic  70.6 us (7%)
  local copies, waits for them, and re-layouts  42.7 us (4%)
  between operations  16.3 us (2%)
    unnamed x19, waiting for transfers between devices  185 us
    reduce_scatter x1, waiting for transfers between devices, shards(): lax.psum_scatter(up_weight_part, 'dp', scatter_dimension=0, tiled=True)  79.6 us
    reduce_scatter x1, waiting for transfers between devices, shards(): lax.psum_scatter(out_weight_part, 'dp', scatter_dimension=1, tiled=True)  61.4 us
    all_gather x1, waiting for transfers between devices, shards(): first_all = lax.all_gather(first_low, 'tensor', axis=0, tiled=True)  45 us
    all_gather x1, waiting for transfers between devices, shards(): lax.all_gather(second_low, 'tensor', axis=0, tiled=True)  44.8 us
    all_gather x1, waiting for transfers between devices, shards(): lax.all_gather(hidden_reduced_precision, 'tensor', axis=0, tiled=True)  44.1 us
    reduce_scatter x1, waiting for transfers between devices, shards(): lax.psum_scatter(jnp.einsum('hky,ty->hkt', block_row_span, up_projection_...  43.3 us
    reduce_scatter x1, waiting for transfers between devices, shards(): lax.psum_scatter(jnp.einsum('kng,gw->knw', block_row_span, down_projectio...  43.3 us
  transfers between devices with their start and end apart: 16, of which 12 were waited for; matrix products, arithmetic and copies ran while one was open for 10% of the time, Pallas kernels for 0%

commit v1 on v0

v1 whole, which is shorter than its diff:
```python
import functools

import jax
import jax.numpy as jnp
from jax import lax
from jax.experimental import pallas as pl
from jax.experimental.pallas import tpu as pltpu
from jax.sharding import PartitionSpec as P

D = 768
H = 12
HD = 64
FF = 3072

NORM_EPSILON = 1e-12
BF = jnp.bfloat16
F32 = jnp.float32


def dot(a, b, da, db):
    return lax.dot_general(a, b, (((da,), (db,)), ((), ())), preferred_element_type=F32)


def layer_norm(resid, gain_vec, shift_vec):
    mean_value = jnp.mean(resid, -1, keepdims=True)
    centred = resid - mean_value
    variance = jnp.mean(centred * centred, -1, keepdims=True)
    inv_std = lax.rsqrt(variance + NORM_EPSILON)
    normed = centred * inv_std
    return (normed * gain_vec + shift_vec, normed, inv_std)


def norm_back(grad_in, normed, inv_std, gain_vec):
    scaled = grad_in * gain_vec
    return inv_std * (
        scaled
        - jnp.mean(scaled, -1, keepdims=True)
        - normed * jnp.mean(scaled * normed, -1, keepdims=True)
    )


def gelu_both(v):
    z = jnp.abs(v) * (0.5**0.5)
    t = 1.0 / (1.0 + 0.3275911 * z)
    gauss = jnp.exp(-0.5 * v * v)
    poly = t * (
        0.5 * 0.254829592
        + t * (0.5 * -0.284496736 + t * (0.5 * 1.421413741 + t * (0.5 * -1.453152027 + t * (0.5 * 1.061405429))))
    )
    tail = poly * gauss
    phi_cum = jnp.where(v < 0, tail, 1.0 - tail)
    return v * phi_cum, phi_cum + v * gauss * 0.3989422804014327


def attend_forward_kernel(heads, half, lens, tindex, q_ref, k_ref, v_ref, ko_ref, vo_ref, ctx_ref, lse_ref):
    seq = pl.program_id(1)
    length = lens[seq]
    own = tindex[0] * half
    other = (1 - tindex[0]) * half
    lane = lax.broadcasted_iota(jnp.int32, (1, half), 1)
    bias_own = jnp.where(lane + own < length, 0.0, -1e30)
    bias_oth = jnp.where(lane + other < length, 0.0, -1e30)
    col = lax.broadcasted_iota(jnp.int32, (half, 128), 1)
    lse_tile = jnp.zeros((half, 128), F32)
    for h in range(heads):
        sl = slice(h * HD, (h + 1) * HD)
        q = q_ref[0, :, sl]
        s_own = dot(q, k_ref[0, :, sl], 1, 1) + bias_own
        s_oth = dot(q, ko_ref[0, :, sl], 1, 1) + bias_oth
        m = jnp.maximum(jnp.max(s_own, -1, keepdims=True), jnp.max(s_oth, -1, keepdims=True))
        e_own = jnp.exp(s_own - m)
        e_oth = jnp.exp(s_oth - m)
        total = jnp.sum(e_own, -1, keepdims=True) + jnp.sum(e_oth, -1, keepdims=True)
        c = dot(e_own.astype(BF), v_ref[0, :, sl], 1, 0) + dot(e_oth.astype(BF), vo_ref[0, :, sl], 1, 0)
        ctx_ref[:, sl] = (c / total).astype(BF)
        lse_tile = jnp.where(col == h, m + jnp.log(total), lse_tile)
    lse_ref[0] = lse_tile


def attend_backward_kernel(
    heads, half, lens, tindex, q_ref, k_ref, v_ref, ko_ref, vo_ref, ctx_ref, lse_ref, dctx_ref, own_ref, oth_ref
):
    seq = pl.program_id(1)
    width = heads * HD
    length = lens[seq]
    own = tindex[0] * half
    other = (1 - tindex[0]) * half
    row = lax.broadcasted_iota(jnp.int32, (half, 1), 0)
    bias_own = jnp.where(row + own < length, 0.0, -1e30)
    bias_oth = jnp.where(row + other < length, 0.0, -1e30)
    lse_rows = jnp.transpose(lse_ref[0])
    prod = ctx_ref[...].astype(F32) * dctx_ref[...].astype(F32)
    col = lax.broadcasted_iota(jnp.int32, (half, 128), 1)
    delta_tile = jnp.zeros((half, 128), F32)
    for h in range(heads):
        delta_tile = jnp.where(
            col == h, jnp.sum(prod[:, h * HD : (h + 1) * HD], -1, keepdims=True), delta_tile
        )
    delta_rows = jnp.transpose(delta_tile)
    for h in range(heads):
        sl = slice(h * HD, (h + 1) * HD)
        q = q_ref[0, :, sl]
        dc = dctx_ref[:, sl]
        lse = lse_rows[h : h + 1, :]
        delta = delta_rows[h : h + 1, :]
        dq = None
        for k_src, v_src, bias, out, base in (
            (k_ref, v_ref, bias_own, own_ref, width),
            (ko_ref, vo_ref, bias_oth, oth_ref, 0),
        ):
            k = k_src[0, :, sl]
            p = jnp.exp(dot(k, q, 1, 1) + bias - lse)
            dp = dot(v_src[0, :, sl], dc, 1, 1)
            ds = (p * (dp - delta)).astype(BF)
            out[0, :, base + h * HD : base + (h + 1) * HD] = dot(ds, q, 1, 0).astype(BF)
            out[0, :, base + width + h * HD : base + width + (h + 1) * HD] = dot(
                p.astype(BF), dc, 1, 0
            ).astype(BF)
            part = dot(ds, k, 0, 0)
            dq = part if dq is None else dq + part
        own_ref[0, :, sl] = (dq * HD**-0.5).astype(BF)


def attend_forward(lengths, tindex, qkv_own, kv_oth, seqs, half):
    halves, rows, width3 = qkv_own.shape
    width = width3 // 3
    heads = width // HD
    spec = lambda j: pl.BlockSpec((1, half, width), lambda t, s, *_: (t, s, j))
    return pl.pallas_call(
        functools.partial(attend_forward_kernel, heads, half),
        grid_spec=pltpu.PrefetchScalarGridSpec(
            num_scalar_prefetch=2,
            grid=(halves, seqs),
            in_specs=[spec(0), spec(1), spec(2), spec(0), spec(1)],
            out_specs=[
                pl.BlockSpec((half, width), lambda t, s, *_: (s, t)),
                pl.BlockSpec((1, half, 128), lambda t, s, *_: (t * seqs + s, 0, 0)),
            ],
        ),
        out_shape=[
            jax.ShapeDtypeStruct((rows, halves * width), BF),
            jax.ShapeDtypeStruct((halves * seqs, half, 128), F32),
        ],
        compiler_params=pltpu.CompilerParams(vmem_limit_bytes=32 * 1024 * 1024),
        cost_estimate=pl.CostEstimate(flops=6_000_000_000, bytes_accessed=9_000_000, transcendentals=7_000_000),
        name="attend_forward",
    )(lengths, tindex, qkv_own, qkv_own, qkv_own, kv_oth, kv_oth)


def attend_backward(lengths, tindex, qkv_own, kv_oth, ctx, lse, dctx, seqs, half):
    halves, rows, width3 = qkv_own.shape
    width = width3 // 3
    heads = width // HD
    spec = lambda j: pl.BlockSpec((1, half, width), lambda t, s, *_: (t, s, j))
    flat = pl.BlockSpec((half, width), lambda t, s, *_: (s, t))
    return pl.pallas_call(
        functools.partial(attend_backward_kernel, heads, half),
        grid_spec=pltpu.PrefetchScalarGridSpec(
            num_scalar_prefetch=2,
            grid=(halves, seqs),
            in_specs=[
                spec(0),
                spec(1),
                spec(2),
                spec(0),
                spec(1),
                flat,
                pl.BlockSpec((1, half, 128), lambda t, s, *_: (t * seqs + s, 0, 0)),
                flat,
            ],
            out_specs=[
                pl.BlockSpec((1, half, 3 * width), lambda t, s, *_: (t, s, 0)),
                pl.BlockSpec((1, half, 2 * width), lambda t, s, *_: (t, s, 0)),
            ],
        ),
        out_shape=[
            jax.ShapeDtypeStruct((halves, rows, 3 * width), BF),
            jax.ShapeDtypeStruct((halves, rows, 2 * width), BF),
        ],
        compiler_params=pltpu.CompilerParams(vmem_limit_bytes=40 * 1024 * 1024),
        cost_estimate=pl.CostEstimate(flops=15_000_000_000, bytes_accessed=20_000_000, transcendentals=7_000_000),
        name="attend_backward",
    )(lengths, tindex, qkv_own, qkv_own, qkv_own, kv_oth, kv_oth, ctx, lse, dctx)


def sum_everywhere(vec, dp_size):
    vec = vec + lax.ppermute(vec, "tensor", [(0, 1), (1, 0)])
    bit = 1
    while bit < dp_size:
        vec = vec + lax.ppermute(vec, "dp", [(i, i ^ bit) for i in range(dp_size)])
        bit *= 2
    return vec


def split_vec(vec, sizes):
    out, at = [], 0
    for size in sizes:
        out.append(lax.slice_in_dim(vec, at, at + size))
        at += size
    return out


def shards(
    inputs,
    lengths,
    query_weight,
    key_weight,
    value_weight,
    query_bias,
    value_bias,
    out_weight,
    out_bias,
    first_gain,
    first_shift,
    input_projection_weight,
    input_projection_bias,
    output_projection_weight,
    output_projection_bias,
    second_gain,
    second_shift,
    out_cotangent,
):
    tensor_index = lax.axis_index("tensor")
    dp_size = lax.axis_size("dp")
    half, seqs, _ = inputs.shape
    rows = half * seqs
    width = D // 2
    hidden_width = FF // 2
    tindex = jnp.reshape(tensor_index, (1,)).astype(jnp.int32)
    everywhere = ("tensor", "dp")

    def gather(packed):
        full = lax.all_gather(packed, everywhere, axis=0, tiled=True)
        return full.reshape(2, D, packed.shape[1])

    def swap(v):
        return lax.ppermute(v, "tensor", [(0, 1), (1, 0)])

    qkv_w = gather(jnp.concatenate([query_weight, key_weight, value_weight], 1))
    out_w = gather(out_weight.T)
    up_w = gather(input_projection_weight)
    down_w = gather(output_projection_weight.T)

    inputs_seq = inputs.transpose(1, 0, 2).reshape(rows, D)
    rows_low = inputs_seq.astype(BF)
    rows_other = swap(rows_low)
    zeros = jnp.zeros((width,), F32)
    own_parts, oth_parts = [], []
    for t in range(2):
        qb = query_bias[t * width : (t + 1) * width]
        vb = value_bias[t * width : (t + 1) * width]
        product = dot(rows_low, qkv_w[t], 1, 0) + jnp.concatenate([qb, zeros, vb])
        scale = jnp.concatenate([jnp.full((width,), HD**-0.5, BF), jnp.ones((2 * width,), BF)])
        own_parts.append(product.astype(BF) * scale)
        product = dot(rows_other, qkv_w[t][:, width:], 1, 0) + jnp.concatenate([zeros, vb])
        oth_parts.append(product.astype(BF))
    qkv_own = jnp.stack(own_parts)
    kv_oth = jnp.stack(oth_parts)
    context, log_sums = attend_forward(lengths, tindex, qkv_own, kv_oth, seqs, half)
    attention = dot(context[:, :width], out_w[0], 1, 1) + dot(context[:, width:], out_w[1], 1, 1)
    hidden, normed_one, inv_one = layer_norm(inputs_seq + attention + out_bias, first_gain, first_shift)
    hidden_low = hidden.astype(BF)
    acts, slopes = [], []
    for t in range(2):
        pre = dot(hidden_low, up_w[t], 1, 0) + input_projection_bias[t * hidden_width : (t + 1) * hidden_width]
        act, slope = gelu_both(pre)
        acts.append(act.astype(BF))
        slopes.append(slope.astype(BF))
    branch = dot(acts[0], down_w[0], 1, 1) + dot(acts[1], down_w[1], 1, 1)
    outputs, normed_two, inv_two = layer_norm(
        hidden + branch + output_projection_bias, second_gain, second_shift
    )
    cotangent = out_cotangent.transpose(1, 0, 2).reshape(rows, D)
    second_grad = norm_back(cotangent, normed_two, inv_two, second_gain)
    second_gain_part = jnp.sum(cotangent * normed_two, axis=0)
    second_shift_part = jnp.sum(cotangent, axis=0)
    down_bias_part = jnp.sum(second_grad, axis=0)
    second_low = second_grad.astype(BF)
    pre_grads, up_bias_parts = [], []
    for t in range(2):
        pre_grad = (dot(second_low, down_w[t], 1, 0) * slopes[t].astype(F32)).astype(BF)
        pre_grads.append(pre_grad)
        up_bias_parts.append(jnp.sum(pre_grad, axis=0, dtype=F32))

    def scatter(parts):
        full = jnp.concatenate([p.astype(BF) for p in parts], 0)
        return lax.psum_scatter(full, everywhere, scatter_dimension=0, tiled=True)

    down_sum = scatter([dot(second_low, acts[t], 0, 0) for t in range(2)])
    up_sum = scatter([dot(hidden_low, pre_grads[t], 0, 0) for t in range(2)])
    hidden_grad = second_grad + (dot(pre_grads[0], up_w[0], 1, 1) + dot(pre_grads[1], up_w[1], 1, 1))
    first_grad = norm_back(hidden_grad, normed_one, inv_one, first_gain)
    first_gain_part = jnp.sum(hidden_grad * normed_one, axis=0)
    first_shift_part = jnp.sum(hidden_grad, axis=0)
    out_bias_part = jnp.sum(first_grad, axis=0)
    first_low = first_grad.astype(BF)
    early = sum_everywhere(
        jnp.concatenate(
            [
                out_bias_part,
                first_gain_part,
                first_shift_part,
                down_bias_part,
                second_gain_part,
                second_shift_part,
                *up_bias_parts,
            ]
        ),
        dp_size,
    )
    out_bias_sum, first_gain_sum, first_shift_sum, down_bias_sum, second_gain_sum, second_shift_sum, up_bias_sum = (
        split_vec(early, [D] * 6 + [FF])
    )
    context_grad = jnp.concatenate([dot(first_low, out_w[t], 1, 0).astype(BF) for t in range(2)], 1)
    out_grads = [dot(first_low, context[:, t * width : (t + 1) * width], 0, 0) for t in range(2)]
    own_grad, oth_grad = attend_backward(
        lengths, tindex, qkv_own, kv_oth, context, log_sums, context_grad, seqs, half
    )
    other_total = dot(oth_grad[0], qkv_w[0][:, width:], 1, 1) + dot(oth_grad[1], qkv_w[1][:, width:], 1, 1)
    from_other = swap(other_total.astype(BF))
    own_total = dot(own_grad[0], qkv_w[0], 1, 1) + dot(own_grad[1], qkv_w[1], 1, 1)
    input_grad = first_grad + (own_total + from_other.astype(F32))
    grads = []
    for t in range(2):
        query_part = dot(rows_low, own_grad[t][:, :width], 0, 0)
        key_value_part = dot(rows_low, own_grad[t][:, width:], 0, 0) + dot(rows_other, oth_grad[t], 0, 0)
        grads.append(jnp.concatenate([query_part.astype(BF), key_value_part.astype(BF), out_grads[t].astype(BF)], 1))
    qkvo_sum = scatter(grads)
    late = sum_everywhere(
        jnp.concatenate(
            [jnp.sum(own_grad[t][:, :width], axis=0, dtype=F32) for t in range(2)]
            + [
                jnp.sum(own_grad[t][:, 2 * width :], axis=0, dtype=F32)
                + jnp.sum(oth_grad[t][:, width:], axis=0, dtype=F32)
                for t in range(2)
            ]
        ),
        dp_size,
    )
    query_bias_sum, value_bias_sum = split_vec(late, [D, D])
    qkvo_sum = qkvo_sum.astype(F32)

    def positions_first(v):
        return v.reshape(seqs, half, D).transpose(1, 0, 2)

    return (
        positions_first(outputs),
        positions_first(input_grad),
        qkvo_sum[:, :width],
        qkvo_sum[:, width : 2 * width],
        qkvo_sum[:, 2 * width : 3 * width],
        query_bias_sum,
        value_bias_sum,
        qkvo_sum[:, 3 * width :].T,
        out_bias_sum,
        first_gain_sum,
        first_shift_sum,
        up_sum.astype(F32),
        up_bias_sum,
        down_sum.astype(F32).T,
        down_bias_sum,
        second_gain_sum,
        second_shift_sum,
    )


def solution(mesh):
    in_specs = (
        P("tensor", "dp", None),
        P("dp"),
        P("dp", "tensor"),
        P("dp", "tensor"),
        P("dp", "tensor"),
        P(),
        P(),
        P("tensor", "dp"),
        P(),
        P(),
        P(),
        P("dp", "tensor"),
        P(),
        P("tensor", "dp"),
        P(),
        P(),
        P(),
        P("tensor", "dp", None),
    )
    out_specs = (
        P("tensor", "dp", None),
        P("tensor", "dp", None),
        P("dp", "tensor"),
        P("dp", "tensor"),
        P("dp", "tensor"),
        P(),
        P(),
        P("tensor", "dp"),
        P(),
        P(),
        P(),
        P("dp", "tensor"),
        P(),
        P("tensor", "dp"),
        P(),
        P(),
        P(),
    )
    return jax.shard_map(shards, mesh=mesh, in_specs=in_specs, out_specs=out_specs, check_vma=False)
```

time: 1040 us -> 745 us (0.72)
  waiting for transfers between devices: 608 us -> 454 us
  blocking collectives: 128 us -> 0 us
  Pallas kernels: 0 us -> 56 us
  matrix products: 164 us -> 116 us
  other arithmetic: 70.6 us -> 42.8 us
  starting transfers between devices: 1.48 us -> 15.8 us
    unnamed x19 -> x8, waiting for transfers between devices: 185 us -> 11.7 us
    all_gather x4 -> x0, blocking collectives: 86.3 us -> none  [the longest x1 24.8 us: shards(): lax.all_gather(value_weight, 'dp', axis=0, tiled=True)]
    ppermute x0 -> x12, waiting for transfers between devices: none -> 82.2 us  [the longest x2 40.5 us: sum_everywhere(): vec = vec + lax.ppermute(vec, 'tensor', [(0, 1), (1, 0)])]
    reduce_scatter x7 -> x2, waiting for transfers between devices: 289 us -> 218 us  [scatter(): return lax.psum_scatter(full, everywhere, scatter_dimension=0, tiled=True)]
    pallas_call x0 -> x2, Pallas kernels: none -> 56 us  [the longest x1 35.6 us: attend_backward(): pl.pallas_call(functools.partial(attend_backward_kernel, heads, half), gr...]
    dot_general x46 -> x32, matrix products: 164 us -> 116 us  [dot(): lax.dot_general(a, b, (((da,), (db,)), ((), ())), preferred_element_type=...]
    convert_element_type x8 -> x6, other arithmetic: 45.8 us -> 3.86 us  [the longest x1 1.64 us: shards(): up_sum.astype(F32)]
    psum x1 -> x0, blocking collectives: 41.9 us -> none  [shards(): lax.psum((embed(query_bias_part, D, tensor_index * head_width), embed(val...]
  transfers between devices with their start and end apart: 16 -> 19, of which waited for: 12 -> 13; matrix products, arithmetic and copies ran while one was open for 10% -> 13% of each run, Pallas kernels for 0% -> 3%
where the time goes in v1:
time: 745 us; the launch traced here: 738 us
  waiting for transfers between devices  454 us (61%)
  matrix products  116 us (16%)
  Pallas kernels  56 us (8%)
  other arithmetic  42.8 us (6%)
  local copies, waits for them, and re-layouts  37.9 us (5%)
  starting transfers between devices  15.8 us (2%)
  between operations  15.4 us (2%)
    reduce_scatter x2, waiting for transfers between devices, scatter(): return lax.psum_scatter(full, everywhere, scatter_dimension=0, tiled=True)  218 us
    all_gather x4, waiting for transfers between devices, gather(): full = lax.all_gather(packed, everywhere, axis=0, tiled=True)  142 us
    dot_general x32, matrix products, dot(): lax.dot_general(a, b, (((da,), (db,)), ((), ())), preferred_element_type=...  116 us
    ppermute x2, waiting for transfers between devices, sum_everywhere(): vec = vec + lax.ppermute(vec, 'tensor', [(0, 1), (1, 0)])  40.5 us
    pallas_call x1, Pallas kernels, attend_backward(): pl.pallas_call(functools.partial(attend_backward_kernel, heads, half), gr...  35.6 us
    ppermute x2, waiting for transfers between devices, swap(): return lax.ppermute(v, 'tensor', [(0, 1), (1, 0)])  33.8 us
    concatenate x3, other arithmetic, scatter(): full = jnp.concatenate([p.astype(BF) for p in parts], 0)  24.8 us
    unnamed x119, local copies, waits for them, and re-layouts  20.9 us
  transfers between devices with their start and end apart: 19, of which 13 were waited for; matrix products, arithmetic and copies ran while one was open for 13% of the time, Pallas kernels for 3%

profile of v1, /device:TPU:0, one launch (start us, length us, event | category | flops | bytes accessed | tf_op | source)
XLA Modules:
  0.0 737.8 jit_solution(15913250140217030414)
XLA Ops:
  21.9 33.8 %collective-permute-done = bf16[1024,768]{1,0:T(8,128)(2,1)} collective-permute-done((bf16[1024,768]{1,0:T(8,128)(2,1)}, bf16[1024,768]{1,0:T(8,128)(2,1)}, u32[]{:S(2)}, u32[]{:S(2)}) %collective-permute-start) | collective-permute-done | bytes 1572896 | tf_op jit(solution)/shard_map/ppermute | solution.py:237
  55.8 19.1 %all-gather.5.cloned.1.call-done = bf16[1536,1152]{1,0:T(8,128)(2,1)} async-done(((bf16[48,1152]{1,0:T(8,128)(2,1)}), bf16[1536,1152]{1,0:T(8,128)(2,1)}) %all-gather.5.cloned.1.call-update) | async-done | bytes 3538960 | tf_op jit(solution)/shard_map/all_gather | solution.py:233
  81.7 4.4 fusion.14
  90.3 20.4 %attend_forward.1 = (bf16[1024,768]{1,0:T(8,128)(2,1)S(1)}, f32[8,256,128]{2,1,0:T(8,128)S(1)}) custom-call(s32[4]{0:T(128)S(1)} %copy-done.5, s32[1]{0:T(128)} %bitcast.2.tindex, bf16[2,1024,1152]{2,1,0:T(8,128)(2,1)S(1)} %pad_maximum_fusion.q_ref.k_ref.v_ref, bf16[2,1024,1152]{2,1,0:T(8,128)(2,1)S(1)} %pad_maximum_fusion.q_ref.k_ref.v_ref, ...), custom_call_target="tpu_custom_call" | custom-call | flops 6000000000 | bytes 9000000 | tf_op jit(solution)/shard_map/attend_forward/pallas_call | solution.py:129
  112.8 17.8 %all-gather.7.cloned.1.call-done = bf16[1536,384]{1,0:T(8,128)(2,1)} async-done(((bf16[48,384]{1,0:T(8,128)(2,1)}), bf16[1536,384]{1,0:T(8,128)(2,1)}) %all-gather.7.cloned.1.call-update) | async-done | bytes 1179664 | tf_op jit(solution)/shard_map/all_gather | solution.py:233
  136.5 59.6 %all-gather.9.cloned.1.call-done = bf16[1536,1536]{1,0:T(8,128)(2,1)} async-done(((bf16[48,1536]{1,0:T(8,128)(2,1)}), bf16[1536,1536]{1,0:T(8,128)(2,1)}) %all-gather.9.cloned.1.call-update) | async-done | bytes 4718608 | tf_op jit(solution)/shard_map/all_gather | solution.py:233
  196.1 10.6 %multiply_convert_fusion.2 = (bf16[1024,1536]{1,0:T(8,128)(2,1)}, f32[1024,1536]{1,0:T(8,128)}) fusion(f32[1536]{0:T(1024)S(1)} %get-tuple-element.122, bf16[1024,768]{1,0:T(8,128)(2,1)S(1)} %fusion.18, bf16[1536,1536]{1,0:T(8,128)(2,1)} %all-gather.9.cloned.1.call-done), kind=kOutput, calls=%fused_computation.20 | convolution fusion | flops 2450522112 | bytes 13375488 | tf_op jit(solution)/shard_map/dot_general | solution.py:21
  206.6 9.0 %multiply_convert_fusion.3 = (bf16[1024,1536]{1,0:T(8,128)(2,1)}, f32[1024,1536]{1,0:T(8,128)}) fusion(f32[1536]{0:T(1024)S(1)} %get-tuple-element.121, bf16[1024,768]{1,0:T(8,128)(2,1)S(1)} %fusion.18, bf16[1536,1536]{1,0:T(8,128)(2,1)S(1)} %copy-done.35), kind=kOutput, calls=%fused_computation.21 | convolution fusion | flops 2450522112 | bytes 13377536 | tf_op jit(solution)/shard_map/dot_general | solution.py:21
  215.6 45.6 %all-gather.11.cloned.1.call-done = bf16[1536,1536]{1,0:T(8,128)(2,1)} async-done(((bf16[48,1536]{1,0:T(8,128)(2,1)}), bf16[1536,1536]{1,0:T(8,128)(2,1)}) %all-gather.11.cloned.1.call-update) | async-done | bytes 4718608 | tf_op jit(solution)/shard_map/all_gather | solution.py:233
  261.2 5.4 fusion.20
  276.0 9.8 %convert_reduce_fusion.1 = (f32[1536]{0:T(1024)S(1)}, bf16[1024,1536]{1,0:T(8,128)(2,1)S(1)}) fusion(f32[1024,1536]{1,0:T(8,128)} %get-tuple-element.136, f32[1536]{0:T(1024)S(1)} %get-tuple-element.121, bf16[1024,768]{1,0:T(8,128)(2,1)S(1)} %convert_element_type.151, bf16[1536,1536]{1,0:T(8,128)(2,1)S(1)} %copy-done.36), kind=kOutput, calls=%fused_computation.17 | convolution fusion | flops 2461530624 | bytes 13383680 | tf_op jit(solution)/shard_map/dot_general | solution.py:21
  285.9 8.4 %convert_reduce_fusion = (f32[1536]{0:T(1024)S(1)}, bf16[1024,1536]{1,0:T(8,128)(2,1)S(1)}) fusion(f32[1024,1536]{1,0:T(8,128)S(1)} %bitcast.119, f32[1536]{0:T(1024)S(1)} %get-tuple-element.122, bf16[1024,768]{1,0:T(8,128)(2,1)S(1)} %convert_element_type.151, bf16[1536,1536]{1,0:T(8,128)(2,1)S(1)} %copy-done.36), kind=kOutput, calls=%fused_computation.16 | convolution fusion | flops 2461530624 | bytes 13383680 | tf_op jit(solution)/shard_map/dot_general | solution.py:21
  308.4 35.6 %attend_backward.1 = (bf16[2,1024,1152]{2,1,0:T(8,128)(2,1)}, bf16[2,1024,768]{2,1,0:T(8,128)(2,1)S(1)}) custom-call(s32[4]{0:T(128)S(1)} %copy-done.5, s32[1]{0:T(128)} %bitcast.2.tindex, bf16[2,1024,1152]{2,1,0:T(8,128)(2,1)} %copy-done, bf16[2,1024,1152]{2,1,0:T(8,128)(2,1)} %copy-done, bf16[2,1024,1152]{2,1,0:T(8,128)(2,1)} %copy-done, ...), custom_call_target="tpu_custom_call" | custom-call | flops 15000000512 | bytes 20000000 | tf_op jit(solution)/shard_map/attend_backward/pallas_call | solution.py:156
  346.7 4.1 fusion.35
  364.0 19.8 %maximum_maximum_fusion = bf16[1536,1536]{0,1:T(8,128)(2,1)} fusion(bf16[768,384]{0,1:T(8,128)(2,1)S(1)} %convolution_convert_fusion.6, bf16[768,768]{0,1:T(8,128)(2,1)S(1)} %fusion.47, bf16[768,384]{0,1:T(8,128)(2,1)S(1)} %fusion.51, bf16[768,384]{0,1:T(8,128)(2,1)S(1)} %convolution_convert_fusion.8, bf16[768,768]{0,1:T(8,128)(2,1)S(1)} %fusion.46, ...), kind=kLoop, calls=%fused_computation.23 | loop fusion | flops 28311552 | bytes 9437184 | tf_op jit(solution)/shard_map/concatenate | solution.py:286
  383.9 6.6 copy.99
  390.6 5.2 convolution_convert_fusion.1
  401.3 5.3 convolution_convert_fusion.3
  425.1 40.5 %collective-permute-done.2 = f32[1536]{0:T(1024)S(1)} collective-permute-done((f32[1536]{0:T(1024)S(1)}, f32[1536]{0:T(1024)S(1)}, u32[]{:S(2)}, u32[]{:S(2)}) %collective-permute-start.2) | collective-permute-done | bytes 6176 | tf_op jit(solution)/shard_map/ppermute | solution.py:187
  479.2 3.7 copy.106
  491.3 3.7 copy.105
  494.9 10.3 %reduce-scatter.10.cloned.1.call-done = bf16[48,1536]{1,0:T(8,128)(2,1)} async-done(((bf16[1536,1536]{1,0:T(8,128)(2,1)}), bf16[48,1536]{1,0:T(8,128)(2,1)}) %reduce-scatter.10.cloned.1.call-update) | async-done | bytes 147472
  509.4 108.1 %reduce-scatter.8.cloned.1.call-done = bf16[48,1536]{1,0:T(8,128)(2,1)} async-done(((bf16[1536,1536]{1,0:T(8,128)(2,1)}), bf16[48,1536]{1,0:T(8,128)(2,1)}) %reduce-scatter.8.cloned.1.call-update) | async-done | bytes 147472 | tf_op jit(solution)/shard_map/reduce_scatter | solution.py:287
  619.2 109.9 %reduce-scatter.6.cloned.1.call-done = bf16[48,1536]{1,0:T(8,128)(2,1)} async-done(((bf16[1536,1536]{1,0:T(8,128)(2,1)}), bf16[48,1536]{1,0:T(8,128)(2,1)}) %reduce-scatter.6.cloned.1.call-update) | async-done | bytes 147472 | tf_op jit(solution)/shard_map/reduce_scatter | solution.py:287
  (242 shorter events, 126.0 us)
Async XLA Ops:
  7.2 67.7 %all-gather.5.cloned.1.call-start = ((), (), s32[]{:S(2)}) async-start(), calls=%async_computation.3 | async-start | bytes 3649536 | tf_op jit(solution)/shard_map/all_gather | solution.py:233
  8.7 121.9 %all-gather.7.cloned.1.call-start = ((), (), s32[]{:S(2)}) async-start(), calls=%async_computation.4 | async-start | bytes 1216512 | tf_op jit(solution)/shard_map/all_gather | solution.py:233
  9.5 186.6 %all-gather.9.cloned.1.call-start = ((), (), s32[]{:S(2)}) async-start(), calls=%async_computation.5 | async-start | bytes 4866048 | tf_op jit(solution)/shard_map/all_gather | solution.py:233
  10.2 251.0 %all-gather.11.cloned.1.call-start = ((), (), s32[]{:S(2)}) async-start(), calls=%async_computation.6 | async-start | bytes 4866048 | tf_op jit(solution)/shard_map/all_gather | solution.py:233
  15.7 40.0 %collective-permute-start = (bf16[1024,768]{1,0:T(8,128)(2,1)}, bf16[1024,768]{1,0:T(8,128)(2,1)}, u32[]{:S(2)}, u32[]{:S(2)}) collective-permute-start(bf16[1024,768]{1,0:T(8,128)(2,1)} %bitcast_convert_fusion), channel_id=1, source_target_pairs={{0,1},{1,0},{2,3},{3,2},{4,5},{5,4},{6,7},{7,6},{8,9},{9,8},{10,11... | collective-permute-start | bytes 4718600 | tf_op jit(solution)/shard_map/ppermute | solution.py:237
  18.7 486.5 %reduce-scatter.10.cloned.1.call-start = ((), (), s32[]{:S(2)}) async-start(), calls=%async_computation.9 | async-start | bytes 4866048
  112.8 21.4 %copy-start.6 = (f32[8,256,128]{2,1,0:T(8,128)}, f32[8,256,128]{2,1,0:T(8,128)S(1)}, u32[]{:S(2)}) copy-start(f32[8,256,128]{2,1,0:T(8,128)S(1)} %get-tuple-element.22.lse_ref) | copy-start | bytes 3145732
  112.8 189.9 %copy-start.3 = (bf16[1024,768]{1,0:T(8,128)(2,1)}, bf16[1024,768]{1,0:T(8,128)(2,1)S(1)}, u32[]{:S(2)}) copy-start(bf16[1024,768]{1,0:T(8,128)(2,1)S(1)} %get-tuple-element.21.ctx_ref) | copy-start | bytes 4718596
  136.4 70.2 %copy-start.21 = (bf16[1024,768]{1,0:T(8,128)(2,1)}, bf16[1024,768]{1,0:T(8,128)(2,1)S(1)}, u32[]{:S(2)}) copy-start(bf16[1024,768]{1,0:T(8,128)(2,1)S(1)} %fusion.18) | copy-start | bytes 4718596
  390.5 227.0 %reduce-scatter.8.cloned.1.call-start = ((), (), s32[]{:S(2)}) async-start(), calls=%async_computation.8 | async-start | bytes 4866048 | tf_op jit(solution)/shard_map/reduce_scatter | solution.py:287
  401.3 327.9 %reduce-scatter.6.cloned.1.call-start = ((), (), s32[]{:S(2)}) async-start(), calls=%async_computation.7 | async-start | bytes 4866048 | tf_op jit(solution)/shard_map/reduce_scatter | solution.py:287
  414.8 7.9 %collective-permute-start.7 = (f32[7680]{0:T(1024)S(1)}, f32[7680]{0:T(1024)S(1)}, u32[]{:S(2)}, u32[]{:S(2)}) collective-permute-start(f32[7680]{0:T(1024)S(1)} %constant_dynamic-update-slice_fusion), channel_id=1, source_target_pairs={{0,1},{1,0},{2,3},{3,2},{4,5},{5,4},{6,7},{7,6},{8,9},{9,8},{10,11... | collective-permute-start | bytes 92168 | tf_op jit(solution)/shard_map/ppermute | solution.py:187
  420.6 68.4 %collective-permute-start.1 = (bf16[1024,768]{1,0:T(8,128)(2,1)S(1)}, bf16[1024,768]{1,0:T(8,128)(2,1)S(1)}, u32[]{:S(2)}, u32[]{:S(2)}) collective-permute-start(bf16[1024,768]{1,0:T(8,128)(2,1)S(1)} %add_convert_fusion.2), channel_id=1, source_target_pairs={{0,1},{1,0},{2,3},{3,2},{4,5},{5,4},{6,7},{7,6},{8,9},{9,8},{10,11... | collective-permute-start | bytes 4718600 | tf_op jit(solution)/shard_map/ppermute | solution.py:237
  421.6 55.4 %slice-start = ((s8[4718592]{0:T(1024)(128)(4,1)}), s8[4194304]{0:T(1024)(128)(4,1)S(1)}, s32[]{:S(2)}) async-start(s8[4718592]{0:T(1024)(128)(4,1)} %bitcast.106), calls=%async_computation.10 | async-start | bytes 8388608
  422.1 54.8 %slice-start.1 = ((s8[4718592]{0:T(1024)(128)(4,1)}), s8[524288]{0:T(1024)(128)(4,1)S(1)}, s32[]{:S(2)}) async-start(s8[4718592]{0:T(1024)(128)(4,1)} %bitcast.106), calls=%async_computation.11 | async-start | bytes 1048576
  422.7 1.3 collective-permute-start.8
  422.8 42.8 %collective-permute-start.2 = (f32[1536]{0:T(1024)S(1)}, f32[1536]{0:T(1024)S(1)}, u32[]{:S(2)}, u32[]{:S(2)}) collective-permute-start(f32[1536]{0:T(1024)S(1)} %pad_maximum_fusion.8), channel_id=1, source_target_pairs={{0,1},{1,0},{2,3},{3,2},{4,5},{5,4},{6,7},{7,6},{8,9},{9,8},{10,11... | collective-permute-start | bytes 18440 | tf_op jit(solution)/shard_map/ppermute | solution.py:187
  424.0 52.2 %collective-permute-start.9 = (f32[7680]{0:T(1024)S(1)}, f32[7680]{0:T(1024)S(1)}, u32[]{:S(2)}, u32[]{:S(2)}) collective-permute-start(f32[7680]{0:T(1024)S(1)} %add.274), channel_id=1, source_target_pairs={{0,4},{2,6},{4,0},{6,2},{8,12},{10,14},{12,8},{14,10},{16,20},{18,... | collective-permute-start | bytes 92168 | tf_op jit(solution)/shard_map/ppermute | solution.py:190
  465.6 1.2 collective-permute-start.3
  466.8 3.7 collective-permute-start.4
  470.5 3.7 collective-permute-start.5
  474.1 8.7 %collective-permute-start.6 = (f32[1536]{0:T(1024)S(1)}, f32[1536]{0:T(1024)S(1)}, u32[]{:S(2)}, u32[]{:S(2)}) collective-permute-start(f32[1536]{0:T(1024)S(1)} %add.271), channel_id=1, source_target_pairs={{0,16},{2,18},{4,20},{6,22},{8,24},{10,26},{12,28},{14,30},{16,0},... | collective-permute-start | bytes 18440 | tf_op jit(solution)/shard_map/ppermute | solution.py:190
  476.3 6.6 collective-permute-start.10
  482.9 4.9 collective-permute-start.11
  (47 other events, 235.1 us)
Sparse Core Ops, SparseCore 0:
  11.5 63.3 all-gather.4
  77.7 52.8 all-gather.6
  133.5 62.5 all-gather.8
  198.8 62.3 all-gather.10
  390.6 114.5 reduce-scatter.9
  511.4 106.0 reduce-scatter.7
  623.0 106.0 reduce-scatter.5

commit v2 on v1

v2 whole, which is shorter than its diff:
```python
import functools

import jax
import jax.numpy as jnp
from jax import lax
from jax.experimental import pallas as pl
from jax.experimental.pallas import tpu as pltpu
from jax.sharding import PartitionSpec as P

D = 768
H = 12
HD = 64
FF = 3072

NORM_EPSILON = 1e-12
BF = jnp.bfloat16
F32 = jnp.float32


def dot(a, b, da, db):
    return lax.dot_general(a, b, (((da,), (db,)), ((), ())), preferred_element_type=F32)


def layer_norm(resid, gain_vec, shift_vec):
    mean_value = jnp.mean(resid, -1, keepdims=True)
    centred = resid - mean_value
    variance = jnp.mean(centred * centred, -1, keepdims=True)
    inv_std = lax.rsqrt(variance + NORM_EPSILON)
    normed = centred * inv_std
    return (normed * gain_vec + shift_vec, normed, inv_std)


def norm_back(grad_in, normed, inv_std, gain_vec):
    scaled = grad_in * gain_vec
    return inv_std * (
        scaled
        - jnp.mean(scaled, -1, keepdims=True)
        - normed * jnp.mean(scaled * normed, -1, keepdims=True)
    )


def gelu_both(v):
    z = jnp.abs(v) * (0.5**0.5)
    t = 1.0 / (1.0 + 0.3275911 * z)
    gauss = jnp.exp(-0.5 * v * v)
    poly = t * (
        0.5 * 0.254829592
        + t * (0.5 * -0.284496736 + t * (0.5 * 1.421413741 + t * (0.5 * -1.453152027 + t * (0.5 * 1.061405429))))
    )
    tail = poly * gauss
    phi_cum = jnp.where(v < 0, tail, 1.0 - tail)
    return v * phi_cum, phi_cum + v * gauss * 0.3989422804014327


def attend_forward_kernel(heads, half, lens, tindex, q_ref, k_ref, v_ref, ctx_ref, lse_ref):
    length = lens[pl.program_id(0)]
    lane = lax.broadcasted_iota(jnp.int32, (1, half), 1)
    bias = [jnp.where(lane + place * half < length, 0.0, -1e30) for place in (tindex[0], 1 - tindex[0])]
    col = lax.broadcasted_iota(jnp.int32, (half, 128), 1)
    lse_tile = jnp.zeros((half, 128), F32)
    for h in range(heads):
        sl = slice(h * HD, (h + 1) * HD)
        q = q_ref[:, sl]
        s_own = dot(q, k_ref[0, :, sl], 1, 1) + bias[0]
        s_oth = dot(q, k_ref[1, :, sl], 1, 1) + bias[1]
        m = jnp.maximum(jnp.max(s_own, -1, keepdims=True), jnp.max(s_oth, -1, keepdims=True))
        e_own = jnp.exp(s_own - m)
        e_oth = jnp.exp(s_oth - m)
        total = jnp.sum(e_own, -1, keepdims=True) + jnp.sum(e_oth, -1, keepdims=True)
        c = dot(e_own.astype(BF), v_ref[0, :, sl], 1, 0) + dot(e_oth.astype(BF), v_ref[1, :, sl], 1, 0)
        ctx_ref[:, sl] = (c / total).astype(BF)
        lse_tile = jnp.where(col == h, m + jnp.log(total), lse_tile)
    lse_ref[0] = lse_tile


def attend_backward_kernel(
    heads, half, lens, tindex, q_ref, k_ref, v_ref, ctx_ref, lse_ref, dctx_ref, dq_ref, dk_ref, dv_ref
):
    length = lens[pl.program_id(0)]
    row = lax.broadcasted_iota(jnp.int32, (half, 1), 0)
    bias = [jnp.where(row + place * half < length, 0.0, -1e30) for place in (tindex[0], 1 - tindex[0])]
    lse_rows = jnp.transpose(lse_ref[0])
    prod = ctx_ref[...].astype(F32) * dctx_ref[...].astype(F32)
    col = lax.broadcasted_iota(jnp.int32, (half, 128), 1)
    delta_tile = jnp.zeros((half, 128), F32)
    for h in range(heads):
        delta_tile = jnp.where(
            col == h, jnp.sum(prod[:, h * HD : (h + 1) * HD], -1, keepdims=True), delta_tile
        )
    delta_rows = jnp.transpose(delta_tile)
    for h in range(heads):
        sl = slice(h * HD, (h + 1) * HD)
        q = q_ref[:, sl]
        dc = dctx_ref[:, sl]
        lse = lse_rows[h : h + 1, :]
        delta = delta_rows[h : h + 1, :]
        dq = None
        for i in range(2):
            k = k_ref[i, :, sl]
            p = jnp.exp(dot(k, q, 1, 1) + bias[i] - lse)
            dp = dot(v_ref[i, :, sl], dc, 1, 1)
            ds = (p * (dp - delta)).astype(BF)
            dk_ref[i, :, sl] = dot(ds, q, 1, 0).astype(BF)
            dv_ref[i, :, sl] = dot(p.astype(BF), dc, 1, 0).astype(BF)
            part = dot(ds, k, 0, 0)
            dq = part if dq is None else dq + part
        dq_ref[:, sl] = (dq * HD**-0.5).astype(BF)


def attend_specs(half, width):
    rows = pl.BlockSpec((half, width), lambda s, *_: (s, 0))
    pair = pl.BlockSpec((2, half, width), lambda s, *_: (0, s, 0))
    stat = pl.BlockSpec((1, half, 128), lambda s, *_: (s, 0, 0))
    return rows, pair, stat


def attend_forward(lengths, tindex, q, k, v, seqs):
    rows, width = q.shape
    half = rows // seqs
    flat, pair, stat = attend_specs(half, width)
    return pl.pallas_call(
        functools.partial(attend_forward_kernel, width // HD, half),
        grid_spec=pltpu.PrefetchScalarGridSpec(
            num_scalar_prefetch=2, grid=(seqs,), in_specs=[flat, pair, pair], out_specs=[flat, stat]
        ),
        out_shape=[
            jax.ShapeDtypeStruct((rows, width), BF),
            jax.ShapeDtypeStruct((seqs, half, 128), F32),
        ],
        compiler_params=pltpu.CompilerParams(vmem_limit_bytes=24 * 1024 * 1024),
        cost_estimate=pl.CostEstimate(flops=8_000_000_000, bytes_accessed=5_000_000, transcendentals=3_500_000),
        name="attend_forward",
    )(lengths, tindex, q, k, v)


def attend_backward(lengths, tindex, q, k, v, ctx, lse, dctx, seqs):
    rows, width = q.shape
    half = rows // seqs
    flat, pair, stat = attend_specs(half, width)
    return pl.pallas_call(
        functools.partial(attend_backward_kernel, width // HD, half),
        grid_spec=pltpu.PrefetchScalarGridSpec(
            num_scalar_prefetch=2,
            grid=(seqs,),
            in_specs=[flat, pair, pair, flat, stat, flat],
            out_specs=[flat, pair, pair],
        ),
        out_shape=[
            jax.ShapeDtypeStruct((rows, width), BF),
            jax.ShapeDtypeStruct((2, rows, width), BF),
            jax.ShapeDtypeStruct((2, rows, width), BF),
        ],
        compiler_params=pltpu.CompilerParams(vmem_limit_bytes=24 * 1024 * 1024),
        cost_estimate=pl.CostEstimate(flops=16_000_000_000, bytes_accessed=10_000_000, transcendentals=3_500_000),
        name="attend_backward",
    )(lengths, tindex, q, k, v, ctx, lse, dctx)


class Links:
    def __init__(self):
        self.dp_size = lax.axis_size("dp")
        self.hi_size = self.dp_size // 4
        index = lax.axis_index("dp")
        self.core = index & 1
        self.at = {"lo": (index >> 1) & 1, "tensor": lax.axis_index("tensor")}
        self.hi = index >> 2

    def over_dp(self, v, mask):
        return lax.ppermute(v, "dp", [(i, i ^ mask) for i in range(self.dp_size)])

    def swap(self, v, axis):
        if axis == "tensor":
            return lax.ppermute(v, "tensor", [(0, 1), (1, 0)])
        return self.over_dp(v, {"core": 1, "lo": 2}[axis])

    def over_hi(self, v, distance):
        return self.over_dp(v, 4 * distance)


def place_kernel(order, where, mine_ref, other_ref, *out_refs):
    hi_size = mine_ref.shape[2]

    def step(distance, carry):
        for i in range(2):
            for j in range(2):
                at = dict(zip(order, (where[0 if order[0] == "lo" else 1] ^ j, where[0 if order[1] == "lo" else 1] ^ i)))
                base = ((where[2] ^ distance) * 2 + at["lo"]) * 2
                for w, out_ref in enumerate(out_refs):
                    out_ref[at["tensor"], base + where[3]] = mine_ref[i, j, distance, w]
                    out_ref[at["tensor"], base + (1 - where[3])] = other_ref[i, j, distance, w]
        return carry

    lax.fori_loop(0, hi_size, step, 0)


def gather_tree(links, shards_in, order):
    stage = jnp.stack(shards_in)[None]
    stage = jnp.concatenate([stage] + [links.over_hi(stage, d) for d in range(1, links.hi_size)], 0)
    for axis in order:
        stage = jnp.stack([stage, links.swap(stage, axis)])
    other = links.swap(stage, "core")
    rows, columns = shards_in[0].shape
    where = jnp.stack([links.at["lo"], links.at["tensor"], links.hi, links.core]).astype(jnp.int32)
    blocks = links.dp_size
    full = pl.BlockSpec(memory_space=pltpu.VMEM)
    placed = pl.pallas_call(
        functools.partial(place_kernel, order),
        in_specs=[pl.BlockSpec(memory_space=pltpu.SMEM), full, full],
        out_specs=[full] * len(shards_in),
        out_shape=[jax.ShapeDtypeStruct((2, blocks, rows, columns), BF)] * len(shards_in),
        compiler_params=pltpu.CompilerParams(vmem_limit_bytes=48 * 1024 * 1024),
        cost_estimate=pl.CostEstimate(flops=0, bytes_accessed=4 * stage.size * 2, transcendentals=0),
        name="place_shards",
    )(where, stage, other)
    return [p.reshape(2, blocks * rows, columns) for p in placed]


def pick(v, index, axis=0):
    return lax.dynamic_index_in_dim(v, index, axis, keepdims=False)


def add_low(a, b):
    return (a.astype(F32) + b.astype(F32)).astype(BF)


def scatter_tree(links, parts, order):
    blocks = [[g.reshape(links.hi_size, 2, 2, -1, g.shape[1]) for g in half] for half in parts]

    def side(core):
        return jnp.stack([jnp.stack([pick(g, core, 2) for g in half]) for half in blocks])

    total = add_low(side(links.core), links.swap(side(1 - links.core), "core"))
    axes = ["tensor", "w", "hi", "lo"]
    for axis in order:
        at = axes.index(axis)
        here = links.at[axis]
        total = add_low(pick(total, here, at), links.swap(pick(total, 1 - here, at), axis))
        axes.pop(at)
    out = pick(total, links.hi, 1).astype(F32)
    for d in range(1, links.hi_size):
        out = out + links.over_hi(pick(total, links.hi ^ d, 1), d).astype(F32)
    return [out[w] for w in range(out.shape[0])]


def sum_everywhere(links, vec):
    first = vec + links.swap(vec, "tensor")
    vec = first
    bit = 1
    while bit < links.dp_size:
        vec = vec + links.over_dp(vec, bit)
        bit *= 2
    return vec, first


def split_vec(vec, sizes):
    out, at = [], 0
    for size in sizes:
        out.append(lax.slice_in_dim(vec, at, at + size))
        at += size
    return out


def shards(
    inputs,
    lengths,
    query_weight,
    key_weight,
    value_weight,
    query_bias,
    value_bias,
    out_weight,
    out_bias,
    first_gain,
    first_shift,
    input_projection_weight,
    input_projection_bias,
    output_projection_weight,
    output_projection_bias,
    second_gain,
    second_shift,
    out_cotangent,
):
    links = Links()
    half, seqs, _ = inputs.shape
    rows = half * seqs
    width = D // 2
    hidden_width = FF // 2
    tindex = jnp.reshape(links.at["tensor"], (1,)).astype(jnp.int32)
    everywhere = ("tensor", "dp")

    ffn_w = lax.all_gather(
        jnp.concatenate([input_projection_weight, output_projection_weight.T], 1), everywhere, axis=0, tiled=True
    ).reshape(2, D, 2 * hidden_width)
    up_w = [ffn_w[t, :, :hidden_width] for t in range(2)]
    down_w = [ffn_w[t, :, hidden_width:] for t in range(2)]
    inputs_seq = inputs.transpose(1, 0, 2).reshape(rows, D)
    rows_low = inputs_seq.astype(BF)
    query_w, key_w = gather_tree(links, [query_weight, key_weight], ("tensor", "lo"))
    value_w, out_w = gather_tree(links, [value_weight, out_weight.T], ("lo", "tensor"))
    rows_both = jnp.stack([rows_low, links.swap(rows_low, "tensor")])
    rows_flat = rows_both.reshape(2 * rows, D)
    queries, keys, values, context, log_sums = [], [], [], [], []
    for t in range(2):
        part = slice(t * width, (t + 1) * width)
        queries.append((dot(rows_low, query_w[t], 1, 0) + query_bias[part]).astype(BF) * jnp.array(HD**-0.5, BF))
        keys.append(dot(rows_flat, key_w[t], 1, 0).astype(BF).reshape(2, rows, width))
        values.append((dot(rows_flat, value_w[t], 1, 0) + value_bias[part]).astype(BF).reshape(2, rows, width))
        ctx, lse = attend_forward(lengths, tindex, queries[t], keys[t], values[t], seqs)
        context.append(ctx)
        log_sums.append(lse)
    attention = dot(context[0], out_w[0], 1, 1) + dot(context[1], out_w[1], 1, 1)
    hidden, normed_one, inv_one = layer_norm(inputs_seq + attention + out_bias, first_gain, first_shift)
    hidden_low = hidden.astype(BF)
    acts, slopes = [], []
    for t in range(2):
        pre = dot(hidden_low, up_w[t], 1, 0) + input_projection_bias[t * hidden_width : (t + 1) * hidden_width]
        act, slope = gelu_both(pre)
        acts.append(act.astype(BF))
        slopes.append(slope.astype(BF))
    branch = dot(acts[0], down_w[0], 1, 1) + dot(acts[1], down_w[1], 1, 1)
    outputs, normed_two, inv_two = layer_norm(
        hidden + branch + output_projection_bias, second_gain, second_shift
    )
    cotangent = out_cotangent.transpose(1, 0, 2).reshape(rows, D)
    second_grad = norm_back(cotangent, normed_two, inv_two, second_gain)
    second_gain_part = jnp.sum(cotangent * normed_two, axis=0)
    second_shift_part = jnp.sum(cotangent, axis=0)
    down_bias_part = jnp.sum(second_grad, axis=0)
    second_low = second_grad.astype(BF)
    (down_sum,) = scatter_tree(
        links, [[dot(second_low, acts[t], 0, 0).astype(BF)] for t in range(2)], ("tensor", "lo")
    )
    pre_grads, up_bias_parts = [], []
    for t in range(2):
        pre_grad = (dot(second_low, down_w[t], 1, 0) * slopes[t].astype(F32)).astype(BF)
        pre_grads.append(pre_grad)
        up_bias_parts.append(jnp.sum(pre_grad, axis=0, dtype=F32))
    (up_sum,) = scatter_tree(
        links, [[dot(hidden_low, pre_grads[t], 0, 0).astype(BF)] for t in range(2)], ("lo", "tensor")
    )
    hidden_grad = second_grad + (dot(pre_grads[0], up_w[0], 1, 1) + dot(pre_grads[1], up_w[1], 1, 1))
    first_grad = norm_back(hidden_grad, normed_one, inv_one, first_gain)
    first_gain_part = jnp.sum(hidden_grad * normed_one, axis=0)
    first_shift_part = jnp.sum(hidden_grad, axis=0)
    out_bias_part = jnp.sum(first_grad, axis=0)
    first_low = first_grad.astype(BF)
    early, _ = sum_everywhere(
        links,
        jnp.concatenate(
            [
                out_bias_part,
                first_gain_part,
                first_shift_part,
                down_bias_part,
                second_gain_part,
                second_shift_part,
                *up_bias_parts,
            ]
        ),
    )
    out_bias_sum, first_gain_sum, first_shift_sum, down_bias_sum, second_gain_sum, second_shift_sum, up_bias_sum = (
        split_vec(early, [D] * 6 + [FF])
    )
    query_grads, key_grads, value_grads = [], [], []
    for t in range(2):
        context_grad = dot(first_low, out_w[t], 1, 0).astype(BF)
        dq, dk, dv = attend_backward(
            lengths, tindex, queries[t], keys[t], values[t], context[t], log_sums[t], context_grad, seqs
        )
        query_grads.append(dq)
        key_grads.append(dk)
        value_grads.append(dv)
    late, late_first = sum_everywhere(
        links,
        jnp.concatenate(
            [jnp.sum(g, axis=0, dtype=F32) for g in query_grads]
            + [jnp.sum(g, axis=(0, 1), dtype=F32) for g in value_grads]
        ),
    )
    query_bias_sum, value_bias_sum = split_vec(late, [D, D])

    def back(side):
        return sum(dot(key_grads[t][side], key_w[t], 1, 1) + dot(value_grads[t][side], value_w[t], 1, 1) for t in range(2))

    other_total, _ = lax.optimization_barrier((back(1).astype(BF), late_first))
    from_other = links.swap(other_total, "tensor")
    own_total = back(0) + (dot(query_grads[0], query_w[0], 1, 1) + dot(query_grads[1], query_w[1], 1, 1))
    input_grad = first_grad + (own_total + from_other.astype(F32))
    query_key_parts, value_out_parts = [], []
    for t in range(2):
        query_key_parts.append(
            [
                dot(rows_low, query_grads[t], 0, 0).astype(BF),
                dot(rows_flat, key_grads[t].reshape(2 * rows, width), 0, 0).astype(BF),
            ]
        )
        value_out_parts.append(
            [
                dot(rows_flat, value_grads[t].reshape(2 * rows, width), 0, 0).astype(BF),
                dot(first_low, context[t], 0, 0).astype(BF),
            ]
        )
    query_sum, key_sum = scatter_tree(links, query_key_parts, ("lo", "tensor"))
    value_sum, out_sum = scatter_tree(links, value_out_parts, ("lo", "tensor"))

    def positions_first(v):
        return v.reshape(seqs, half, D).transpose(1, 0, 2)

    return (
        positions_first(outputs),
        positions_first(input_grad),
        query_sum,
        key_sum,
        value_sum,
        query_bias_sum,
        value_bias_sum,
        out_sum.T,
        out_bias_sum,
        first_gain_sum,
        first_shift_sum,
        up_sum,
        up_bias_sum,
        down_sum.T,
        down_bias_sum,
        second_gain_sum,
        second_shift_sum,
    )


def solution(mesh):
    in_specs = (
        P("tensor", "dp", None),
        P("dp"),
        P("dp", "tensor"),
        P("dp", "tensor"),
        P("dp", "tensor"),
        P(),
        P(),
        P("tensor", "dp"),
        P(),
        P(),
        P(),
        P("dp", "tensor"),
        P(),
        P("tensor", "dp"),
        P(),
        P(),
        P(),
        P("tensor", "dp", None),
    )
    out_specs = (
        P("tensor", "dp", None),
        P("tensor", "dp", None),
        P("dp", "tensor"),
        P("dp", "tensor"),
        P("dp", "tensor"),
        P(),
        P(),
        P("tensor", "dp"),
        P(),
        P(),
        P(),
        P("dp", "tensor"),
        P(),
        P("tensor", "dp"),
        P(),
        P(),
        P(),
    )
    return jax.shard_map(shards, mesh=mesh, in_specs=in_specs, out_specs=out_specs, check_vma=False)
```

time: 745 us -> 509 us (0.68)
  waiting for transfers between devices: 454 us -> 118 us
  starting transfers between devices: 15.8 us -> 62.5 us
  local copies, waits for them, and re-layouts: 37.9 us -> 64.4 us
  other arithmetic: 42.8 us -> 56.1 us
  matrix products: 116 us -> 126 us
    reduce_scatter x2 -> x0, waiting for transfers between devices: 218 us -> none  [scatter(): return lax.psum_scatter(full, everywhere, scatter_dimension=0, tiled=True)]
    all_gather x4 -> x1, waiting for transfers between devices: 142 us -> 0.01 us  [shards(): lax.all_gather(jnp.concatenate([input_projection_weight, output_projectio...]
    ppermute x10 -> x38, starting transfers between devices: 11.6 us -> 53.5 us  [over_dp(): return lax.ppermute(v, 'dp', [(i, i ^ mask) for i in range(self.dp_size)])]
    ppermute x2 -> x10, waiting for transfers between devices: 33.8 us -> 65.8 us  [swap(): return lax.ppermute(v, 'tensor', [(0, 1), (1, 0)])]
    concatenate x7 -> x2, other arithmetic: 26.4 us -> 1.72 us  [the longest x1 1.72 us: shards(): jnp.concatenate([input_projection_weight, output_projection_weight.T], 1)]
    dynamic_slice x0 -> x24, local copies, waits for them, and re-layouts: none -> 16 us  [pick(): return lax.dynamic_index_in_dim(v, index, axis, keepdims=False)]
    another operation x2 -> x20, other arithmetic: 0.77 us -> 16.2 us  [the longest x12 8.89 us: side(): jnp.stack([jnp.stack([pick(g, core, 2) for g in half]) for half in blocks])]
    unnamed x8 -> x1, waiting for transfers between devices: 11.7 us -> 0.02 us
  transfers between devices with their start and end apart: 19 -> 49, of which waited for: 13 -> 22; matrix products, arithmetic and copies ran while one was open for 13% -> 21% of each run, Pallas kernels for 3% -> 5%
where the time goes in v2:
time: 509 us; the launch traced here: 503 us
  matrix products  126 us (25%)
  waiting for transfers between devices  118 us (23%)
  local copies, waits for them, and re-layouts  64.4 us (13%)
  starting transfers between devices  62.5 us (12%)
  Pallas kernels  59.1 us (12%)
  other arithmetic  56.1 us (11%)
  between operations  16.1 us (3%)
    dot_general x40, matrix products, dot(): lax.dot_general(a, b, (((da,), (db,)), ((), ())), preferred_element_type=...  126 us
    ppermute x10, waiting for transfers between devices, swap(): return lax.ppermute(v, 'tensor', [(0, 1), (1, 0)])  65.8 us
    ppermute x38, starting transfers between devices, over_dp(): return lax.ppermute(v, 'dp', [(i, i ^ mask) for i in range(self.dp_size)])  53.5 us
    ppermute x38, waiting for transfers between devices, over_dp(): return lax.ppermute(v, 'dp', [(i, i ^ mask) for i in range(self.dp_size)])  52.6 us
    pallas_call x2, Pallas kernels, attend_backward(): pl.pallas_call(functools.partial(attend_backward_kernel, width // HD, hal...  35.8 us
    pallas_call x2, Pallas kernels, attend_forward(): pl.pallas_call(functools.partial(attend_forward_kernel, width // HD, half...  20.6 us
    unnamed x179, local copies, waits for them, and re-layouts  18.3 us
    dynamic_slice x24, local copies, waits for them, and re-layouts, pick(): return lax.dynamic_index_in_dim(v, index, axis, keepdims=False)  16 us
  transfers between devices with their start and end apart: 49, of which 22 were waited for; matrix products, arithmetic and copies ran while one was open for 21% of the time, Pallas kernels for 5%

profile of v2, /device:TPU:0, one launch (start us, length us, event | category | flops | bytes accessed | tf_op | source)
XLA Modules:
  0.0 503.0 jit_solution(17181807140879199867)
XLA Ops:
  24.1 5.5 %collective-permute-done.1 = bf16[1,2,48,384]{3,2,1,0:T(8,128)(2,1)S(1)} collective-permute-done((bf16[1,2,48,384]{3,2,1,0:T(8,128)(2,1)S(1)}, bf16[1,2,48,384]{3,2,1,0:T(8,128)(2,1)S(1)}, u32[]{:S(2)}, u32[]{:S(2)}) %collective-permute-start.1) | collective-permute-done | bytes 73760 | tf_op jit(solution)/shard_map/ppermute | solution.py:169
  35.5 4.1 collective-permute-done.3
  51.5 5.1 %collective-permute-done.11 = bf16[2,4,2,48,384]{4,3,2,1,0:T(8,128)(2,1)} collective-permute-done((bf16[2,4,2,48,384]{4,3,2,1,0:T(8,128)(2,1)}, bf16[2,4,2,48,384]{4,3,2,1,0:T(8,128)(2,1)}, u32[]{:S(2)}, u32[]{:S(2)}) %collective-permute-start.11) | collective-permute-done | bytes 589856 | tf_op jit(solution)/shard_map/ppermute | solution.py:173
  68.9 34.9 %collective-permute-done.6 = bf16[1024,768]{1,0:T(8,128)(2,1)} collective-permute-done((bf16[1024,768]{1,0:T(8,128)(2,1)}, bf16[1024,768]{1,0:T(8,128)(2,1)}, u32[]{:S(2)}, u32[]{:S(2)}) %collective-permute-start.6) | collective-permute-done | bytes 1572896 | tf_op jit(solution)/shard_map/ppermute | solution.py:173
  115.3 10.1 %attend_forward.3 = (bf16[1024,384]{1,0:T(8,128)(2,1)S(1)}, f32[4,256,128]{2,1,0:T(8,128)S(1)}) custom-call(s32[4]{0:T(128)S(1)} %copy-done.2, s32[1]{0:T(128)} %bitcast.2.tindex, bf16[1024,384]{1,0:T(8,128)(2,1)S(1)} %fusion.29.q_ref, bf16[2,1024,384]{2,1,0:T(8,128)(2,1)S(1)} %bitcast.399, bf16[2,1024,384]{2,1,0:T(8,128)(2,1)S(1)} %bitcast.401), custom_call_target="tpu_custom_call" | custom-call | flops 8000000000 | bytes 5000000 | tf_op jit(solution)/shard_map/attend_forward/pallas_call | solution.py:121
  130.2 10.5 %attend_forward.2 = (bf16[1024,384]{1,0:T(8,128)(2,1)S(1)}, f32[4,256,128]{2,1,0:T(8,128)S(1)}) custom-call(s32[4]{0:T(128)S(1)} %copy-done.2, s32[1]{0:T(128)} %bitcast.2.tindex, bf16[1024,384]{1,0:T(8,128)(2,1)S(1)} %fusion.30.q_ref, bf16[2,1024,384]{2,1,0:T(8,128)(2,1)S(1)} %bitcast.403, bf16[2,1024,384]{2,1,0:T(8,128)(2,1)S(1)} %bitcast.405), custom_call_target="tpu_custom_call" | custom-call | flops 8000000000 | bytes 5000000 | tf_op jit(solution)/shard_map/attend_forward/pallas_call | solution.py:121
  145.4 9.9 %multiply_convert_fusion.3 = (bf16[1024,1536]{1,0:T(8,128)(2,1)S(1)}, f32[1024,1536]{1,0:T(8,128)}) fusion(f32[1536]{0:T(1024)S(1)} %copy-done.76, bf16[1024,768]{1,0:T(8,128)(2,1)} %fusion.14, bf16[2,768,3072]{2,1,0:T(8,128)(2,1)} %bitcast.480), kind=kOutput, calls=%fused_computation.21 | convolution fusion | flops 2450522112 | bytes 13375488 | tf_op jit(solution)/shard_map/dot_general | solution.py:21
  158.0 8.4 %multiply_convert_fusion.2 = (bf16[1024,1536]{1,0:T(8,128)(2,1)S(1)}, f32[1024,1536]{1,0:T(8,128)}) fusion(f32[1536]{0:T(1024)S(1)} %copy-done.75, bf16[1024,768]{1,0:T(8,128)(2,1)S(1)} %copy-done.61, bf16[2,768,3072]{2,1,0:T(8,128)(2,1)S(1)} %bitcast.483), kind=kOutput, calls=%fused_computation.20 | convolution fusion | flops 2450522112 | bytes 13377536 | tf_op jit(solution)/shard_map/dot_general | solution.py:21
  181.3 9.1 %convert_reduce_fusion.1 = (f32[1536]{0:T(1024)S(1)}, bf16[1024,1536]{1,0:T(8,128)(2,1)S(1)}) fusion(f32[1024,1536]{1,0:T(8,128)} %get-tuple-element.131, f32[1536]{0:T(1024)S(1)} %copy-done.76, bf16[1024,768]{1,0:T(8,128)(2,1)S(1)} %convert_element_type.413, bf16[2,768,3072]{2,1,0:T(8,128)(2,1)S(1)} %bitcast.485), kind=kOutput, calls=%fused_computation.17 | convolution fusion | flops 2461530624 | bytes 13383680 | tf_op jit(solution)/shard_map/dot_general | solution.py:21
  193.7 4.3 fusion.17
  198.0 9.1 %convert_reduce_fusion = (f32[1536]{0:T(1024)S(1)}, bf16[1024,1536]{1,0:T(8,128)(2,1)S(1)}) fusion(f32[1024,1536]{1,0:T(8,128)} %get-tuple-element.133, f32[1536]{0:T(1024)S(1)} %copy-done.75, bf16[1024,768]{1,0:T(8,128)(2,1)S(1)} %convert_element_type.413, bf16[2,768,3072]{2,1,0:T(8,128)(2,1)S(1)} %bitcast.487), kind=kOutput, calls=%fused_computation.16 | convolution fusion | flops 2461530624 | bytes 13383680 | tf_op jit(solution)/shard_map/dot_general | solution.py:21
  211.8 6.5 %multiply_reduce_fusion = (f32[768]{0:T(1024)S(1)}, f32[1024]{0:T(1024)S(1)}, f32[1024]{0:T(1024)S(1)}, f32[768]{0:T(1024)S(1)}, f32[1024,768]{1,0:T(8,128)S(1)}) fusion(f32[1024,768]{1,0:T(8,128)S(1)} %copy-done.18, f32[1024]{0:T(1024)S(1)} %add_rsqrt_fusion.1, f32[1024]{0:T(1024)S(1)} %broadcast_multiply_fusion.5, f32[768]{0:T(1024)S(1)} %copy-done.73, ...), kind=kOutput, calls=%fused_computation.38 | convolution fusion | flops 2424566272 | bytes 18113536 | tf_op jit(solution)/shard_map/dot_general | solution.py:21
  223.8 18.1 %attend_backward.2 = (bf16[1024,384]{1,0:T(8,128)(2,1)S(1)}, bf16[2,1024,384]{2,1,0:T(8,128)(2,1)S(1)}, bf16[2,1024,384]{2,1,0:T(8,128)(2,1)S(1)}) custom-call(s32[4]{0:T(128)S(1)} %copy-done.2, s32[1]{0:T(128)} %bitcast.2.tindex, bf16[1024,384]{1,0:T(8,128)(2,1)S(1)} %copy-done.12, bf16[2,1024,384]{2,1,0:T(8,128)(2,1)S(1)} %bitcast.404, ...), custom_call_target="tpu_custom_call" | custom-call | flops 16000000000 | bytes 10000000 | tf_op jit(solution)/shard_map/attend_backward/pallas_call | solution.py:140
  247.7 17.8 %attend_backward.3 = (bf16[1024,384]{1,0:T(8,128)(2,1)S(1)}, bf16[2,1024,384]{2,1,0:T(8,128)(2,1)S(1)}, bf16[2,1024,384]{2,1,0:T(8,128)(2,1)S(1)}) custom-call(s32[4]{0:T(128)S(1)} %copy-done.2, s32[1]{0:T(128)} %bitcast.2.tindex, bf16[1024,384]{1,0:T(8,128)(2,1)S(1)} %copy-done.10, bf16[2,1024,384]{2,1,0:T(8,128)(2,1)S(1)} %bitcast.400, ...), custom_call_target="tpu_custom_call" | custom-call | flops 16000000000 | bytes 10000000 | tf_op jit(solution)/shard_map/attend_backward/pallas_call | solution.py:140
  289.8 4.1 fusion.24
  361.2 3.7 copy.245
  379.7 10.0 %add_add_fusion = f32[1024,768]{1,0:T(8,128)} fusion(f32[1024,768]{1,0:T(8,128)S(1)} %copy-done.21, bf16[1024,768]{1,0:T(8,128)(2,1)} %collective-permute-done.14, f32[1024,768]{1,0:T(8,128)} %fusion.91, f32[1024,768]{1,0:T(8,128)} %fusion.92, f32[1024,768]{1,0:T(8,128)} %fusion.46, f32[1024,768]{1,0:T(8,128)} %fusion.44, f32[1024,768]{1,0:T(8,128)} %fusion.50, ...), kind=kLoop, calls=%fused_computation.39 | loop fusion | flops 6291456 | bytes 26738688 | tf_op jit(solution)/shard_map/add | solution.py:388
  389.7 6.0 %copy.244 = f32[4,256,768]{2,0,1:T(4,128)} copy(f32[4,256,768]{2,1,0:T(8,128)} %bitcast.408) | data formatting | bytes 6291456 | tf_op jit(solution)/shard_map/reshape | solution.py:407
  397.3 5.9 %collective-permute-done.16 = bf16[2,2,4,48,384]{4,3,2,1,0:T(8,128)(2,1)} collective-permute-done((bf16[2,2,4,48,384]{4,3,2,1,0:T(8,128)(2,1)}, bf16[2,2,4,48,384]{4,3,2,1,0:T(8,128)(2,1)}, u32[]{:S(2)}, u32[]{:S(2)}) %collective-permute-start.16) | collective-permute-done | bytes 589856 | tf_op jit(solution)/shard_map/ppermute | solution.py:169
  435.1 18.5 %collective-permute-done.43 = bf16[1,4,2,48,1536]{4,3,1,2,0:T(8,128)(2,1)S(1)} collective-permute-done((bf16[1,4,2,48,1536]{4,3,1,2,0:T(8,128)(2,1)S(1)}, bf16[1,4,2,48,1536]{4,3,1,2,0:T(8,128)(2,1)S(1)}, u32[]{:S(2)}, u32[]{:S(2)}) %collective-permute-start.43) | collective-permute-done | bytes 1179680 | tf_op jit(solution)/shard_map/ppermute | solution.py:173
  455.2 5.5 %collective-permute-done.37 = bf16[2,1,4,48,1536]{4,3,2,1,0:T(8,128)(2,1)S(1)} collective-permute-done((bf16[2,1,4,48,1536]{4,3,2,1,0:T(8,128)(2,1)S(1)}, bf16[2,1,4,48,1536]{4,3,2,1,0:T(8,128)(2,1)S(1)}, u32[]{:S(2)}, u32[]{:S(2)}) %collective-permute-start.37) | collective-permute-done | bytes 1179680 | tf_op jit(solution)/shard_map/ppermute | solution.py:169
  462.3 7.1 %collective-permute-done.44 = bf16[1,4,48,1536]{3,2,1,0:T(8,128)(2,1)S(1)} collective-permute-done((bf16[1,4,48,1536]{3,2,1,0:T(8,128)(2,1)S(1)}, bf16[1,4,48,1536]{3,2,1,0:T(8,128)(2,1)S(1)}, u32[]{:S(2)}, u32[]{:S(2)}) %collective-permute-start.44) | collective-permute-done | bytes 589856 | tf_op jit(solution)/shard_map/ppermute | solution.py:169
  481.3 4.1 collective-permute-done.46
  486.2 8.7 %collective-permute-done.40 = bf16[1,48,1536]{2,1,0:T(8,128)(2,1)S(1)} collective-permute-done((bf16[1,48,1536]{2,1,0:T(8,128)(2,1)S(1)}, bf16[1,48,1536]{2,1,0:T(8,128)(2,1)S(1)}, u32[]{:S(2)}, u32[]{:S(2)}) %collective-permute-start.40) | collective-permute-done | bytes 147488 | tf_op jit(solution)/shard_map/ppermute | solution.py:169
  (431 shorter events, 259.9 us)
Async XLA Ops:
  7.2 138.2 %all-gather.2.cloned.1.call-start = ((), (), s32[]{:S(2)}) async-start(), calls=%async_computation | async-start | bytes 9732096 | tf_op jit(solution)/shard_map/all_gather | solution.py:291
  17.2 12.4 %collective-permute-start.1 = (bf16[1,2,48,384]{3,2,1,0:T(8,128)(2,1)S(1)}, bf16[1,2,48,384]{3,2,1,0:T(8,128)(2,1)S(1)}, u32[]{:S(2)}, u32[]{:S(2)}) collective-permute-start(bf16[1,2,48,384]{3,2,1,0:T(8,128)(2,1)S(1)} %maximum_bitcast_fusion.8), channel_id=1, source_target_pairs={{0,16},{2,18},{4,20},{6,22},{8,24},{10,26},{12,28},{14,30},{16,0},... | collective-permute-start | bytes 221192 | tf_op jit(solution)/shard_map/ppermute | solution.py:169
  35.0 21.5 %collective-permute-start.11 = (bf16[2,4,2,48,384]{4,3,2,1,0:T(8,128)(2,1)}, bf16[2,4,2,48,384]{4,3,2,1,0:T(8,128)(2,1)}, u32[]{:S(2)}, u32[]{:S(2)}) collective-permute-start(bf16[2,4,2,48,384]{4,3,2,1,0:T(8,128)(2,1)} %get-tuple-element.97), channel_id=1, source_target_pairs={{0,1},{1,0},{2,3},{3,2},{4,5},{5,4},{6,7},{7,6},{8,9},{9,8},{10,11... | collective-permute-start | bytes 1769480 | tf_op jit(solution)/shard_map/ppermute | solution.py:173
  40.7 18.1 %collective-permute-start.4 = (bf16[2,4,2,48,384]{4,3,2,1,0:T(8,128)(2,1)}, bf16[2,4,2,48,384]{4,3,2,1,0:T(8,128)(2,1)}, u32[]{:S(2)}, u32[]{:S(2)}) collective-permute-start(bf16[2,4,2,48,384]{4,3,2,1,0:T(8,128)(2,1)} %get-tuple-element.99), channel_id=1, source_target_pairs={{0,4},{2,6},{4,0},{6,2},{8,12},{10,14},{12,8},{14,10},{16,20},{18,... | collective-permute-start | bytes 1769480 | tf_op jit(solution)/shard_map/ppermute | solution.py:169
  43.6 60.2 %collective-permute-start.6 = (bf16[1024,768]{1,0:T(8,128)(2,1)}, bf16[1024,768]{1,0:T(8,128)(2,1)}, u32[]{:S(2)}, u32[]{:S(2)}) collective-permute-start(bf16[1024,768]{1,0:T(8,128)(2,1)} %bitcast_convert_fusion), channel_id=1, source_target_pairs={{0,1},{1,0},{2,3},{3,2},{4,5},{5,4},{6,7},{7,6},{8,9},{9,8},{10,11... | collective-permute-start | bytes 4718600 | tf_op jit(solution)/shard_map/ppermute | solution.py:173
  57.8 48.4 %collective-permute-start.12 = (bf16[2,2,4,2,48,384]{5,4,3,2,1,0:T(8,128)(2,1)S(1)}, bf16[2,2,4,2,48,384]{5,4,3,2,1,0:T(8,128)(2,1)S(1)}, u32[]{:S(2)}, u32[]{:S(2)}) collective-permute-start(bf16[2,2,4,2,48,384]{5,4,3,2,1,0:T(8,128)(2,1)S(1)} %pad_maximum_fusion.4.mine_ref), channel_id=1, source_target_pairs={{0,2},{2,0},{4,6},{6,4},{8,10},{10,8},{12,14},{14,12},{16,18},{18,... | collective-permute-start | bytes 3538952 | tf_op jit(solution)/shard_map/ppermute | solution.py:169
  60.1 47.1 %collective-permute-start.5 = (bf16[2,2,4,2,48,384]{5,4,3,2,1,0:T(8,128)(2,1)S(1)}, bf16[2,2,4,2,48,384]{5,4,3,2,1,0:T(8,128)(2,1)}, u32[]{:S(2)}, u32[]{:S(2)}) collective-permute-start(bf16[2,2,4,2,48,384]{5,4,3,2,1,0:T(8,128)(2,1)S(1)} %pad_maximum_fusion.3.mine_ref), channel_id=1, source_target_pairs={{0,2},{2,0},{4,6},{6,4},{8,10},{10,8},{12,14},{14,12},{16,18},{18,... | collective-permute-start | bytes 3538952 | tf_op jit(solution)/shard_map/ppermute | solution.py:169
  315.8 30.0 %collective-permute-start.31 = (f32[7680]{0:T(1024)S(1)}, f32[7680]{0:T(1024)S(1)}, u32[]{:S(2)}, u32[]{:S(2)}) collective-permute-start(f32[7680]{0:T(1024)S(1)} %constant_dynamic-update-slice_fusion), channel_id=1, source_target_pairs={{0,1},{1,0},{2,3},{3,2},{4,5},{5,4},{6,7},{7,6},{8,9},{9,8},{10,11... | collective-permute-start | bytes 92168 | tf_op jit(solution)/shard_map/ppermute | solution.py:173
  316.2 26.2 %collective-permute-start.13 = (f32[1536]{0:T(1024)S(1)}, f32[1536]{0:T(1024)S(1)}, u32[]{:S(2)}, u32[]{:S(2)}) collective-permute-start(f32[1536]{0:T(1024)S(1)} %pad_maximum_fusion.12), channel_id=1, source_target_pairs={{0,1},{1,0},{2,3},{3,2},{4,5},{5,4},{6,7},{7,6},{8,9},{9,8},{10,11... | collective-permute-start | bytes 18440 | tf_op jit(solution)/shard_map/ppermute | solution.py:173
  322.5 48.5 %collective-permute-start.21 = (bf16[2,2,4,2,48,384]{5,4,1,2,0,3:T(8,128)(2,1)}, bf16[2,2,4,2,48,384]{5,4,1,2,0,3:T(8,128)(2,1)}, u32[]{:S(2)}, u32[]{:S(2)}) collective-permute-start(bf16[2,2,4,2,48,384]{5,4,1,2,0,3:T(8,128)(2,1)} %pad_maximum_fusion.6), channel_id=1, source_target_pairs={{0,2},{2,0},{4,6},{6,4},{8,10},{10,8},{12,14},{14,12},{16,18},{18,... | collective-permute-start | bytes 3538952 | tf_op jit(solution)/shard_map/ppermute | solution.py:169
  335.2 40.7 %collective-permute-start.15 = (bf16[2,2,4,2,48,384]{5,4,3,2,1,0:T(8,128)(2,1)S(1)}, bf16[2,2,4,2,48,384]{5,4,3,2,1,0:T(8,128)(2,1)S(1)}, u32[]{:S(2)}, u32[]{:S(2)}) collective-permute-start(bf16[2,2,4,2,48,384]{5,4,3,2,1,0:T(8,128)(2,1)S(1)} %pad_maximum_fusion.5), channel_id=1, source_target_pairs={{0,2},{2,0},{4,6},{6,4},{8,10},{10,8},{12,14},{14,12},{16,18},{18,... | collective-permute-start | bytes 3538952 | tf_op jit(solution)/shard_map/ppermute | solution.py:169
  343.2 36.5 %collective-permute-start.14 = (bf16[1024,768]{1,0:T(8,128)(2,1)S(1)}, bf16[1024,768]{1,0:T(8,128)(2,1)}, u32[]{:S(2)}, u32[]{:S(2)}) collective-permute-start(bf16[1024,768]{1,0:T(8,128)(2,1)S(1)} %add_convert_fusion.2), channel_id=1, source_target_pairs={{0,1},{1,0},{2,3},{3,2},{4,5},{5,4},{6,7},{7,6},{8,9},{9,8},{10,11... | collective-permute-start | bytes 4718600 | tf_op jit(solution)/shard_map/ppermute | solution.py:173
  364.9 61.1 %collective-permute-start.42 = (bf16[2,1,4,2,48,1536]{5,4,2,3,1,0:T(8,128)(2,1)}, bf16[2,1,4,2,48,1536]{5,4,2,3,1,0:T(8,128)(2,1)}, u32[]{:S(2)}, u32[]{:S(2)}) collective-permute-start(bf16[2,1,4,2,48,1536]{5,4,2,3,1,0:T(8,128)(2,1)} %pad_maximum_fusion.2), channel_id=1, source_target_pairs={{0,2},{2,0},{4,6},{6,4},{8,10},{10,8},{12,14},{14,12},{16,18},{18,... | collective-permute-start | bytes 7077896 | tf_op jit(solution)/shard_map/ppermute | solution.py:169
  369.8 59.5 %collective-permute-start.36 = (bf16[2,1,4,2,48,1536]{5,4,2,0,3,1:T(8,128)(2,1)}, bf16[2,1,4,2,48,1536]{5,4,2,0,3,1:T(8,128)(2,1)}, u32[]{:S(2)}, u32[]{:S(2)}) collective-permute-start(bf16[2,1,4,2,48,1536]{5,4,2,0,3,1:T(8,128)(2,1)} %pad_maximum_fusion.1), channel_id=1, source_target_pairs={{0,2},{2,0},{4,6},{6,4},{8,10},{10,8},{12,14},{14,12},{16,18},{18,... | collective-permute-start | bytes 7077896 | tf_op jit(solution)/shard_map/ppermute | solution.py:169
  374.5 21.2 %collective-permute-start.22 = (bf16[2,2,4,48,384]{4,3,1,2,0:T(8,128)(2,1)}, bf16[2,2,4,48,384]{4,3,1,2,0:T(8,128)(2,1)}, u32[]{:S(2)}, u32[]{:S(2)}) collective-permute-start(bf16[2,2,4,48,384]{4,3,1,2,0:T(8,128)(2,1)} %dynamic-slice_bitcast_fusion.4), channel_id=1, source_target_pairs={{0,4},{2,6},{4,0},{6,2},{8,12},{10,14},{12,8},{14,10},{16,20},{18,... | collective-permute-start | bytes 1769480 | tf_op jit(solution)/shard_map/ppermute | solution.py:169
  378.1 25.1 %collective-permute-start.16 = (bf16[2,2,4,48,384]{4,3,2,1,0:T(8,128)(2,1)}, bf16[2,2,4,48,384]{4,3,2,1,0:T(8,128)(2,1)}, u32[]{:S(2)}, u32[]{:S(2)}) collective-permute-start(bf16[2,2,4,48,384]{4,3,2,1,0:T(8,128)(2,1)} %dynamic-slice_bitcast_fusion.5), channel_id=1, source_target_pairs={{0,4},{2,6},{4,0},{6,2},{8,12},{10,14},{12,8},{14,10},{16,20},{18,... | collective-permute-start | bytes 1769480 | tf_op jit(solution)/shard_map/ppermute | solution.py:169
  428.7 24.9 %collective-permute-start.43 = (bf16[1,4,2,48,1536]{4,3,1,2,0:T(8,128)(2,1)S(1)}, bf16[1,4,2,48,1536]{4,3,1,2,0:T(8,128)(2,1)S(1)}, u32[]{:S(2)}, u32[]{:S(2)}) collective-permute-start(bf16[1,4,2,48,1536]{4,3,1,2,0:T(8,128)(2,1)S(1)} %dynamic-slice_bitcast_fusion), channel_id=1, source_target_pairs={{0,1},{1,0},{2,3},{3,2},{4,5},{5,4},{6,7},{7,6},{8,9},{9,8},{10,11... | collective-permute-start | bytes 3538952 | tf_op jit(solution)/shard_map/ppermute | solution.py:173
  431.7 29.0 %collective-permute-start.37 = (bf16[2,1,4,48,1536]{4,3,2,1,0:T(8,128)(2,1)S(1)}, bf16[2,1,4,48,1536]{4,3,2,1,0:T(8,128)(2,1)S(1)}, u32[]{:S(2)}, u32[]{:S(2)}) collective-permute-start(bf16[2,1,4,48,1536]{4,3,2,1,0:T(8,128)(2,1)S(1)} %dynamic-slice_bitcast_fusion.1), channel_id=1, source_target_pairs={{0,4},{2,6},{4,0},{6,2},{8,12},{10,14},{12,8},{14,10},{16,20},{18,... | collective-permute-start | bytes 3538952 | tf_op jit(solution)/shard_map/ppermute | solution.py:169
  454.0 15.5 %collective-permute-start.44 = (bf16[1,4,48,1536]{3,2,1,0:T(8,128)(2,1)S(1)}, bf16[1,4,48,1536]{3,2,1,0:T(8,128)(2,1)S(1)}, u32[]{:S(2)}, u32[]{:S(2)}) collective-permute-start(bf16[1,4,48,1536]{3,2,1,0:T(8,128)(2,1)S(1)} %dynamic-slice_bitcast_fusion.2), channel_id=1, source_target_pairs={{0,4},{2,6},{4,0},{6,2},{8,12},{10,14},{12,8},{14,10},{16,20},{18,... | collective-permute-start | bytes 1769480 | tf_op jit(solution)/shard_map/ppermute | solution.py:169
  461.1 13.0 %collective-permute-start.38 = (bf16[1,4,48,1536]{3,2,1,0:T(8,128)(2,1)S(1)}, bf16[1,4,48,1536]{3,2,1,0:T(8,128)(2,1)S(1)}, u32[]{:S(2)}, u32[]{:S(2)}) collective-permute-start(bf16[1,4,48,1536]{3,2,1,0:T(8,128)(2,1)S(1)} %dynamic-slice_bitcast_fusion.3), channel_id=1, source_target_pairs={{0,1},{1,0},{2,3},{3,2},{4,5},{5,4},{6,7},{7,6},{8,9},{9,8},{10,11... | collective-permute-start | bytes 1769480 | tf_op jit(solution)/shard_map/ppermute | solution.py:173
  471.4 14.0 %collective-permute-start.46 = (bf16[1,48,1536]{2,1,0:T(8,128)(2,1)S(1)}, bf16[1,48,1536]{2,1,0:T(8,128)(2,1)S(1)}, u32[]{:S(2)}, u32[]{:S(2)}) collective-permute-start(bf16[1,48,1536]{2,1,0:T(8,128)(2,1)S(1)} %get-tuple-element.76), channel_id=1, source_target_pairs={{0,16},{2,18},{4,20},{6,22},{8,24},{10,26},{12,28},{14,30},{16,0},... | collective-permute-start | bytes 442376 | tf_op jit(solution)/shard_map/ppermute | solution.py:169
  472.3 13.2 %collective-permute-start.47 = (bf16[1,48,1536]{2,1,0:T(8,128)(2,1)S(1)}, bf16[1,48,1536]{2,1,0:T(8,128)(2,1)S(1)}, u32[]{:S(2)}, u32[]{:S(2)}) collective-permute-start(bf16[1,48,1536]{2,1,0:T(8,128)(2,1)S(1)} %get-tuple-element.75), channel_id=1, source_target_pairs={{0,24},{2,26},{4,28},{6,30},{8,16},{10,18},{12,20},{14,22},{16,8},... | collective-permute-start | bytes 442376 | tf_op jit(solution)/shard_map/ppermute | solution.py:169
  475.2 19.7 %collective-permute-start.40 = (bf16[1,48,1536]{2,1,0:T(8,128)(2,1)S(1)}, bf16[1,48,1536]{2,1,0:T(8,128)(2,1)S(1)}, u32[]{:S(2)}, u32[]{:S(2)}) collective-permute-start(bf16[1,48,1536]{2,1,0:T(8,128)(2,1)S(1)} %get-tuple-element.79), channel_id=1, source_target_pairs={{0,16},{2,18},{4,20},{6,22},{8,24},{10,26},{12,28},{14,30},{16,0},... | collective-permute-start | bytes 442376 | tf_op jit(solution)/shard_map/ppermute | solution.py:169
  479.8 15.1 %collective-permute-start.41 = (bf16[1,48,1536]{2,1,0:T(8,128)(2,1)S(1)}, bf16[1,48,1536]{2,1,0:T(8,128)(2,1)S(1)}, u32[]{:S(2)}, u32[]{:S(2)}) collective-permute-start(bf16[1,48,1536]{2,1,0:T(8,128)(2,1)S(1)} %get-tuple-element.78), channel_id=1, source_target_pairs={{0,24},{2,26},{4,28},{6,30},{8,16},{10,18},{12,20},{14,22},{16,8},... | collective-permute-start | bytes 442376 | tf_op jit(solution)/shard_map/ppermute | solution.py:169
  (109 other events, 673.3 us)
Sparse Core Ops, SparseCore 0:
  11.5 107.2 all-gather.1

commit v3 on v2

--- a/solution.py
+++ b/solution.py
@@ -52,33 +52,35 @@
     return v * phi_cum, phi_cum + v * gauss * 0.3989422804014327
 
 
+def mask_bias(half, axis, length, place):
+    shape = (1, half) if axis else (half, 1)
+    at = lax.broadcasted_iota(jnp.int32, shape, axis)
+    parts = [jnp.where(at + p * half < length, 0.0, -1e30) for p in (place, 1 - place)]
+    return jnp.concatenate(parts, axis)
+
+
 def attend_forward_kernel(heads, half, lens, tindex, q_ref, k_ref, v_ref, ctx_ref, lse_ref):
-    length = lens[pl.program_id(0)]
-    lane = lax.broadcasted_iota(jnp.int32, (1, half), 1)
-    bias = [jnp.where(lane + place * half < length, 0.0, -1e30) for place in (tindex[0], 1 - tindex[0])]
+    bias = mask_bias(half, 1, lens[pl.program_id(0)], tindex[0])
     col = lax.broadcasted_iota(jnp.int32, (half, 128), 1)
     lse_tile = jnp.zeros((half, 128), F32)
     for h in range(heads):
         sl = slice(h * HD, (h + 1) * HD)
-        q = q_ref[:, sl]
-        s_own = dot(q, k_ref[0, :, sl], 1, 1) + bias[0]
-        s_oth = dot(q, k_ref[1, :, sl], 1, 1) + bias[1]
-        m = jnp.maximum(jnp.max(s_own, -1, keepdims=True), jnp.max(s_oth, -1, keepdims=True))
-        e_own = jnp.exp(s_own - m)
-        e_oth = jnp.exp(s_oth - m)
-        total = jnp.sum(e_own, -1, keepdims=True) + jnp.sum(e_oth, -1, keepdims=True)
-        c = dot(e_own.astype(BF), v_ref[0, :, sl], 1, 0) + dot(e_oth.astype(BF), v_ref[1, :, sl], 1, 0)
-        ctx_ref[:, sl] = (c / total).astype(BF)
+        k = k_ref[:, :, sl].reshape(2 * half, HD)
+        v = v_ref[:, :, sl].reshape(2 * half, HD)
+        s = dot(q_ref[:, sl], k, 1, 1) + bias
+        m = jnp.max(s, -1, keepdims=True)
+        e = jnp.exp(s - m)
+        total = jnp.sum(e, -1, keepdims=True)
+        ctx_ref[:, sl] = (dot(e.astype(BF), v, 1, 0) / total).astype(BF)
         lse_tile = jnp.where(col == h, m + jnp.log(total), lse_tile)
     lse_ref[0] = lse_tile
 
 
 def attend_backward_kernel(
-    heads, half, lens, tindex, q_ref, k_ref, v_ref, ctx_ref, lse_ref, dctx_ref, dq_ref, dk_ref, dv_ref
+    heads, half, lens, tindex, q_ref, k_ref, v_ref, ctx_ref, lse_ref, dctx_ref, *rest
 ):
-    length = lens[pl.program_id(0)]
-    row = lax.broadcasted_iota(jnp.int32, (half, 1), 0)
-    bias = [jnp.where(row + place * half < length, 0.0, -1e30) for place in (tindex[0], 1 - tindex[0])]
+    dq_ref, dk_ref, dv_ref, sums_ref = rest[-4:]
+    bias = mask_bias(half, 0, lens[pl.program_id(0)], tindex[0])
     lse_rows = jnp.transpose(lse_ref[0])
     prod = ctx_ref[...].astype(F32) * dctx_ref[...].astype(F32)
     col = lax.broadcasted_iota(jnp.int32, (half, 128), 1)
@@ -92,19 +94,17 @@
         sl = slice(h * HD, (h + 1) * HD)
         q = q_ref[:, sl]
         dc = dctx_ref[:, sl]
-        lse = lse_rows[h : h + 1, :]
-        delta = delta_rows[h : h + 1, :]
-        dq = None
-        for i in range(2):
-            k = k_ref[i, :, sl]
-            p = jnp.exp(dot(k, q, 1, 1) + bias[i] - lse)
-            dp = dot(v_ref[i, :, sl], dc, 1, 1)
-            ds = (p * (dp - delta)).astype(BF)
-            dk_ref[i, :, sl] = dot(ds, q, 1, 0).astype(BF)
-            dv_ref[i, :, sl] = dot(p.astype(BF), dc, 1, 0).astype(BF)
-            part = dot(ds, k, 0, 0)
-            dq = part if dq is None else dq + part
-        dq_ref[:, sl] = (dq * HD**-0.5).astype(BF)
+        k = k_ref[:, :, sl].reshape(2 * half, HD)
+        v = v_ref[:, :, sl].reshape(2 * half, HD)
+        p = jnp.exp(dot(k, q, 1, 1) + bias - lse_rows[h : h + 1, :])
+        ds = (p * (dot(v, dc, 1, 1) - delta_rows[h : h + 1, :])).astype(BF)
+        dk_ref[:, :, sl] = dot(ds, q, 1, 0).astype(BF).reshape(2, half, HD)
+        dv = dot(p.astype(BF), dc, 1, 0).astype(BF)
+        dv_ref[:, :, sl] = dv.reshape(2, half, HD)
+        dq = (dot(ds, k, 0, 0) * HD**-0.5).astype(BF)
+        dq_ref[:, sl] = dq
+        sums_ref[0, 0:1, sl] = jnp.sum(dq.astype(F32), 0, keepdims=True)
+        sums_ref[0, 1:2, sl] = jnp.sum(dv.astype(F32), 0, keepdims=True)
 
 
 def attend_specs(half, width):
@@ -133,27 +133,172 @@
     )(lengths, tindex, q, k, v)
 
 
-def attend_backward(lengths, tindex, q, k, v, ctx, lse, dctx, seqs):
+def attend_backward(lengths, tindex, q, k, v, ctx, lse, dctx, seqs, after):
     rows, width = q.shape
     half = rows // seqs
     flat, pair, stat = attend_specs(half, width)
-    return pl.pallas_call(
+    dq, dk, dv, sums = pl.pallas_call(
         functools.partial(attend_backward_kernel, width // HD, half),
         grid_spec=pltpu.PrefetchScalarGridSpec(
             num_scalar_prefetch=2,
             grid=(seqs,),
-            in_specs=[flat, pair, pair, flat, stat, flat],
-            out_specs=[flat, pair, pair],
+            in_specs=[flat, pair, pair, flat, stat, flat] + [pl.BlockSpec(memory_space=pl.ANY)] * len(after),
+            out_specs=[flat, pair, pair, pl.BlockSpec((1, 2, width), lambda s, *_: (s, 0, 0))],
         ),
         out_shape=[
             jax.ShapeDtypeStruct((rows, width), BF),
             jax.ShapeDtypeStruct((2, rows, width), BF),
             jax.ShapeDtypeStruct((2, rows, width), BF),
+            jax.ShapeDtypeStruct((seqs, 2, width), F32),
         ],
         compiler_params=pltpu.CompilerParams(vmem_limit_bytes=24 * 1024 * 1024),
-        cost_estimate=pl.CostEstimate(flops=16_000_000_000, bytes_accessed=10_000_000, transcendentals=3_500_000),
+        cost_estimate=pl.CostEstimate(flops=18_000_000_000, bytes_accessed=10_000_000, transcendentals=3_500_000),
         name="attend_backward",
-    )(lengths, tindex, q, k, v, ctx, lse, dctx)
+    )(lengths, tindex, q, k, v, ctx, lse, dctx, *after)
+    return dq, dk, dv, jnp.sum(sums, 0)
+
+
+def back_kernel(count, has_base, *refs):
+    out_ref = refs[-1]
+    total = refs[2 * count][...] if has_base else None
+    for i in range(count):
+        g = refs[i][...].reshape(out_ref.shape[0], -1)
+        part = dot(g, refs[count + i][0], 1, 1)
+        total = part if total is None else total + part
+    out_ref[...] = total.astype(out_ref.dtype)
+
+
+def back_product(terms, base, dtype, seqs, after):
+    block = (base if base is not None else terms[0][0]).shape[-2] // seqs
+    specs, weight_specs = [], []
+    for grad, side, weight, t in terms:
+        if side is None:
+            specs.append(pl.BlockSpec((block, grad.shape[1]), lambda i: (i, 0)))
+        else:
+            specs.append(pl.BlockSpec((1, block, grad.shape[2]), lambda i, side=side: (side, i, 0)))
+        weight_specs.append(pl.BlockSpec((1,) + weight.shape[1:], lambda i, t=t: (t, 0, 0)))
+    out_spec = pl.BlockSpec((block, D), lambda i: (i, 0))
+    args = [x[0] for x in terms] + [x[2] for x in terms] + ([base] if base is not None else [])
+    return pl.pallas_call(
+        functools.partial(back_kernel, len(terms), base is not None),
+        grid=(seqs,),
+        in_specs=specs
+        + weight_specs
+        + ([out_spec] if base is not None else [])
+        + [pl.BlockSpec(memory_space=pl.ANY)] * len(after),
+        out_specs=out_spec,
+        out_shape=jax.ShapeDtypeStruct((block * seqs, D), dtype),
+        compiler_params=pltpu.CompilerParams(vmem_limit_bytes=32 * 1024 * 1024),
+        cost_estimate=pl.CostEstimate(
+            flops=sum(2 * block * seqs * w.shape[1] * w.shape[2] for _, _, w, _ in terms),
+            bytes_accessed=8_000_000,
+            transcendentals=0,
+        ),
+        name="back_product",
+    )(*args, *after)
+
+
+def weight_kernel(core, own_ref, oth_ref, first_ref, dq_ref, dk_ref, dv_ref, ctx_ref, *rest):
+    keep_ref, send_ref = rest[-2:]
+    _, blocks, rows, columns = keep_ref.shape
+    own = jnp.transpose(own_ref[...])
+    oth = jnp.transpose(oth_ref[...])
+    first = core[0] == 0
+
+    def put(w, full):
+        full = full.astype(BF).reshape(blocks, 2, rows, columns)
+        keep_ref[w] = jnp.where(first, full[:, 0], full[:, 1])
+        send_ref[w] = jnp.where(first, full[:, 1], full[:, 0])
+
+    put(0, dot(own, dq_ref[...], 1, 0))
+    put(1, dot(own, dk_ref[0], 1, 0) + dot(oth, dk_ref[1], 1, 0))
+    put(2, dot(own, dv_ref[0], 1, 0) + dot(oth, dv_ref[1], 1, 0))
+    put(3, dot(jnp.transpose(first_ref[...]), ctx_ref[...], 1, 0))
+
+
+def weight_products(links, own, oth, first_low, dq, dk, dv, ctx, after):
+    rows = D // links.dp_size
+    columns = dq.shape[-1]
+    if rows % 16:
+        both = jnp.concatenate([own, oth], 0)
+        parts = [
+            dot(own, dq, 0, 0),
+            dot(both, dk.reshape(-1, columns), 0, 0),
+            dot(both, dv.reshape(-1, columns), 0, 0),
+            dot(first_low, ctx, 0, 0),
+        ]
+        return halve_cores(links, [[p.astype(BF) for p in parts]])[0], parts[0]
+    shape = (4, links.dp_size // 2, rows, columns)
+    full = pl.BlockSpec(memory_space=pltpu.VMEM)
+    keep, send = pl.pallas_call(
+        weight_kernel,
+        in_specs=[pl.BlockSpec(memory_space=pltpu.SMEM)]
+        + [full] * 7
+        + [pl.BlockSpec(memory_space=pl.ANY)] * len(after),
+        out_specs=[full, full],
+        out_shape=[jax.ShapeDtypeStruct(shape, BF)] * 2,
+        compiler_params=pltpu.CompilerParams(vmem_limit_bytes=40 * 1024 * 1024),
+        cost_estimate=pl.CostEstimate(
+            flops=2 * D * columns * own.shape[0] * 6, bytes_accessed=10_000_000, transcendentals=0
+        ),
+        name="weight_products",
+    )(links.core.reshape(1).astype(jnp.int32), own, oth, first_low, dq, dk, dv, ctx, *after)
+    total = add_low(keep, links.swap(send, "core"))
+    return total.reshape(4, links.hi_size, 2, rows, columns), keep
+
+
+def project_kernel(
+    own_ref, oth_ref, qw_ref, kw_ref, vw_ref, qb_ref, vb_ref, q0, q1, k0, k1, v0, v1
+):
+    own, oth = own_ref[...], oth_ref[...]
+    for t, (q, k, v) in enumerate(((q0, k0, v0), (q1, k1, v1))):
+        q[...] = ((dot(own, qw_ref[t], 1, 0) + qb_ref[t]).astype(BF) * jnp.array(HD**-0.5, BF)).astype(BF)
+        for i, x in enumerate((own, oth)):
+            k[i] = dot(x, kw_ref[t], 1, 0).astype(BF)
+            v[i] = (dot(x, vw_ref[t], 1, 0) + vb_ref[t]).astype(BF)
+
+
+def project(own, oth, query_w, key_w, value_w, query_bias, value_bias, seqs):
+    rows, width = own.shape[0], query_w.shape[2]
+    half = rows // seqs
+    full = pl.BlockSpec(memory_space=pltpu.VMEM)
+    flat = pl.BlockSpec((half, width), lambda i: (i, 0))
+    pair = pl.BlockSpec((2, half, width), lambda i: (0, i, 0))
+    q0, q1, k0, k1, v0, v1 = pl.pallas_call(
+        project_kernel,
+        grid=(seqs,),
+        in_specs=[pl.BlockSpec((half, D), lambda i: (i, 0))] * 2 + [full] * 5,
+        out_specs=[flat, flat, pair, pair, pair, pair],
+        out_shape=[jax.ShapeDtypeStruct((rows, width), BF)] * 2 + [jax.ShapeDtypeStruct((2, rows, width), BF)] * 4,
+        compiler_params=pltpu.CompilerParams(vmem_limit_bytes=32 * 1024 * 1024),
+        cost_estimate=pl.CostEstimate(flops=2 * 10 * rows * D * width, bytes_accessed=16_000_000, transcendentals=0),
+        name="project",
+    )(
+        own,
+        oth,
+        query_w,
+        key_w,
+        value_w,
+        query_bias.reshape(2, 1, width),
+        value_bias.reshape(2, 1, width),
+    )
+    return [q0, q1], [k0, k1], [v0, v1]
+
+
+def pack_kernel(count, *refs):
+    for i in range(count):
+        refs[-1][i] = refs[i][...]
+
+
+def pack(arrays, after):
+    full = pl.BlockSpec(memory_space=pltpu.VMEM)
+    return pl.pallas_call(
+        functools.partial(pack_kernel, len(arrays)),
+        in_specs=[full] * len(arrays) + [pl.BlockSpec(memory_space=pl.ANY)] * len(after),
+        out_specs=full,
+        out_shape=jax.ShapeDtypeStruct((len(arrays),) + arrays[0].shape, arrays[0].dtype),
+        name="pack_shards",
+    )(*arrays, *after)
 
 
 class Links:
@@ -193,11 +338,11 @@
     lax.fori_loop(0, hi_size, step, 0)
 
 
-def gather_tree(links, shards_in, order):
-    stage = jnp.stack(shards_in)[None]
-    stage = jnp.concatenate([stage] + [links.over_hi(stage, d) for d in range(1, links.hi_size)], 0)
-    for axis in order:
-        stage = jnp.stack([stage, links.swap(stage, axis)])
+def gather_tree(links, shards_in, order, after):
+    stage = pack(shards_in, after[0])
+    stage = pack([stage] + [links.over_hi(stage, d) for d in range(1, links.hi_size)], after[1])
+    stage = jnp.stack([stage, links.swap(stage, order[0])])
+    stage = jnp.stack([stage, links.swap(stage, order[1])])
     other = links.swap(stage, "core")
     rows, columns = shards_in[0].shape
     where = jnp.stack([links.at["lo"], links.at["tensor"], links.hi, links.core]).astype(jnp.int32)
@@ -223,19 +368,21 @@
     return (a.astype(F32) + b.astype(F32)).astype(BF)
 
 
-def scatter_tree(links, parts, order):
+def halve_cores(links, parts):
     blocks = [[g.reshape(links.hi_size, 2, 2, -1, g.shape[1]) for g in half] for half in parts]
 
     def side(core):
         return jnp.stack([jnp.stack([pick(g, core, 2) for g in half]) for half in blocks])
 
-    total = add_low(side(links.core), links.swap(side(1 - links.core), "core"))
-    axes = ["tensor", "w", "hi", "lo"]
-    for axis in order:
-        at = axes.index(axis)
-        here = links.at[axis]
-        total = add_low(pick(total, here, at), links.swap(pick(total, 1 - here, at), axis))
-        axes.pop(at)
+    return add_low(side(links.core), links.swap(side(1 - links.core), "core"))
+
+
+def halve(links, total, axis, at):
+    here = links.at[axis]
+    return add_low(pick(total, here, at), links.swap(pick(total, 1 - here, at), axis))
+
+
+def finish(links, total):
     out = pick(total, links.hi, 1).astype(F32)
     for d in range(1, links.hi_size):
         out = out + links.over_hi(pick(total, links.hi ^ d, 1), d).astype(F32)
@@ -243,13 +390,12 @@
 
 
 def sum_everywhere(links, vec):
-    first = vec + links.swap(vec, "tensor")
-    vec = first
+    vec = vec + links.swap(vec, "tensor")
     bit = 1
     while bit < links.dp_size:
         vec = vec + links.over_dp(vec, bit)
         bit *= 2
-    return vec, first
+    return vec
 
 
 def split_vec(vec, sizes):
@@ -295,16 +441,12 @@
     down_w = [ffn_w[t, :, hidden_width:] for t in range(2)]
     inputs_seq = inputs.transpose(1, 0, 2).reshape(rows, D)
     rows_low = inputs_seq.astype(BF)
-    query_w, key_w = gather_tree(links, [query_weight, key_weight], ("tensor", "lo"))
-    value_w, out_w = gather_tree(links, [value_weight, out_weight.T], ("lo", "tensor"))
-    rows_both = jnp.stack([rows_low, links.swap(rows_low, "tensor")])
-    rows_flat = rows_both.reshape(2 * rows, D)
-    queries, keys, values, context, log_sums = [], [], [], [], []
+    rows_other = links.swap(rows_low, "tensor")
+    query_w, key_w = gather_tree(links, [query_weight, key_weight], ("tensor", "lo"), [[rows_low], [rows_other]])
+    value_w, out_w = gather_tree(links, [value_weight, out_weight.T], ("lo", "tensor"), [[rows_low], []])
+    queries, keys, values = project(rows_low, rows_other, query_w, key_w, value_w, query_bias, value_bias, seqs)
+    context, log_sums = [], []
     for t in range(2):
-        part = slice(t * width, (t + 1) * width)
-        queries.append((dot(rows_low, query_w[t], 1, 0) + query_bias[part]).astype(BF) * jnp.array(HD**-0.5, BF))
-        keys.append(dot(rows_flat, key_w[t], 1, 0).astype(BF).reshape(2, rows, width))
-        values.append((dot(rows_flat, value_w[t], 1, 0) + value_bias[part]).astype(BF).reshape(2, rows, width))
         ctx, lse = attend_forward(lengths, tindex, queries[t], keys[t], values[t], seqs)
         context.append(ctx)
         log_sums.append(lse)
@@ -316,7 +458,7 @@
         pre = dot(hidden_low, up_w[t], 1, 0) + input_projection_bias[t * hidden_width : (t + 1) * hidden_width]
         act, slope = gelu_both(pre)
         acts.append(act.astype(BF))
-        slopes.append(slope.astype(BF))
+        slopes.append(lax.optimization_barrier(slope.astype(BF)))
     branch = dot(acts[0], down_w[0], 1, 1) + dot(acts[1], down_w[1], 1, 1)
     outputs, normed_two, inv_two = layer_norm(
         hidden + branch + output_projection_bias, second_gain, second_shift
@@ -327,26 +469,51 @@
     second_shift_part = jnp.sum(cotangent, axis=0)
     down_bias_part = jnp.sum(second_grad, axis=0)
     second_low = second_grad.astype(BF)
-    (down_sum,) = scatter_tree(
-        links, [[dot(second_low, acts[t], 0, 0).astype(BF)] for t in range(2)], ("tensor", "lo")
-    )
+    down_chip = halve_cores(links, [[dot(second_low, acts[t], 0, 0).astype(BF)] for t in range(2)])
     pre_grads, up_bias_parts = [], []
     for t in range(2):
         pre_grad = (dot(second_low, down_w[t], 1, 0) * slopes[t].astype(F32)).astype(BF)
         pre_grads.append(pre_grad)
         up_bias_parts.append(jnp.sum(pre_grad, axis=0, dtype=F32))
-    (up_sum,) = scatter_tree(
-        links, [[dot(hidden_low, pre_grads[t], 0, 0).astype(BF)] for t in range(2)], ("lo", "tensor")
-    )
+    up_chip = halve_cores(links, [[dot(hidden_low, pre_grads[t], 0, 0).astype(BF)] for t in range(2)])
     hidden_grad = second_grad + (dot(pre_grads[0], up_w[0], 1, 1) + dot(pre_grads[1], up_w[1], 1, 1))
     first_grad = norm_back(hidden_grad, normed_one, inv_one, first_gain)
     first_gain_part = jnp.sum(hidden_grad * normed_one, axis=0)
     first_shift_part = jnp.sum(hidden_grad, axis=0)
     out_bias_part = jnp.sum(first_grad, axis=0)
     first_low = first_grad.astype(BF)
-    early, _ = sum_everywhere(
-        links,
-        jnp.concatenate(
+    down_half = halve(links, down_chip, "tensor", 0)
+    up_half = halve(links, up_chip, "lo", 3)
+    query_grads, key_grads, value_grads, bias_parts, chip = [], [], [], [], []
+    down_quarter = halve(links, down_half, "lo", 2)
+    up_quarter = halve(links, up_half, "tensor", 0)
+    after = [down_chip, up_chip]
+    for t in range(2):
+        context_grad = dot(first_low, out_w[t], 1, 0).astype(BF)
+        dq, dk, dv, sums = attend_backward(
+            lengths, tindex, queries[t], keys[t], values[t], context[t], log_sums[t], context_grad, seqs, after
+        )
+        query_grads.append(dq)
+        key_grads.append(dk)
+        value_grads.append(dv)
+        bias_parts.append(sums)
+        if t == 1:
+            other_total = back_product(
+                [(key_grads[i], 1, key_w, i) for i in range(2)] + [(value_grads[i], 1, value_w, i) for i in range(2)],
+                None,
+                BF,
+                seqs,
+                [chip[0]],
+            )
+            after = [other_total, down_quarter, up_quarter]
+        total, made = weight_products(
+            links, rows_low, rows_other, first_low, dq, dk, dv, context[t], after if t else []
+        )
+        chip.append(total)
+        after = [down_half, up_half, made]
+    from_other = links.swap(other_total, "tensor")
+    chip_half = [halve(links, c, "lo", 2) for c in chip]
+    vectors = jnp.concatenate(
             [
                 out_bias_part,
                 first_gain_part,
@@ -355,53 +522,42 @@
                 second_gain_part,
                 second_shift_part,
                 *up_bias_parts,
+                bias_parts[0][0],
+                bias_parts[1][0],
+                bias_parts[0][1],
+                bias_parts[1][1],
             ]
-        ),
-    )
-    out_bias_sum, first_gain_sum, first_shift_sum, down_bias_sum, second_gain_sum, second_shift_sum, up_bias_sum = (
-        split_vec(early, [D] * 6 + [FF])
-    )
-    query_grads, key_grads, value_grads = [], [], []
-    for t in range(2):
-        context_grad = dot(first_low, out_w[t], 1, 0).astype(BF)
-        dq, dk, dv = attend_backward(
-            lengths, tindex, queries[t], keys[t], values[t], context[t], log_sums[t], context_grad, seqs
-        )
-        query_grads.append(dq)
-        key_grads.append(dk)
-        value_grads.append(dv)
-    late, late_first = sum_everywhere(
-        links,
-        jnp.concatenate(
-            [jnp.sum(g, axis=0, dtype=F32) for g in query_grads]
-            + [jnp.sum(g, axis=(0, 1), dtype=F32) for g in value_grads]
-        ),
-    )
-    query_bias_sum, value_bias_sum = split_vec(late, [D, D])
-
-    def back(side):
-        return sum(dot(key_grads[t][side], key_w[t], 1, 1) + dot(value_grads[t][side], value_w[t], 1, 1) for t in range(2))
-
-    other_total, _ = lax.optimization_barrier((back(1).astype(BF), late_first))
-    from_other = links.swap(other_total, "tensor")
-    own_total = back(0) + (dot(query_grads[0], query_w[0], 1, 1) + dot(query_grads[1], query_w[1], 1, 1))
-    input_grad = first_grad + (own_total + from_other.astype(F32))
-    query_key_parts, value_out_parts = [], []
-    for t in range(2):
-        query_key_parts.append(
-            [
-                dot(rows_low, query_grads[t], 0, 0).astype(BF),
-                dot(rows_flat, key_grads[t].reshape(2 * rows, width), 0, 0).astype(BF),
-            ]
-        )
-        value_out_parts.append(
-            [
-                dot(rows_flat, value_grads[t].reshape(2 * rows, width), 0, 0).astype(BF),
-                dot(first_low, context[t], 0, 0).astype(BF),
-            ]
-        )
-    query_sum, key_sum = scatter_tree(links, query_key_parts, ("lo", "tensor"))
-    value_sum, out_sum = scatter_tree(links, value_out_parts, ("lo", "tensor"))
+        ).reshape(-1, 128)
+    sums = sum_everywhere(links, pack([vectors], [chip[1], chip_half[0]])[0]).reshape(-1)
+    (
+        out_bias_sum,
+        first_gain_sum,
+        first_shift_sum,
+        down_bias_sum,
+        second_gain_sum,
+        second_shift_sum,
+        up_bias_sum,
+        query_bias_sum,
+        value_bias_sum,
+    ) = split_vec(sums, [D] * 6 + [FF, D, D])
+    own_total = back_product(
+        [(query_grads[t], None, query_w, t) for t in range(2)]
+        + [(key_grads[t], 0, key_w, t) for t in range(2)]
+        + [(value_grads[t], 0, value_w, t) for t in range(2)],
+        first_grad,
+        F32,
+        seqs,
+        [],
+    )
+    input_grad = own_total + from_other.astype(F32)
+    (down_sum,) = finish(links, down_quarter)
+    (up_sum,) = finish(links, up_quarter)
+    first_side = links.at["tensor"] == 0
+    mine = jnp.where(first_side, chip_half[0], chip_half[1])
+    theirs = jnp.where(first_side, chip_half[1], chip_half[0])
+    query_sum, key_sum, value_sum, out_sum = finish(
+        links, add_low(mine, links.swap(pack([theirs], [from_other])[0], "tensor"))
+    )
 
     def positions_first(v):
         return v.reshape(seqs, half, D).transpose(1, 0, 2)

time: 509 us -> 401 us (0.79)
  matrix products: 126 us -> 60 us
  Pallas kernels: 59.1 us -> 90.1 us
  waiting for transfers between devices: 118 us -> 87.6 us
  other arithmetic: 56.1 us -> 34.9 us
  local copies, waits for them, and re-layouts: 64.4 us -> 51.6 us
  starting transfers between devices: 62.5 us -> 54.6 us
    dot_general x40 -> x16, matrix products: 126 us -> 60 us  [dot(): lax.dot_general(a, b, (((da,), (db,)), ((), ())), preferred_element_type=...]
    pallas_call x0 -> x11, Pallas kernels: none -> 40.4 us  [the longest x2 11.2 us: weight_products(): pl.pallas_call(weight_kernel, in_specs=[pl.BlockSpec(memory_space=pltpu.S...]
    ppermute x10 -> x8, waiting for transfers between devices: 65.8 us -> 47.4 us  [swap(): return lax.ppermute(v, 'tensor', [(0, 1), (1, 0)])]
    dynamic_slice x24 -> x2, local copies, waits for them, and re-layouts: 16 us -> 0.85 us  [pick(): return lax.dynamic_index_in_dim(v, index, axis, keepdims=False)]
    ppermute x38 -> x31, waiting for transfers between devices: 52.6 us -> 40.1 us  [over_dp(): return lax.ppermute(v, 'dp', [(i, i ^ mask) for i in range(self.dp_size)])]
    pallas_call x2, Pallas kernels: 35.8 us -> 25.9 us  [attend_backward(): pl.pallas_call(functools.partial(attend_backward_kernel, width // HD, hal...]
    ppermute x38 -> x31, starting transfers between devices: 53.5 us -> 43.9 us  [over_dp(): return lax.ppermute(v, 'dp', [(i, i ^ mask) for i in range(self.dp_size)])]
    unnamed x179 -> x219, local copies, waits for them, and re-layouts: 18.3 us -> 27.5 us
  transfers between devices with their start and end apart: 49 -> 40, of which waited for: 22 -> 17; matrix products, arithmetic and copies ran while one was open for 21% -> 18% of each run, Pallas kernels for 5% -> 21%
where the time goes in v3:
time: 401 us; the launch traced here: 395 us
  Pallas kernels  90.1 us (22%)
  waiting for transfers between devices  87.6 us (22%)
  matrix products  60 us (15%)
  starting transfers between devices  54.6 us (14%)
  local copies, waits for them, and re-layouts  51.6 us (13%)
  other arithmetic  34.9 us (9%)
  between operations  16.2 us (4%)
    dot_general x16, matrix products, dot(): lax.dot_general(a, b, (((da,), (db,)), ((), ())), preferred_element_type=...  60 us
    ppermute x8, waiting for transfers between devices, swap(): return lax.ppermute(v, 'tensor', [(0, 1), (1, 0)])  47.4 us
    ppermute x31, starting transfers between devices, over_dp(): return lax.ppermute(v, 'dp', [(i, i ^ mask) for i in range(self.dp_size)])  43.9 us
    ppermute x31, waiting for transfers between devices, over_dp(): return lax.ppermute(v, 'dp', [(i, i ^ mask) for i in range(self.dp_size)])  40.1 us
    unnamed x219, local copies, waits for them, and re-layouts  27.5 us
    pallas_call x2, Pallas kernels, attend_backward(): pl.pallas_call(functools.partial(attend_backward_kernel, width // HD, hal...  25.9 us
    pallas_call x2, Pallas kernels, attend_forward(): pl.pallas_call(functools.partial(attend_forward_kernel, width // HD, half...  20.6 us
    pallas_call x2, Pallas kernels, weight_products(): pl.pallas_call(weight_kernel, in_specs=[pl.BlockSpec(memory_space=pltpu.S...  11.2 us
  transfers between devices with their start and end apart: 40, of which 17 were waited for; matrix products, arithmetic and copies ran while one was open for 18% of the time, Pallas kernels for 21%

profile of v3, /device:TPU:0, one launch (start us, length us, event | category | flops | bytes accessed | tf_op | source)
XLA Modules:
  0.0 395.0 jit_solution(8448581715935582741)
XLA Ops:
  22.3 7.5 %collective-permute-done.8.refs_2_ = bf16[2,48,384]{2,1,0:T(8,128)(2,1)S(1)} collective-permute-done((bf16[2,48,384]{2,1,0:T(8,128)(2,1)}, bf16[2,48,384]{2,1,0:T(8,128)(2,1)S(1)}, u32[]{:S(2)}, u32[]{:S(2)}) %collective-permute-start.8) | collective-permute-done | bytes 73760 | tf_op jit(solution)/shard_map/ppermute | solution.py:314
  47.2 9.9 %collective-permute-done.refs_4_.oth_ref = bf16[1024,768]{1,0:T(8,128)(2,1)S(1)} collective-permute-done((bf16[1024,768]{1,0:T(8,128)(2,1)S(1)}, bf16[1024,768]{1,0:T(8,128)(2,1)S(1)}, u32[]{:S(2)}, u32[]{:S(2)}) %collective-permute-start) | collective-permute-done | bytes 1572896 | tf_op jit(solution)/shard_map/ppermute | solution.py:318
  63.2 9.5 %collective-permute-done.4 = bf16[4,2,48,384]{3,2,1,0:T(8,128)(2,1)S(1)} collective-permute-done((bf16[4,2,48,384]{3,2,1,0:T(8,128)(2,1)}, bf16[4,2,48,384]{3,2,1,0:T(8,128)(2,1)S(1)}, u32[]{:S(2)}, u32[]{:S(2)}) %collective-permute-start.4) | collective-permute-done | bytes 294944 | tf_op jit(solution)/shard_map/ppermute | solution.py:318
  75.1 20.8 %collective-permute-done.11 = bf16[2,4,2,48,384]{4,3,2,1,0:T(8,128)(2,1)S(1)} collective-permute-done((bf16[2,4,2,48,384]{4,3,2,1,0:T(8,128)(2,1)S(1)}, bf16[2,4,2,48,384]{4,3,2,1,0:T(8,128)(2,1)S(1)}, u32[]{:S(2)}, u32[]{:S(2)}) %collective-permute-start.11) | collective-permute-done | bytes 589856 | tf_op jit(solution)/shard_map/ppermute | solution.py:318
  98.1 4.6 %copy.106 = f32[4,256,768]{2,1,0:T(8,128)} copy(f32[4,256,768]{2,0,1:T(4,128)} %bitcast.256) | data formatting | bytes 6291456 | tf_op jit(solution)/shard_map/transpose | solution.py:466
  114.4 9.5 %project.1 = (bf16[1024,384]{1,0:T(8,128)(2,1)S(1)}, bf16[1024,384]{1,0:T(8,128)(2,1)S(1)}, bf16[2,1024,384]{2,1,0:T(8,128)(2,1)S(1)}, bf16[2,1024,384]{2,1,0:T(...) custom-call(bf16[1024,768]{1,0:T(8,128)(2,1)S(1)} %copy-done.7, ...), custom_call_target="tpu_custom_call" | custom-call | flops 6039797760 | bytes 16000000 | tf_op jit(solution)/shard_map/project/pallas_call | solution.py:267
  124.0 10.3 %attend_forward.3 = (bf16[1024,384]{1,0:T(8,128)(2,1)S(1)}, f32[4,256,128]{2,1,0:T(8,128)S(1)}) custom-call(s32[4]{0:T(128)S(1)} %copy-done.39, s32[1]{0:T(128)} %bitcast.2.tindex, bf16[1024,384]{1,0:T(8,128)(2,1)S(1)} %get-tuple-element.51.q_ref, bf16[2,1024,384]{2,1,0:T(8,128)(2,1)S(1)} %get-tuple-element.52.k_ref, ...), custom_call_target="tpu_custom_call" | custom-call | flops 8000000000 | bytes 5000000 | tf_op jit(solution)/shard_map/attend_forward/pallas_call | solution.py:121
  135.4 10.3 %attend_forward.2 = (bf16[1024,384]{1,0:T(8,128)(2,1)S(1)}, f32[4,256,128]{2,1,0:T(8,128)S(1)}) custom-call(s32[4]{0:T(128)S(1)} %copy-done.39, s32[1]{0:T(128)} %bitcast.2.tindex, bf16[1024,384]{1,0:T(8,128)(2,1)S(1)} %get-tuple-element.46.q_ref, bf16[2,1024,384]{2,1,0:T(8,128)(2,1)S(1)} %get-tuple-element.47.k_ref, ...), custom_call_target="tpu_custom_call" | custom-call | flops 8000000000 | bytes 5000000 | tf_op jit(solution)/shard_map/attend_forward/pallas_call | solution.py:121
  149.4 10.3 %fusion.5 = (bf16[1024,1536]{1,0:T(8,128)(2,1)}, bf16[1024,1536]{1,0:T(8,128)(2,1)S(1)}) fusion(f32[1536]{0:T(1024)S(1)} %copy-done.86, bf16[1024,768]{1,0:T(8,128)(2,1)} %fusion.14, bf16[2,768,3072]{2,1,0:T(8,128)(2,1)} %bitcast.294), kind=kOutput, calls=%fused_computation.9 | convolution fusion | flops 2456813568 | bytes 10229760 | tf_op jit(solution)/shard_map/dot_general | solution.py:21
  162.4 8.7 %fusion.11 = (bf16[1024,1536]{1,0:T(8,128)(2,1)}, bf16[1024,1536]{1,0:T(8,128)(2,1)S(1)}) fusion(f32[1536]{0:T(1024)S(1)} %copy-done.85, bf16[1024,768]{1,0:T(8,128)(2,1)S(1)} %copy-done.72, bf16[2,768,3072]{2,1,0:T(8,128)(2,1)S(1)} %bitcast.298), kind=kOutput, calls=%fused_computation.15 | convolution fusion | flops 2456813568 | bytes 10231808 | tf_op jit(solution)/shard_map/dot_general | solution.py:21
  188.0 4.3 %convert_reduce_fusion.1 = (f32[1536]{0:T(1024)S(1)}, bf16[1024,1536]{1,0:T(8,128)(2,1)S(1)}) fusion(bf16[1024,1536]{1,0:T(8,128)(2,1)} %get-tuple-element.87, bf16[1024,768]{1,0:T(8,128)(2,1)S(1)} %convert_element_type.293, bf16[2,768,3072]{2,1,0:T(8,128)(2,1)S(1)} %bitcast.300), kind=kOutput, calls=%fused_computation.17 | convolution fusion | flops 2423781888 | bytes 10229760 | tf_op jit(solution)/shard_map/dot_general | solution.py:21
  195.3 4.3 %fusion.17 = f32[1024,768]{1,0:T(8,128)} fusion(bf16[1024,1536]{1,0:T(8,128)(2,1)S(1)} %get-tuple-element.133, bf16[2,768,3072]{2,1,0:T(8,128)(2,1)S(1)} %bitcast.301), kind=kOutput, calls=%fused_computation.65 | convolution fusion | flops 2415919104 | bytes 8650752 | tf_op jit(solution)/shard_map/dot_general | solution.py:21
  200.9 5.0 %convert_reduce_fusion = (f32[1536]{0:T(1024)S(1)}, bf16[1024,1536]{1,0:T(8,128)(2,1)S(1)}) fusion(bf16[1024,1536]{1,0:T(8,128)(2,1)} %get-tuple-element.85, bf16[1024,768]{1,0:T(8,128)(2,1)S(1)} %convert_element_type.293, bf16[2,768,3072]{2,1,0:T(8,128)(2,1)} %bitcast.295), kind=kOutput, calls=%fused_computation.16 | convolution fusion | flops 2423781888 | bytes 10229760 | tf_op jit(solution)/shard_map/dot_general | solution.py:21
  212.2 5.4 %multiply_reduce_fusion = (f32[768]{0:T(1024)S(1)}, f32[1024]{0:T(1024)S(1)}, f32[1024]{0:T(1024)S(1)}, f32[768]{0:T(1024)S(1)}, f32[1024,768]{1,0:T(8,128)S(1)}) fusion(f32[1024,768]{1,0:T(8,128)S(1)} %get-tuple-element.128, f32[1024]{0:T(1024)S(1)} %add_rsqrt_fusion.1, f32[1024]{0:T(1024)S(1)} %broadcast_multiply_fusion.5, f32[768]{0:T(1024)S(1)} %copy-done.83, ...), kind=kOutput, calls=%fused_computation.36 | convolution fusion | flops 2424566272 | bytes 18113536 | tf_op jit(solution)/shard_map/dot_general | solution.py:21
  230.9 13.0 %attend_backward.2 = (bf16[1024,384]{1,0:T(8,128)(2,1)S(1)}, bf16[2,1024,384]{2,1,0:T(8,128)(2,1)S(1)}, bf16[2,1024,384]{2,1,0:T(8,128)(2,1)S(1)}, f32[4,2,384]{2,1,0:T(2,128)S(1)}) custom-call(s32[4]{0:T(128)S(1)} %copy-done.39, s32[1]{0:T(128)} %bitcast.2.tindex, bf16[1024,384]{1,0:T(8,128)(2,1)S(1)} %copy-done.51, bf16[2,1024,384]{2,1,0:T(8,128)(2,1)S(1)} %copy-done.45, ...), custom_call_target="tpu_custom_call" | custom-call | flops 17999998976 | bytes 10000000 | tf_op jit(solution)/shard_map/attend_backward/pallas_call | solution.py:140
  244.0 5.1 %weight_products.2 = (bf16[4,8,48,384]{3,2,1,0:T(8,128)(2,1)S(1)}, bf16[4,8,48,384]{3,2,1,0:T(8,128)(2,1)S(1)}) custom-call(s32[1]{0:T(128)} %bitcast.5.core, bf16[1024,768]{1,0:T(8,128)(2,1)S(1)} %copy-done.8, bf16[1024,768]{1,0:T(8,128)(2,1)S(1)} %copy-done.28, bf16[1024,768]{1,0:T(8,128)(2,1)S(1)} %convert_element_type.300.first_ref, ...), custom_call_target="tpu_custom_call" | custom-call | flops 3623878656 | bytes 10000000 | tf_op jit(solution)/shard_map/weight_products/pallas_call | solution.py:233
  249.2 5.0 %collective-permute-done.15 = bf16[1,4,2,48,1536]{4,3,1,2,0:T(8,128)(2,1)} collective-permute-done((bf16[1,4,2,48,1536]{4,3,1,2,0:T(8,128)(2,1)}, bf16[1,4,2,48,1536]{4,3,1,2,0:T(8,128)(2,1)}, u32[]{:S(2)}, u32[]{:S(2)}) %collective-permute-start.15) | collective-permute-done | bytes 1179680 | tf_op jit(solution)/shard_map/ppermute | solution.py:318
  260.4 12.8 %attend_backward.3 = (bf16[1024,384]{1,0:T(8,128)(2,1)S(1)}, bf16[2,1024,384]{2,1,0:T(8,128)(2,1)S(1)}, bf16[2,1024,384]{2,1,0:T(8,128)(2,1)S(1)}, f32[4,2,384]{2,1,0:T(2,128)S(1)}) custom-call(s32[4]{0:T(128)S(1)} %copy-done.39, s32[1]{0:T(128)} %bitcast.2.tindex, bf16[1024,384]{1,0:T(8,128)(2,1)S(1)} %copy-done.49, bf16[2,1024,384]{2,1,0:T(8,128)(2,1)S(1)} %copy-done.41, ...), custom_call_target="tpu_custom_call" | custom-call | flops 17999998976 | bytes 10000000 | tf_op jit(solution)/shard_map/attend_backward/pallas_call | solution.py:140
  282.8 6.2 %weight_products.3 = (bf16[4,8,48,384]{3,2,1,0:T(8,128)(2,1)S(1)}, bf16[4,8,48,384]{3,2,1,0:T(8,128)(2,1)}) custom-call(s32[1]{0:T(128)} %bitcast.5.core, bf16[1024,768]{1,0:T(8,128)(2,1)S(1)} %copy-done.8, bf16[1024,768]{1,0:T(8,128)(2,1)S(1)} %copy-done.28, bf16[1024,768]{1,0:T(8,128)(2,1)S(1)} %convert_element_type.300.first_ref, ...), custom_call_target="tpu_custom_call" | custom-call | flops 3623878656 | bytes 10000000 | tf_op jit(solution)/shard_map/weight_products/pallas_call | solution.py:233
  305.7 5.9 %back_product.2 = f32[1024,768]{1,0:T(8,128)S(1)} custom-call(bf16[1024,384]{1,0:T(8,128)(2,1)S(1)} %copy-done.36, bf16[1024,384]{1,0:T(8,128)(2,1)S(1)} %copy-done.38, bf16[2,1024,384]{2,1,0:T(8,128)(2,1)S(1)} %copy-done.14, bf16[2,1024,384]{2,1,0:T(8,128)(2,1)S(1)} %copy-done.18, bf16[2,1024,384]{2,1,0:T(8,128)(2,1)S(1)} %copy-done.16, ...), custom_call_target="tpu_custom_call" | custom-call | flops 3623878656 | bytes 8000000 | tf_op jit(solution)/shard_map/back_product/pallas_call | solution.py:182
  313.3 10.0 %collective-permute-done.23 = bf16[4,4,48,384]{3,2,1,0:T(8,128)(2,1)S(1)} collective-permute-done((bf16[4,4,48,384]{3,2,1,0:T(8,128)(2,1)S(1)}, bf16[4,4,48,384]{3,2,1,0:T(8,128)(2,1)S(1)}, u32[]{:S(2)}, u32[]{:S(2)}) %collective-permute-start.23) | collective-permute-done | bytes 589856 | tf_op jit(solution)/shard_map/ppermute | solution.py:314
  338.0 5.0 %collective-permute-done.37 = bf16[1,48,1536]{2,1,0:T(8,128)(2,1)S(1)} collective-permute-done((bf16[1,48,1536]{2,1,0:T(8,128)(2,1)S(1)}, bf16[1,48,1536]{2,1,0:T(8,128)(2,1)S(1)}, u32[]{:S(2)}, u32[]{:S(2)}) %collective-permute-start.37) | collective-permute-done | bytes 147488 | tf_op jit(solution)/shard_map/ppermute | solution.py:314
  349.3 7.1 %collective-permute-start.31 = (f32[72,128]{1,0:T(8,128)S(1)}, f32[72,128]{1,0:T(8,128)S(1)}, u32[]{:S(2)}, u32[]{:S(2)}) collective-permute-start(f32[72,128]{1,0:T(8,128)S(1)} %add.318), channel_id=1, source_target_pairs={{0,8},{2,10},{4,12},{6,14},{8,0},{10,2},{12,4},{14,6},{16,24},{18,... | collective-permute-start | bytes 110600 | tf_op jit(solution)/shard_map/ppermute | solution.py:314
  378.8 8.0 %collective-permute-done.26 = bf16[4,48,384]{2,1,0:T(8,128)(2,1)S(1)} collective-permute-done((bf16[4,48,384]{2,1,0:T(8,128)(2,1)S(1)}, bf16[4,48,384]{2,1,0:T(8,128)(2,1)S(1)}, u32[]{:S(2)}, u32[]{:S(2)}) %collective-permute-start.26) | collective-permute-done | bytes 147488 | tf_op jit(solution)/shard_map/ppermute | solution.py:314
  (385 shorter events, 180.6 us)
Async XLA Ops:
  7.2 142.2 %all-gather.2.cloned.1.call-start = ((), (), s32[]{:S(2)}) async-start(), calls=%async_computation | async-start | bytes 9732096 | tf_op jit(solution)/shard_map/all_gather | solution.py:437
  13.3 43.7 %collective-permute-start = (bf16[1024,768]{1,0:T(8,128)(2,1)S(1)}, bf16[1024,768]{1,0:T(8,128)(2,1)S(1)}, u32[]{:S(2)}, u32[]{:S(2)}) collective-permute-start(bf16[1024,768]{1,0:T(8,128)(2,1)S(1)} %bitcast_convert_fusion.refs_2_.own_ref), channel_id=1, source_target_pairs={{0,1},{1,0},{2,3},{3,2},{4,5},{5,4},{6,7},{7,6},{8,9},{9,8},{10,11... | collective-permute-start | bytes 4718600 | tf_op jit(solution)/shard_map/ppermute | solution.py:318
  32.9 28.9 %collective-permute-start.10 = (bf16[4,2,48,384]{3,2,1,0:T(8,128)(2,1)}, bf16[4,2,48,384]{3,2,1,0:T(8,128)(2,1)}, u32[]{:S(2)}, u32[]{:S(2)}) collective-permute-start(bf16[4,2,48,384]{3,2,1,0:T(8,128)(2,1)} %pack_shards.9), channel_id=1, source_target_pairs={{0,4},{2,6},{4,0},{6,2},{8,12},{10,14},{12,8},{14,10},{16,20},{18,... | collective-permute-start | bytes 884744 | tf_op jit(solution)/shard_map/ppermute | solution.py:314
  60.0 12.6 %collective-permute-start.4 = (bf16[4,2,48,384]{3,2,1,0:T(8,128)(2,1)}, bf16[4,2,48,384]{3,2,1,0:T(8,128)(2,1)S(1)}, u32[]{:S(2)}, u32[]{:S(2)}) collective-permute-start(bf16[4,2,48,384]{3,2,1,0:T(8,128)(2,1)} %pack_shards.7), channel_id=1, source_target_pairs={{0,1},{1,0},{2,3},{3,2},{4,5},{5,4},{6,7},{7,6},{8,9},{9,8},{10,11... | collective-permute-start | bytes 884744 | tf_op jit(solution)/shard_map/ppermute | solution.py:318
  62.8 33.0 %collective-permute-start.11 = (bf16[2,4,2,48,384]{4,3,2,1,0:T(8,128)(2,1)S(1)}, bf16[2,4,2,48,384]{4,3,2,1,0:T(8,128)(2,1)S(1)}, u32[]{:S(2)}, u32[]{:S(2)}) collective-permute-start(bf16[2,4,2,48,384]{4,3,2,1,0:T(8,128)(2,1)S(1)} %get-tuple-element.110), channel_id=1, source_target_pairs={{0,1},{1,0},{2,3},{3,2},{4,5},{5,4},{6,7},{7,6},{8,9},{9,8},{10,11... | collective-permute-start | bytes 1769480 | tf_op jit(solution)/shard_map/ppermute | solution.py:318
  73.7 24.0 %collective-permute-start.5 = (bf16[2,4,2,48,384]{4,3,2,1,0:T(8,128)(2,1)S(1)}, bf16[2,4,2,48,384]{4,3,2,1,0:T(8,128)(2,1)S(1)}, u32[]{:S(2)}, u32[]{:S(2)}) collective-permute-start(bf16[2,4,2,48,384]{4,3,2,1,0:T(8,128)(2,1)S(1)} %get-tuple-element.112), channel_id=1, source_target_pairs={{0,4},{2,6},{4,0},{6,2},{8,12},{10,14},{12,8},{14,10},{16,20},{18,... | collective-permute-start | bytes 1769480 | tf_op jit(solution)/shard_map/ppermute | solution.py:314
  96.0 14.9 %collective-permute-start.12 = (bf16[2,2,4,2,48,384]{5,4,3,2,1,0:T(8,128)(2,1)S(1)}, bf16[2,2,4,2,48,384]{5,4,3,2,1,0:T(8,128)(2,1)S(1)}, u32[]{:S(2)}, u32[]{:S(2)}) collective-permute-start(bf16[2,2,4,2,48,384]{5,4,3,2,1,0:T(8,128)(2,1)S(1)} %pad_maximum_fusion.3.mine_ref), channel_id=1, source_target_pairs={{0,2},{2,0},{4,6},{6,4},{8,10},{10,8},{12,14},{14,12},{16,18},{18,... | collective-permute-start | bytes 3538952 | tf_op jit(solution)/shard_map/ppermute | solution.py:314
  97.9 14.2 %collective-permute-start.6 = (bf16[2,2,4,2,48,384]{5,4,3,2,1,0:T(8,128)(2,1)S(1)}, bf16[2,2,4,2,48,384]{5,4,3,2,1,0:T(8,128)(2,1)}, u32[]{:S(2)}, u32[]{:S(2)}) collective-permute-start(bf16[2,2,4,2,48,384]{5,4,3,2,1,0:T(8,128)(2,1)S(1)} %pad_maximum_fusion.2.mine_ref), channel_id=1, source_target_pairs={{0,2},{2,0},{4,6},{6,4},{8,10},{10,8},{12,14},{14,12},{16,18},{18,... | collective-permute-start | bytes 3538952 | tf_op jit(solution)/shard_map/ppermute | solution.py:314
  200.4 23.4 %collective-permute-start.13 = (bf16[2,1,4,2,48,1536]{5,4,2,3,1,0:T(8,128)(2,1)S(1)}, bf16[2,1,4,2,48,1536]{5,4,2,3,1,0:T(8,128)(2,1)S(1)}, u32[]{:S(2)}, u32[]{:S(2)}) collective-permute-start(bf16[2,1,4,2,48,1536]{5,4,2,3,1,0:T(8,128)(2,1)S(1)} %pad_maximum_fusion), channel_id=1, source_target_pairs={{0,2},{2,0},{4,6},{6,4},{8,10},{10,8},{12,14},{14,12},{16,18},{18,... | collective-permute-start | bytes 7077896 | tf_op jit(solution)/shard_map/ppermute | solution.py:314
  211.2 16.1 %collective-permute-start.14 = (bf16[2,1,4,2,48,1536]{5,4,2,0,3,1:T(8,128)(2,1)}, bf16[2,1,4,2,48,1536]{5,4,2,0,3,1:T(8,128)(2,1)S(1)}, u32[]{:S(2)}, u32[]{:S(2)}) collective-permute-start(bf16[2,1,4,2,48,1536]{5,4,2,0,3,1:T(8,128)(2,1)} %pad_maximum_fusion.1), channel_id=1, source_target_pairs={{0,2},{2,0},{4,6},{6,4},{8,10},{10,8},{12,14},{14,12},{16,18},{18,... | collective-permute-start | bytes 7077896 | tf_op jit(solution)/shard_map/ppermute | solution.py:314
  225.8 28.3 %collective-permute-start.15 = (bf16[1,4,2,48,1536]{4,3,1,2,0:T(8,128)(2,1)}, bf16[1,4,2,48,1536]{4,3,1,2,0:T(8,128)(2,1)}, u32[]{:S(2)}, u32[]{:S(2)}) collective-permute-start(bf16[1,4,2,48,1536]{4,3,1,2,0:T(8,128)(2,1)} %dynamic-slice_bitcast_fusion.1), channel_id=1, source_target_pairs={{0,1},{1,0},{2,3},{3,2},{4,5},{5,4},{6,7},{7,6},{8,9},{9,8},{10,11... | collective-permute-start | bytes 3538952 | tf_op jit(solution)/shard_map/ppermute | solution.py:318
  229.4 28.0 %collective-permute-start.16 = (bf16[2,1,4,48,1536]{4,3,2,1,0:T(8,128)(2,1)}, bf16[2,1,4,48,1536]{4,3,2,1,0:T(8,128)(2,1)}, u32[]{:S(2)}, u32[]{:S(2)}) collective-permute-start(bf16[2,1,4,48,1536]{4,3,2,1,0:T(8,128)(2,1)} %dynamic-slice_bitcast_fusion), channel_id=1, source_target_pairs={{0,4},{2,6},{4,0},{6,2},{8,12},{10,14},{12,8},{14,10},{16,20},{18,... | collective-permute-start | bytes 3538952 | tf_op jit(solution)/shard_map/ppermute | solution.py:314
  249.1 24.3 %collective-permute-start.17 = (bf16[4,8,48,384]{3,2,1,0:T(8,128)(2,1)S(1)}, bf16[4,8,48,384]{3,2,1,0:T(8,128)(2,1)S(1)}, u32[]{:S(2)}, u32[]{:S(2)}) collective-permute-start(bf16[4,8,48,384]{3,2,1,0:T(8,128)(2,1)S(1)} %get-tuple-element.64), channel_id=1, source_target_pairs={{0,2},{2,0},{4,6},{6,4},{8,10},{10,8},{12,14},{14,12},{16,18},{18,... | collective-permute-start | bytes 3538952 | tf_op jit(solution)/shard_map/ppermute | solution.py:314
  255.9 25.0 %collective-permute-start.20 = (bf16[1,4,48,1536]{3,2,1,0:T(8,128)(2,1)S(1)}, bf16[1,4,48,1536]{3,2,1,0:T(8,128)(2,1)}, u32[]{:S(2)}, u32[]{:S(2)}) collective-permute-start(bf16[1,4,48,1536]{3,2,1,0:T(8,128)(2,1)S(1)} %dynamic-slice_bitcast_fusion.4), channel_id=1, source_target_pairs={{0,4},{2,6},{4,0},{6,2},{8,12},{10,14},{12,8},{14,10},{16,20},{18,... | collective-permute-start | bytes 1769480 | tf_op jit(solution)/shard_map/ppermute | solution.py:314
  259.1 23.6 %collective-permute-start.21 = (bf16[1,4,48,1536]{3,2,1,0:T(8,128)(2,1)S(1)}, bf16[1,4,48,1536]{3,2,1,0:T(8,128)(2,1)S(1)}, u32[]{:S(2)}, u32[]{:S(2)}) collective-permute-start(bf16[1,4,48,1536]{3,2,1,0:T(8,128)(2,1)S(1)} %dynamic-slice_bitcast_fusion.3), channel_id=1, source_target_pairs={{0,1},{1,0},{2,3},{3,2},{4,5},{5,4},{6,7},{7,6},{8,9},{9,8},{10,11... | collective-permute-start | bytes 1769480 | tf_op jit(solution)/shard_map/ppermute | solution.py:318
  292.9 65.2 %collective-permute-start.18 = (bf16[1024,768]{1,0:T(8,128)(2,1)}, bf16[1024,768]{1,0:T(8,128)(2,1)}, u32[]{:S(2)}, u32[]{:S(2)}) collective-permute-start(bf16[1024,768]{1,0:T(8,128)(2,1)} %copy-done.29), channel_id=1, source_target_pairs={{0,1},{1,0},{2,3},{3,2},{4,5},{5,4},{6,7},{7,6},{8,9},{9,8},{10,11... | collective-permute-start | bytes 4718600 | tf_op jit(solution)/shard_map/ppermute | solution.py:318
  295.1 18.2 %collective-permute-start.19 = (bf16[4,4,48,384]{3,2,1,0:T(8,128)(2,1)S(1)}, bf16[4,4,48,384]{3,2,1,0:T(8,128)(2,1)S(1)}, u32[]{:S(2)}, u32[]{:S(2)}) collective-permute-start(bf16[4,4,48,384]{3,2,1,0:T(8,128)(2,1)S(1)} %dynamic-slice_bitcast_fusion.5), channel_id=1, source_target_pairs={{0,4},{2,6},{4,0},{6,2},{8,12},{10,14},{12,8},{14,10},{16,20},{18,... | collective-permute-start | bytes 1769480 | tf_op jit(solution)/shard_map/ppermute | solution.py:314
  298.0 25.2 %collective-permute-start.23 = (bf16[4,4,48,384]{3,2,1,0:T(8,128)(2,1)S(1)}, bf16[4,4,48,384]{3,2,1,0:T(8,128)(2,1)S(1)}, u32[]{:S(2)}, u32[]{:S(2)}) collective-permute-start(bf16[4,4,48,384]{3,2,1,0:T(8,128)(2,1)S(1)} %dynamic-slice_bitcast_fusion.2), channel_id=1, source_target_pairs={{0,4},{2,6},{4,0},{6,2},{8,12},{10,14},{12,8},{14,10},{16,20},{18,... | collective-permute-start | bytes 1769480 | tf_op jit(solution)/shard_map/ppermute | solution.py:314
  328.9 14.1 %collective-permute-start.37 = (bf16[1,48,1536]{2,1,0:T(8,128)(2,1)S(1)}, bf16[1,48,1536]{2,1,0:T(8,128)(2,1)S(1)}, u32[]{:S(2)}, u32[]{:S(2)}) collective-permute-start(bf16[1,48,1536]{2,1,0:T(8,128)(2,1)S(1)} %get-tuple-element.102), channel_id=1, source_target_pairs={{0,16},{2,18},{4,20},{6,22},{8,24},{10,26},{12,28},{14,30},{16,0},... | collective-permute-start | bytes 442376 | tf_op jit(solution)/shard_map/ppermute | solution.py:314
  331.5 13.9 %collective-permute-start.38 = (bf16[1,48,1536]{2,1,0:T(8,128)(2,1)S(1)}, bf16[1,48,1536]{2,1,0:T(8,128)(2,1)S(1)}, u32[]{:S(2)}, u32[]{:S(2)}) collective-permute-start(bf16[1,48,1536]{2,1,0:T(8,128)(2,1)S(1)} %get-tuple-element.101), channel_id=1, source_target_pairs={{0,24},{2,26},{4,28},{6,30},{8,16},{10,18},{12,20},{14,22},{16,8},... | collective-permute-start | bytes 442376 | tf_op jit(solution)/shard_map/ppermute | solution.py:314
  333.8 22.7 %collective-permute-start.33 = (bf16[1,48,1536]{2,1,0:T(8,128)(2,1)S(1)}, bf16[1,48,1536]{2,1,0:T(8,128)(2,1)S(1)}, u32[]{:S(2)}, u32[]{:S(2)}) collective-permute-start(bf16[1,48,1536]{2,1,0:T(8,128)(2,1)S(1)} %get-tuple-element.103), channel_id=1, source_target_pairs={{0,8},{2,10},{4,12},{6,14},{8,0},{10,2},{12,4},{14,6},{16,24},{18,... | collective-permute-start | bytes 442376 | tf_op jit(solution)/shard_map/ppermute | solution.py:314
  334.4 22.0 %collective-permute-start.34 = (bf16[1,48,1536]{2,1,0:T(8,128)(2,1)S(1)}, bf16[1,48,1536]{2,1,0:T(8,128)(2,1)S(1)}, u32[]{:S(2)}, u32[]{:S(2)}) collective-permute-start(bf16[1,48,1536]{2,1,0:T(8,128)(2,1)S(1)} %get-tuple-element.105), channel_id=1, source_target_pairs={{0,16},{2,18},{4,20},{6,22},{8,24},{10,26},{12,28},{14,30},{16,0},... | collective-permute-start | bytes 442376 | tf_op jit(solution)/shard_map/ppermute | solution.py:314
  343.0 13.5 %collective-permute-start.35 = (bf16[1,48,1536]{2,1,0:T(8,128)(2,1)S(1)}, bf16[1,48,1536]{2,1,0:T(8,128)(2,1)S(1)}, u32[]{:S(2)}, u32[]{:S(2)}) collective-permute-start(bf16[1,48,1536]{2,1,0:T(8,128)(2,1)S(1)} %get-tuple-element.104), channel_id=1, source_target_pairs={{0,24},{2,26},{4,28},{6,30},{8,16},{10,18},{12,20},{14,22},{16,8},... | collective-permute-start | bytes 442376 | tf_op jit(solution)/shard_map/ppermute | solution.py:314
  375.0 11.9 %collective-permute-start.26 = (bf16[4,48,384]{2,1,0:T(8,128)(2,1)S(1)}, bf16[4,48,384]{2,1,0:T(8,128)(2,1)S(1)}, u32[]{:S(2)}, u32[]{:S(2)}) collective-permute-start(bf16[4,48,384]{2,1,0:T(8,128)(2,1)S(1)} %get-tuple-element.108), channel_id=1, source_target_pairs={{0,16},{2,18},{4,20},{6,22},{8,24},{10,26},{12,28},{14,30},{16,0},... | collective-permute-start | bytes 442376 | tf_op jit(solution)/shard_map/ppermute | solution.py:314
  (115 other events, 893.3 us)
Sparse Core Ops, SparseCore 0:
  10.9 101.1 all-gather.1

commit v4 on v3

--- a/solution.py
+++ b/solution.py
@@ -342,7 +342,8 @@
     stage = pack(shards_in, after[0])
     stage = pack([stage] + [links.over_hi(stage, d) for d in range(1, links.hi_size)], after[1])
     stage = jnp.stack([stage, links.swap(stage, order[0])])
-    stage = jnp.stack([stage, links.swap(stage, order[1])])
+    second = [stage, links.swap(stage, order[1])]
+    stage = pack(second, after[2]) if after[2] else jnp.stack(second)
     other = links.swap(stage, "core")
     rows, columns = shards_in[0].shape
     where = jnp.stack([links.at["lo"], links.at["tensor"], links.hi, links.core]).astype(jnp.int32)
@@ -442,8 +443,14 @@
     inputs_seq = inputs.transpose(1, 0, 2).reshape(rows, D)
     rows_low = inputs_seq.astype(BF)
     rows_other = links.swap(rows_low, "tensor")
-    query_w, key_w = gather_tree(links, [query_weight, key_weight], ("tensor", "lo"), [[rows_low], [rows_other]])
-    value_w, out_w = gather_tree(links, [value_weight, out_weight.T], ("lo", "tensor"), [[rows_low], []])
+    cotangent = out_cotangent.transpose(1, 0, 2).reshape(rows, D)
+    second_shift_part = jnp.sum(cotangent, axis=0)
+    scaled_mean = jnp.mean(cotangent * second_gain, -1, keepdims=True)
+    idle = [cotangent, second_shift_part, scaled_mean.reshape(seqs, half)]
+    query_w, key_w = gather_tree(
+        links, [query_weight, key_weight], ("tensor", "lo"), [[rows_low], [rows_other], idle]
+    )
+    value_w, out_w = gather_tree(links, [value_weight, out_weight.T], ("lo", "tensor"), [[rows_low], [], []])
     queries, keys, values = project(rows_low, rows_other, query_w, key_w, value_w, query_bias, value_bias, seqs)
     context, log_sums = [], []
     for t in range(2):
@@ -463,10 +470,8 @@
     outputs, normed_two, inv_two = layer_norm(
         hidden + branch + output_projection_bias, second_gain, second_shift
     )
-    cotangent = out_cotangent.transpose(1, 0, 2).reshape(rows, D)
     second_grad = norm_back(cotangent, normed_two, inv_two, second_gain)
     second_gain_part = jnp.sum(cotangent * normed_two, axis=0)
-    second_shift_part = jnp.sum(cotangent, axis=0)
     down_bias_part = jnp.sum(second_grad, axis=0)
     second_low = second_grad.astype(BF)
     down_chip = halve_cores(links, [[dot(second_low, acts[t], 0, 0).astype(BF)] for t in range(2)])
@@ -510,7 +515,7 @@
             links, rows_low, rows_other, first_low, dq, dk, dv, context[t], after if t else []
         )
         chip.append(total)
-        after = [down_half, up_half, made]
+        after = [down_half, up_half, made, total]
     from_other = links.swap(other_total, "tensor")
     chip_half = [halve(links, c, "lo", 2) for c in chip]
     vectors = jnp.concatenate(

time: 401 us -> 392 us (0.978)
  local copies, waits for them, and re-layouts: 51.6 us -> 45.6 us
  waiting for transfers between devices: 87.6 us -> 83 us
    ppermute x8, waiting for transfers between devices: 47.4 us -> 26.4 us  [swap(): return lax.ppermute(v, 'tensor', [(0, 1), (1, 0)])]
    ppermute x31, waiting for transfers between devices: 40.1 us -> 56.7 us  [over_dp(): return lax.ppermute(v, 'dp', [(i, i ^ mask) for i in range(self.dp_size)])]
    pallas_call x6 -> x7, Pallas kernels: 9.64 us -> 12.2 us  [pack(): pl.pallas_call(functools.partial(pack_kernel, len(arrays)), in_specs=[ful...]
    unnamed x219 -> x228, local copies, waits for them, and re-layouts: 27.5 us -> 24.9 us
  transfers between devices with their start and end apart: 40 -> 40, of which waited for: 17 -> 19; matrix products, arithmetic and copies ran while one was open for 18% -> 18% of each run, Pallas kernels for 21% -> 22%
where the time goes in v4:
time: 392 us; the launch traced here: 387 us
  Pallas kernels  92.7 us (24%)
  waiting for transfers between devices  83 us (21%)
  matrix products  58.3 us (15%)
  starting transfers between devices  52.2 us (13%)
  local copies, waits for them, and re-layouts  45.6 us (12%)
  other arithmetic  38.8 us (10%)
  between operations  16.2 us (4%)
    dot_general x16, matrix products, dot(): lax.dot_general(a, b, (((da,), (db,)), ((), ())), preferred_element_type=...  58.3 us
    ppermute x31, waiting for transfers between devices, over_dp(): return lax.ppermute(v, 'dp', [(i, i ^ mask) for i in range(self.dp_size)])  56.7 us
    ppermute x31, starting transfers between devices, over_dp(): return lax.ppermute(v, 'dp', [(i, i ^ mask) for i in range(self.dp_size)])  43.8 us
    ppermute x8, waiting for transfers between devices, swap(): return lax.ppermute(v, 'tensor', [(0, 1), (1, 0)])  26.4 us
    pallas_call x2, Pallas kernels, attend_backward(): pl.pallas_call(functools.partial(attend_backward_kernel, width // HD, hal...  25.9 us
    unnamed x228, local copies, waits for them, and re-layouts  24.9 us
    pallas_call x2, Pallas kernels, attend_forward(): pl.pallas_call(functools.partial(attend_forward_kernel, width // HD, half...  20.6 us
    pallas_call x7, Pallas kernels, pack(): pl.pallas_call(functools.partial(pack_kernel, len(arrays)), in_specs=[ful...  12.2 us
  transfers between devices with their start and end apart: 40, of which 19 were waited for; matrix products, arithmetic and copies ran while one was open for 18% of the time, Pallas kernels for 22%

profile of v4, /device:TPU:0, one launch (start us, length us, event | category | flops | bytes accessed | tf_op | source)
XLA Modules:
  0.0 386.9 jit_solution(10662629821354797916)
XLA Ops:
  22.3 5.3 %collective-permute-done.8.refs_2_ = bf16[2,48,384]{2,1,0:T(8,128)(2,1)S(1)} collective-permute-done((bf16[2,48,384]{2,1,0:T(8,128)(2,1)}, bf16[2,48,384]{2,1,0:T(8,128)(2,1)S(1)}, u32[]{:S(2)}, u32[]{:S(2)}) %collective-permute-start.8) | collective-permute-done | bytes 73760 | tf_op jit(solution)/shard_map/ppermute | solution.py:314
  33.7 5.5 %collective-permute-done.10 = bf16[4,2,48,384]{3,2,1,0:T(8,128)(2,1)S(1)} collective-permute-done((bf16[4,2,48,384]{3,2,1,0:T(8,128)(2,1)}, bf16[4,2,48,384]{3,2,1,0:T(8,128)(2,1)S(1)}, u32[]{:S(2)}, u32[]{:S(2)}) %collective-permute-start.10) | collective-permute-done | bytes 294944 | tf_op jit(solution)/shard_map/ppermute | solution.py:314
  50.9 5.7 %collective-permute-done.2.refs_2_ = bf16[2,48,384]{2,1,0:T(8,128)(2,1)S(1)} collective-permute-done((bf16[2,48,384]{2,1,0:T(8,128)(2,1)}, bf16[2,48,384]{2,1,0:T(8,128)(2,1)S(1)}, u32[]{:S(2)}, u32[]{:S(2)}) %collective-permute-start.2) | collective-permute-done | bytes 73760 | tf_op jit(solution)/shard_map/ppermute | solution.py:314
  62.9 19.3 %collective-permute-done.4 = bf16[4,2,48,384]{3,2,1,0:T(8,128)(2,1)S(1)} collective-permute-done((bf16[4,2,48,384]{3,2,1,0:T(8,128)(2,1)}, bf16[4,2,48,384]{3,2,1,0:T(8,128)(2,1)S(1)}, u32[]{:S(2)}, u32[]{:S(2)}) %collective-permute-start.4) | collective-permute-done | bytes 294944 | tf_op jit(solution)/shard_map/ppermute | solution.py:318
  94.2 6.9 %collective-permute-done.5.refs_1_ = bf16[2,4,2,48,384]{4,3,2,1,0:T(8,128)(2,1)S(1)} collective-permute-done((bf16[2,4,2,48,384]{4,3,2,1,0:T(8,128)(2,1)S(1)}, bf16[2,4,2,48,384]{4,3,2,1,0:T(8,128)(2,1)S(1)}, u32[]{:S(2)}, u32[]{:S(2)}) %collective-permute-start.5) | collective-permute-done | bytes 589856 | tf_op jit(solution)/shard_map/ppermute | solution.py:314
  110.3 9.5 %project.1 = (bf16[1024,384]{1,0:T(8,128)(2,1)S(1)}, bf16[1024,384]{1,0:T(8,128)(2,1)S(1)}, bf16[2,1024,384]{2,1,0:T(8,128)(2,1)S(1)}, bf16[2,1024,384]{2,1,0:T(...) custom-call(bf16[1024,768]{1,0:T(8,128)(2,1)S(1)} %copy-done.7, ...), custom_call_target="tpu_custom_call" | custom-call | flops 6039797760 | bytes 16000000 | tf_op jit(solution)/shard_map/project/pallas_call | solution.py:267
  119.9 10.3 %attend_forward.3 = (bf16[1024,384]{1,0:T(8,128)(2,1)S(1)}, f32[4,256,128]{2,1,0:T(8,128)S(1)}) custom-call(s32[4]{0:T(128)S(1)} %copy-done.40, s32[1]{0:T(128)} %bitcast.2.tindex, bf16[1024,384]{1,0:T(8,128)(2,1)S(1)} %get-tuple-element.51.q_ref, bf16[2,1024,384]{2,1,0:T(8,128)(2,1)S(1)} %get-tuple-element.52.k_ref, ...), custom_call_target="tpu_custom_call" | custom-call | flops 8000000000 | bytes 5000000 | tf_op jit(solution)/shard_map/attend_forward/pallas_call | solution.py:121
  131.3 10.3 %attend_forward.2 = (bf16[1024,384]{1,0:T(8,128)(2,1)S(1)}, f32[4,256,128]{2,1,0:T(8,128)S(1)}) custom-call(s32[4]{0:T(128)S(1)} %copy-done.40, s32[1]{0:T(128)} %bitcast.2.tindex, bf16[1024,384]{1,0:T(8,128)(2,1)S(1)} %get-tuple-element.46.q_ref, bf16[2,1024,384]{2,1,0:T(8,128)(2,1)S(1)} %get-tuple-element.47.k_ref, ...), custom_call_target="tpu_custom_call" | custom-call | flops 8000000000 | bytes 5000000 | tf_op jit(solution)/shard_map/attend_forward/pallas_call | solution.py:121
  145.5 10.3 %fusion.5 = (bf16[1024,1536]{1,0:T(8,128)(2,1)}, bf16[1024,1536]{1,0:T(8,128)(2,1)S(1)}) fusion(f32[1536]{0:T(1024)S(1)} %copy-done.90, bf16[1024,768]{1,0:T(8,128)(2,1)} %fusion.13, bf16[2,768,3072]{2,1,0:T(8,128)(2,1)} %bitcast.287), kind=kOutput, calls=%fused_computation.9 | convolution fusion | flops 2456813568 | bytes 10229760 | tf_op jit(solution)/shard_map/dot_general | solution.py:21
  158.4 8.7 %fusion.11 = (bf16[1024,1536]{1,0:T(8,128)(2,1)}, bf16[1024,1536]{1,0:T(8,128)(2,1)S(1)}) fusion(f32[1536]{0:T(1024)S(1)} %copy-done.89, bf16[1024,768]{1,0:T(8,128)(2,1)S(1)} %copy-done.76, bf16[2,768,3072]{2,1,0:T(8,128)(2,1)S(1)} %bitcast.290), kind=kOutput, calls=%fused_computation.15 | convolution fusion | flops 2456813568 | bytes 10231808 | tf_op jit(solution)/shard_map/dot_general | solution.py:21
  188.4 4.3 %fusion.16 = f32[1024,768]{1,0:T(8,128)} fusion(bf16[1024,1536]{1,0:T(8,128)(2,1)S(1)} %get-tuple-element.133, bf16[2,768,3072]{2,1,0:T(8,128)(2,1)S(1)} %bitcast.293), kind=kOutput, calls=%fused_computation.63 | convolution fusion | flops 2415919104 | bytes 8650752 | tf_op jit(solution)/shard_map/dot_general | solution.py:21
  195.3 4.3 %convert_reduce_fusion = (f32[1536]{0:T(1024)S(1)}, bf16[1024,1536]{1,0:T(8,128)(2,1)S(1)}) fusion(bf16[1024,1536]{1,0:T(8,128)(2,1)} %get-tuple-element.85, bf16[1024,768]{1,0:T(8,128)(2,1)S(1)} %convert_element_type.293, bf16[2,768,3072]{2,1,0:T(8,128)(2,1)S(1)} %bitcast.294), kind=kOutput, calls=%fused_computation.16 | convolution fusion | flops 2423781888 | bytes 10229760 | tf_op jit(solution)/shard_map/dot_general | solution.py:21
  207.1 5.4 %multiply_reduce_fusion.1 = (f32[768]{0:T(1024)S(1)}, f32[1024]{0:T(1024)S(1)}, f32[1024]{0:T(1024)S(1)}, f32[768]{0:T(1024)S(1)}, f32[1024,768]{1,0:T(8,128)S(1)}) fusion(f32[1024,768]{1,0:T(8,128)S(1)} %get-tuple-element.128, f32[1024]{0:T(1024)S(1)} %add_rsqrt_fusion.1, f32[1024]{0:T(1024)S(1)} %broadcast_multiply_fusion.4, f32[768]{0:T(1024)S(1)} %copy-done.88, ...), kind=kOutput, calls=%fused_computation.34 | convolution fusion | flops 2424566272 | bytes 18113536 | tf_op jit(solution)/shard_map/dot_general | solution.py:21
  225.2 13.0 %attend_backward.2 = (bf16[1024,384]{1,0:T(8,128)(2,1)S(1)}, bf16[2,1024,384]{2,1,0:T(8,128)(2,1)S(1)}, bf16[2,1024,384]{2,1,0:T(8,128)(2,1)S(1)}, f32[4,2,384]{2,1,0:T(2,128)S(1)}) custom-call(s32[4]{0:T(128)S(1)} %copy-done.40, s32[1]{0:T(128)} %bitcast.2.tindex, bf16[1024,384]{1,0:T(8,128)(2,1)S(1)} %copy-done.52, bf16[2,1024,384]{2,1,0:T(8,128)(2,1)S(1)} %copy-done.46, ...), custom_call_target="tpu_custom_call" | custom-call | flops 17999998976 | bytes 10000000 | tf_op jit(solution)/shard_map/attend_backward/pallas_call | solution.py:140
  238.3 5.1 %weight_products.2 = (bf16[4,8,48,384]{3,2,1,0:T(8,128)(2,1)S(1)}, bf16[4,8,48,384]{3,2,1,0:T(8,128)(2,1)S(1)}) custom-call(s32[1]{0:T(128)} %bitcast.5.core, bf16[1024,768]{1,0:T(8,128)(2,1)S(1)} %copy-done.8, bf16[1024,768]{1,0:T(8,128)(2,1)S(1)} %copy-done.29, bf16[1024,768]{1,0:T(8,128)(2,1)S(1)} %convert_element_type.300.first_ref, ...), custom_call_target="tpu_custom_call" | custom-call | flops 3623878656 | bytes 10000000 | tf_op jit(solution)/shard_map/weight_products/pallas_call | solution.py:233
  243.5 4.3 %collective-permute-done.15 = bf16[1,4,2,48,1536]{4,3,1,2,0:T(8,128)(2,1)} collective-permute-done((bf16[1,4,2,48,1536]{4,3,1,2,0:T(8,128)(2,1)S(1)}, bf16[1,4,2,48,1536]{4,3,1,2,0:T(8,128)(2,1)}, u32[]{:S(2)}, u32[]{:S(2)}) %collective-permute-start.15) | collective-permute-done | bytes 1179680 | tf_op jit(solution)/shard_map/ppermute | solution.py:318
  255.5 12.8 %attend_backward.3 = (bf16[1024,384]{1,0:T(8,128)(2,1)S(1)}, bf16[2,1024,384]{2,1,0:T(8,128)(2,1)S(1)}, bf16[2,1024,384]{2,1,0:T(8,128)(2,1)S(1)}, f32[4,2,384]{2,1,0:T(2,128)S(1)}) custom-call(s32[4]{0:T(128)S(1)} %copy-done.40, s32[1]{0:T(128)} %bitcast.2.tindex, bf16[1024,384]{1,0:T(8,128)(2,1)S(1)} %copy-done.50, bf16[2,1024,384]{2,1,0:T(8,128)(2,1)S(1)} %copy-done.42, ...), custom_call_target="tpu_custom_call" | custom-call | flops 17999998976 | bytes 10000000 | tf_op jit(solution)/shard_map/attend_backward/pallas_call | solution.py:140
  268.4 4.2 %back_product.3.rest_0_ = bf16[1024,768]{1,0:T(8,128)(2,1)S(1)} custom-call(bf16[2,1024,384]{2,1,0:T(8,128)(2,1)S(1)} %get-tuple-element.58.dk_ref.refs_2_.refs_0_, bf16[2,1024,384]{2,1,0:T(8,128)(2,1)S(1)} %get-tuple-element.63.refs_3_.refs_1_.dk_ref, bf16[2,1024,384]{2,1,0:T(8,128)(2,1)S(1)} %get-tuple-element.59.dv_ref.refs_4_.refs_2_, ...), custom_call_target="tpu_custom_call" | custom-call | flops 2415919104 | bytes 8000000 | tf_op jit(solution)/shard_map/back_product/pallas_call | solution.py:182
  274.5 6.1 %weight_products.3 = (bf16[4,8,48,384]{3,2,1,0:T(8,128)(2,1)S(1)}, bf16[4,8,48,384]{3,2,1,0:T(8,128)(2,1)}) custom-call(s32[1]{0:T(128)} %bitcast.5.core, bf16[1024,768]{1,0:T(8,128)(2,1)S(1)} %copy-done.8, bf16[1024,768]{1,0:T(8,128)(2,1)S(1)} %copy-done.29, bf16[1024,768]{1,0:T(8,128)(2,1)S(1)} %convert_element_type.300.first_ref, ...), custom_call_target="tpu_custom_call" | custom-call | flops 3623878656 | bytes 10000000 | tf_op jit(solution)/shard_map/weight_products/pallas_call | solution.py:233
  297.0 5.9 %back_product.2 = f32[1024,768]{1,0:T(8,128)S(1)} custom-call(bf16[1024,384]{1,0:T(8,128)(2,1)S(1)} %copy-done.37, bf16[1024,384]{1,0:T(8,128)(2,1)S(1)} %copy-done.39, bf16[2,1024,384]{2,1,0:T(8,128)(2,1)S(1)} %copy-done.14, bf16[2,1024,384]{2,1,0:T(8,128)(2,1)S(1)} %copy-done.18, bf16[2,1024,384]{2,1,0:T(8,128)(2,1)S(1)} %copy-done.16, ...), custom_call_target="tpu_custom_call" | custom-call | flops 3623878656 | bytes 8000000 | tf_op jit(solution)/shard_map/back_product/pallas_call | solution.py:182
  304.5 9.9 %collective-permute-done.23 = bf16[4,4,48,384]{3,2,1,0:T(8,128)(2,1)S(1)} collective-permute-done((bf16[4,4,48,384]{3,2,1,0:T(8,128)(2,1)S(1)}, bf16[4,4,48,384]{3,2,1,0:T(8,128)(2,1)S(1)}, u32[]{:S(2)}, u32[]{:S(2)}) %collective-permute-start.23) | collective-permute-done | bytes 589856 | tf_op jit(solution)/shard_map/ppermute | solution.py:314
  329.3 5.2 %collective-permute-done.37 = bf16[1,48,1536]{2,1,0:T(8,128)(2,1)S(1)} collective-permute-done((bf16[1,48,1536]{2,1,0:T(8,128)(2,1)S(1)}, bf16[1,48,1536]{2,1,0:T(8,128)(2,1)S(1)}, u32[]{:S(2)}, u32[]{:S(2)}) %collective-permute-start.37) | collective-permute-done | bytes 147488 | tf_op jit(solution)/shard_map/ppermute | solution.py:314
  340.8 7.1 %collective-permute-start.31 = (f32[72,128]{1,0:T(8,128)S(1)}, f32[72,128]{1,0:T(8,128)S(1)}, u32[]{:S(2)}, u32[]{:S(2)}) collective-permute-start(f32[72,128]{1,0:T(8,128)S(1)} %add.318), channel_id=1, source_target_pairs={{0,8},{2,10},{4,12},{6,14},{8,0},{10,2},{12,4},{14,6},{16,24},{18,... | collective-permute-start | bytes 110600 | tf_op jit(solution)/shard_map/ppermute | solution.py:314
  370.9 7.8 %collective-permute-done.26 = bf16[4,48,384]{2,1,0:T(8,128)(2,1)S(1)} collective-permute-done((bf16[4,48,384]{2,1,0:T(8,128)(2,1)S(1)}, bf16[4,48,384]{2,1,0:T(8,128)(2,1)S(1)}, u32[]{:S(2)}, u32[]{:S(2)}) %collective-permute-start.26) | collective-permute-done | bytes 147488 | tf_op jit(solution)/shard_map/ppermute | solution.py:314
  (395 shorter events, 183.5 us)
Async XLA Ops:
  7.2 138.3 %all-gather.2.cloned.1.call-start = ((), (), s32[]{:S(2)}) async-start(), calls=%async_computation | async-start | bytes 9732096 | tf_op jit(solution)/shard_map/all_gather | solution.py:438
  13.3 45.7 %collective-permute-start = (bf16[1024,768]{1,0:T(8,128)(2,1)S(1)}, bf16[1024,768]{1,0:T(8,128)(2,1)S(1)}, u32[]{:S(2)}, u32[]{:S(2)}) collective-permute-start(bf16[1024,768]{1,0:T(8,128)(2,1)S(1)} %bitcast_convert_fusion.refs_2_.own_ref), channel_id=1, source_target_pairs={{0,1},{1,0},{2,3},{3,2},{4,5},{5,4},{6,7},{7,6},{8,9},{9,8},{10,11... | collective-permute-start | bytes 4718600 | tf_op jit(solution)/shard_map/ppermute | solution.py:318
  41.2 43.3 %collective-permute-start.11 = (bf16[2,4,2,48,384]{4,3,2,1,0:T(8,128)(2,1)}, bf16[2,4,2,48,384]{4,3,2,1,0:T(8,128)(2,1)}, u32[]{:S(2)}, u32[]{:S(2)}) collective-permute-start(bf16[2,4,2,48,384]{4,3,2,1,0:T(8,128)(2,1)} %get-tuple-element.110), channel_id=1, source_target_pairs={{0,1},{1,0},{2,3},{3,2},{4,5},{5,4},{6,7},{7,6},{8,9},{9,8},{10,11... | collective-permute-start | bytes 1769480 | tf_op jit(solution)/shard_map/ppermute | solution.py:318
  62.6 19.5 %collective-permute-start.4 = (bf16[4,2,48,384]{3,2,1,0:T(8,128)(2,1)}, bf16[4,2,48,384]{3,2,1,0:T(8,128)(2,1)S(1)}, u32[]{:S(2)}, u32[]{:S(2)}) collective-permute-start(bf16[4,2,48,384]{3,2,1,0:T(8,128)(2,1)} %pack_shards.8), channel_id=1, source_target_pairs={{0,1},{1,0},{2,3},{3,2},{4,5},{5,4},{6,7},{7,6},{8,9},{9,8},{10,11... | collective-permute-start | bytes 884744 | tf_op jit(solution)/shard_map/ppermute | solution.py:318
  83.2 18.0 %collective-permute-start.5 = (bf16[2,4,2,48,384]{4,3,2,1,0:T(8,128)(2,1)S(1)}, bf16[2,4,2,48,384]{4,3,2,1,0:T(8,128)(2,1)S(1)}, u32[]{:S(2)}, u32[]{:S(2)}) collective-permute-start(bf16[2,4,2,48,384]{4,3,2,1,0:T(8,128)(2,1)S(1)} %pad_maximum_fusion.3.refs_0_), channel_id=1, source_target_pairs={{0,4},{2,6},{4,0},{6,2},{8,12},{10,14},{12,8},{14,10},{16,20},{18,... | collective-permute-start | bytes 1769480 | tf_op jit(solution)/shard_map/ppermute | solution.py:314
  85.9 20.9 %collective-permute-start.12 = (bf16[2,2,4,2,48,384]{5,4,3,2,1,0:T(8,128)(2,1)S(1)}, bf16[2,2,4,2,48,384]{5,4,3,2,1,0:T(8,128)(2,1)S(1)}, u32[]{:S(2)}, u32[]{:S(2)}) collective-permute-start(bf16[2,2,4,2,48,384]{5,4,3,2,1,0:T(8,128)(2,1)S(1)} %pad_maximum_fusion.2.mine_ref), channel_id=1, source_target_pairs={{0,2},{2,0},{4,6},{6,4},{8,10},{10,8},{12,14},{14,12},{16,18},{18,... | collective-permute-start | bytes 3538952 | tf_op jit(solution)/shard_map/ppermute | solution.py:314
  194.9 23.7 %collective-permute-start.13 = (bf16[2,1,4,2,48,1536]{5,4,2,3,1,0:T(8,128)(2,1)}, bf16[2,1,4,2,48,1536]{5,4,2,3,1,0:T(8,128)(2,1)S(1)}, u32[]{:S(2)}, u32[]{:S(2)}) collective-permute-start(bf16[2,1,4,2,48,1536]{5,4,2,3,1,0:T(8,128)(2,1)} %pad_maximum_fusion), channel_id=1, source_target_pairs={{0,2},{2,0},{4,6},{6,4},{8,10},{10,8},{12,14},{14,12},{16,18},{18,... | collective-permute-start | bytes 7077896 | tf_op jit(solution)/shard_map/ppermute | solution.py:314
  205.2 16.0 %collective-permute-start.14 = (bf16[2,1,4,2,48,1536]{5,4,2,0,3,1:T(8,128)(2,1)}, bf16[2,1,4,2,48,1536]{5,4,2,0,3,1:T(8,128)(2,1)S(1)}, u32[]{:S(2)}, u32[]{:S(2)}) collective-permute-start(bf16[2,1,4,2,48,1536]{5,4,2,0,3,1:T(8,128)(2,1)} %pad_maximum_fusion.1), channel_id=1, source_target_pairs={{0,2},{2,0},{4,6},{6,4},{8,10},{10,8},{12,14},{14,12},{16,18},{18,... | collective-permute-start | bytes 7077896 | tf_op jit(solution)/shard_map/ppermute | solution.py:314
  219.7 28.1 %collective-permute-start.15 = (bf16[1,4,2,48,1536]{4,3,1,2,0:T(8,128)(2,1)S(1)}, bf16[1,4,2,48,1536]{4,3,1,2,0:T(8,128)(2,1)}, u32[]{:S(2)}, u32[]{:S(2)}) collective-permute-start(bf16[1,4,2,48,1536]{4,3,1,2,0:T(8,128)(2,1)S(1)} %dynamic-slice_bitcast_fusion.1), channel_id=1, source_target_pairs={{0,1},{1,0},{2,3},{3,2},{4,5},{5,4},{6,7},{7,6},{8,9},{9,8},{10,11... | collective-permute-start | bytes 3538952 | tf_op jit(solution)/shard_map/ppermute | solution.py:318
  223.3 27.8 %collective-permute-start.16 = (bf16[2,1,4,48,1536]{4,3,2,1,0:T(8,128)(2,1)S(1)}, bf16[2,1,4,48,1536]{4,3,2,1,0:T(8,128)(2,1)}, u32[]{:S(2)}, u32[]{:S(2)}) collective-permute-start(bf16[2,1,4,48,1536]{4,3,2,1,0:T(8,128)(2,1)S(1)} %dynamic-slice_bitcast_fusion), channel_id=1, source_target_pairs={{0,4},{2,6},{4,0},{6,2},{8,12},{10,14},{12,8},{14,10},{16,20},{18,... | collective-permute-start | bytes 3538952 | tf_op jit(solution)/shard_map/ppermute | solution.py:314
  249.5 23.1 %collective-permute-start.20 = (bf16[1,4,48,1536]{3,2,1,0:T(8,128)(2,1)S(1)}, bf16[1,4,48,1536]{3,2,1,0:T(8,128)(2,1)}, u32[]{:S(2)}, u32[]{:S(2)}) collective-permute-start(bf16[1,4,48,1536]{3,2,1,0:T(8,128)(2,1)S(1)} %dynamic-slice_bitcast_fusion.4), channel_id=1, source_target_pairs={{0,4},{2,6},{4,0},{6,2},{8,12},{10,14},{12,8},{14,10},{16,20},{18,... | collective-permute-start | bytes 1769480 | tf_op jit(solution)/shard_map/ppermute | solution.py:314
  252.8 21.5 %collective-permute-start.21 = (bf16[1,4,48,1536]{3,2,1,0:T(8,128)(2,1)S(1)}, bf16[1,4,48,1536]{3,2,1,0:T(8,128)(2,1)S(1)}, u32[]{:S(2)}, u32[]{:S(2)}) collective-permute-start(bf16[1,4,48,1536]{3,2,1,0:T(8,128)(2,1)S(1)} %dynamic-slice_bitcast_fusion.3), channel_id=1, source_target_pairs={{0,1},{1,0},{2,3},{3,2},{4,5},{5,4},{6,7},{7,6},{8,9},{9,8},{10,11... | collective-permute-start | bytes 1769480 | tf_op jit(solution)/shard_map/ppermute | solution.py:318
  284.6 65.0 %collective-permute-start.18 = (bf16[1024,768]{1,0:T(8,128)(2,1)}, bf16[1024,768]{1,0:T(8,128)(2,1)}, u32[]{:S(2)}, u32[]{:S(2)}) collective-permute-start(bf16[1024,768]{1,0:T(8,128)(2,1)} %copy-done.30), channel_id=1, source_target_pairs={{0,1},{1,0},{2,3},{3,2},{4,5},{5,4},{6,7},{7,6},{8,9},{9,8},{10,11... | collective-permute-start | bytes 4718600 | tf_op jit(solution)/shard_map/ppermute | solution.py:318
  286.2 18.3 %collective-permute-start.19 = (bf16[4,4,48,384]{3,2,1,0:T(8,128)(2,1)S(1)}, bf16[4,4,48,384]{3,2,1,0:T(8,128)(2,1)S(1)}, u32[]{:S(2)}, u32[]{:S(2)}) collective-permute-start(bf16[4,4,48,384]{3,2,1,0:T(8,128)(2,1)S(1)} %dynamic-slice_bitcast_fusion.5), channel_id=1, source_target_pairs={{0,4},{2,6},{4,0},{6,2},{8,12},{10,14},{12,8},{14,10},{16,20},{18,... | collective-permute-start | bytes 1769480 | tf_op jit(solution)/shard_map/ppermute | solution.py:314
  290.1 24.4 %collective-permute-start.23 = (bf16[4,4,48,384]{3,2,1,0:T(8,128)(2,1)S(1)}, bf16[4,4,48,384]{3,2,1,0:T(8,128)(2,1)S(1)}, u32[]{:S(2)}, u32[]{:S(2)}) collective-permute-start(bf16[4,4,48,384]{3,2,1,0:T(8,128)(2,1)S(1)} %dynamic-slice_bitcast_fusion.2), channel_id=1, source_target_pairs={{0,4},{2,6},{4,0},{6,2},{8,12},{10,14},{12,8},{14,10},{16,20},{18,... | collective-permute-start | bytes 1769480 | tf_op jit(solution)/shard_map/ppermute | solution.py:314
  320.4 14.1 %collective-permute-start.37 = (bf16[1,48,1536]{2,1,0:T(8,128)(2,1)S(1)}, bf16[1,48,1536]{2,1,0:T(8,128)(2,1)S(1)}, u32[]{:S(2)}, u32[]{:S(2)}) collective-permute-start(bf16[1,48,1536]{2,1,0:T(8,128)(2,1)S(1)} %get-tuple-element.102), channel_id=1, source_target_pairs={{0,16},{2,18},{4,20},{6,22},{8,24},{10,26},{12,28},{14,30},{16,0},... | collective-permute-start | bytes 442376 | tf_op jit(solution)/shard_map/ppermute | solution.py:314
  322.9 14.0 %collective-permute-start.38 = (bf16[1,48,1536]{2,1,0:T(8,128)(2,1)S(1)}, bf16[1,48,1536]{2,1,0:T(8,128)(2,1)S(1)}, u32[]{:S(2)}, u32[]{:S(2)}) collective-permute-start(bf16[1,48,1536]{2,1,0:T(8,128)(2,1)S(1)} %get-tuple-element.101), channel_id=1, source_target_pairs={{0,24},{2,26},{4,28},{6,30},{8,16},{10,18},{12,20},{14,22},{16,8},... | collective-permute-start | bytes 442376 | tf_op jit(solution)/shard_map/ppermute | solution.py:314
  325.4 22.5 %collective-permute-start.33 = (bf16[1,48,1536]{2,1,0:T(8,128)(2,1)S(1)}, bf16[1,48,1536]{2,1,0:T(8,128)(2,1)S(1)}, u32[]{:S(2)}, u32[]{:S(2)}) collective-permute-start(bf16[1,48,1536]{2,1,0:T(8,128)(2,1)S(1)} %get-tuple-element.103), channel_id=1, source_target_pairs={{0,8},{2,10},{4,12},{6,14},{8,0},{10,2},{12,4},{14,6},{16,24},{18,... | collective-permute-start | bytes 442376 | tf_op jit(solution)/shard_map/ppermute | solution.py:314
  326.0 21.9 %collective-permute-start.34 = (bf16[1,48,1536]{2,1,0:T(8,128)(2,1)S(1)}, bf16[1,48,1536]{2,1,0:T(8,128)(2,1)S(1)}, u32[]{:S(2)}, u32[]{:S(2)}) collective-permute-start(bf16[1,48,1536]{2,1,0:T(8,128)(2,1)S(1)} %get-tuple-element.105), channel_id=1, source_target_pairs={{0,16},{2,18},{4,20},{6,22},{8,24},{10,26},{12,28},{14,30},{16,0},... | collective-permute-start | bytes 442376 | tf_op jit(solution)/shard_map/ppermute | solution.py:314
  334.5 13.4 %collective-permute-start.35 = (bf16[1,48,1536]{2,1,0:T(8,128)(2,1)S(1)}, bf16[1,48,1536]{2,1,0:T(8,128)(2,1)S(1)}, u32[]{:S(2)}, u32[]{:S(2)}) collective-permute-start(bf16[1,48,1536]{2,1,0:T(8,128)(2,1)S(1)} %get-tuple-element.104), channel_id=1, source_target_pairs={{0,24},{2,26},{4,28},{6,30},{8,16},{10,18},{12,20},{14,22},{16,8},... | collective-permute-start | bytes 442376 | tf_op jit(solution)/shard_map/ppermute | solution.py:314
  340.8 11.2 %collective-permute-start.31 = (f32[72,128]{1,0:T(8,128)S(1)}, f32[72,128]{1,0:T(8,128)S(1)}, u32[]{:S(2)}, u32[]{:S(2)}) collective-permute-start(f32[72,128]{1,0:T(8,128)S(1)} %add.318), channel_id=1, source_target_pairs={{0,8},{2,10},{4,12},{6,14},{8,0},{10,2},{12,4},{14,6},{16,24},{18,... | collective-permute-start | bytes 110600 | tf_op jit(solution)/shard_map/ppermute | solution.py:314
  351.6 11.1 %collective-permute-start.24 = (bf16[4,4,48,384]{3,2,1,0:T(8,128)(2,1)}, bf16[4,4,48,384]{3,2,1,0:T(8,128)(2,1)S(1)}, u32[]{:S(2)}, u32[]{:S(2)}) collective-permute-start(bf16[4,4,48,384]{3,2,1,0:T(8,128)(2,1)} %bitcast.279), channel_id=1, source_target_pairs={{0,1},{1,0},{2,3},{3,2},{4,5},{5,4},{6,7},{7,6},{8,9},{9,8},{10,11... | collective-permute-start | bytes 1769480 | tf_op jit(solution)/shard_map/ppermute | solution.py:318
  366.8 11.9 %collective-permute-start.26 = (bf16[4,48,384]{2,1,0:T(8,128)(2,1)S(1)}, bf16[4,48,384]{2,1,0:T(8,128)(2,1)S(1)}, u32[]{:S(2)}, u32[]{:S(2)}) collective-permute-start(bf16[4,48,384]{2,1,0:T(8,128)(2,1)S(1)} %get-tuple-element.108), channel_id=1, source_target_pairs={{0,16},{2,18},{4,20},{6,22},{8,24},{10,26},{12,28},{14,30},{16,0},... | collective-permute-start | bytes 442376 | tf_op jit(solution)/shard_map/ppermute | solution.py:314
  367.8 10.9 %collective-permute-start.27 = (bf16[4,48,384]{2,1,0:T(8,128)(2,1)S(1)}, bf16[4,48,384]{2,1,0:T(8,128)(2,1)S(1)}, u32[]{:S(2)}, u32[]{:S(2)}) collective-permute-start(bf16[4,48,384]{2,1,0:T(8,128)(2,1)S(1)} %get-tuple-element.107), channel_id=1, source_target_pairs={{0,24},{2,26},{4,28},{6,30},{8,16},{10,18},{12,20},{14,22},{16,8},... | collective-permute-start | bytes 442376 | tf_op jit(solution)/shard_map/ppermute | solution.py:314
  (120 other events, 918.6 us)
Sparse Core Ops, SparseCore 0:
  11.5 96.8 all-gather.1

commit v5 on v4

--- a/solution.py
+++ b/solution.py
@@ -533,7 +533,11 @@
                 bias_parts[1][1],
             ]
         ).reshape(-1, 128)
-    sums = sum_everywhere(links, pack([vectors], [chip[1], chip_half[0]])[0]).reshape(-1)
+    first_side = links.at["tensor"] == 0
+    mine = jnp.where(first_side, chip_half[0], chip_half[1])
+    theirs = jnp.where(first_side, chip_half[1], chip_half[0])
+    total_half = add_low(mine, links.swap(theirs, "tensor"))
+    sums = sum_everywhere(links, pack([vectors], [total_half])[0]).reshape(-1)
     (
         out_bias_sum,
         first_gain_sum,
@@ -557,12 +561,7 @@
     input_grad = own_total + from_other.astype(F32)
     (down_sum,) = finish(links, down_quarter)
     (up_sum,) = finish(links, up_quarter)
-    first_side = links.at["tensor"] == 0
-    mine = jnp.where(first_side, chip_half[0], chip_half[1])
-    theirs = jnp.where(first_side, chip_half[1], chip_half[0])
-    query_sum, key_sum, value_sum, out_sum = finish(
-        links, add_low(mine, links.swap(pack([theirs], [from_other])[0], "tensor"))
-    )
+    query_sum, key_sum, value_sum, out_sum = finish(links, total_half)
 
     def positions_first(v):
         return v.reshape(seqs, half, D).transpose(1, 0, 2)

time: 392 us -> 389 us (level)
  starting transfers between devices: 52.2 us -> 44.8 us
  waiting for transfers between devices: 83 us -> 88.5 us
    ppermute x8, waiting for transfers between devices: 26.4 us -> 37.4 us  [swap(): return lax.ppermute(v, 'tensor', [(0, 1), (1, 0)])]
    ppermute x31, starting transfers between devices: 43.8 us -> 36.5 us  [over_dp(): return lax.ppermute(v, 'dp', [(i, i ^ mask) for i in range(self.dp_size)])]
    ppermute x31, waiting for transfers between devices: 56.7 us -> 51 us  [over_dp(): return lax.ppermute(v, 'dp', [(i, i ^ mask) for i in range(self.dp_size)])]
    pallas_call x7 -> x6, Pallas kernels: 12.2 us -> 10.4 us  [pack(): pl.pallas_call(functools.partial(pack_kernel, len(arrays)), in_specs=[ful...]
    unnamed x228 -> x220, local copies, waits for them, and re-layouts: 24.9 us -> 23.2 us
  transfers between devices with their start and end apart: 40 -> 40, of which waited for: 19 -> 18; matrix products, arithmetic and copies ran while one was open for 18% -> 18% of each run, Pallas kernels for 22% -> 22%
where the time goes in v5:
time: 389 us; the launch traced here: 384 us
  Pallas kernels  90.9 us (23%)
  waiting for transfers between devices  88.5 us (23%)
  matrix products  58.3 us (15%)
  local copies, waits for them, and re-layouts  45.4 us (12%)
  starting transfers between devices  44.8 us (12%)
  other arithmetic  39.7 us (10%)
  between operations  16.2 us (4%)
    dot_general x16, matrix products, dot(): lax.dot_general(a, b, (((da,), (db,)), ((), ())), preferred_element_type=...  58.3 us
    ppermute x31, waiting for transfers between devices, over_dp(): return lax.ppermute(v, 'dp', [(i, i ^ mask) for i in range(self.dp_size)])  51 us
    ppermute x8, waiting for transfers between devices, swap(): return lax.ppermute(v, 'tensor', [(0, 1), (1, 0)])  37.4 us
    ppermute x31, starting transfers between devices, over_dp(): return lax.ppermute(v, 'dp', [(i, i ^ mask) for i in range(self.dp_size)])  36.5 us
    pallas_call x2, Pallas kernels, attend_backward(): pl.pallas_call(functools.partial(attend_backward_kernel, width // HD, hal...  25.8 us
    unnamed x220, local copies, waits for them, and re-layouts  23.2 us
    pallas_call x2, Pallas kernels, attend_forward(): pl.pallas_call(functools.partial(attend_forward_kernel, width // HD, half...  20.6 us
    pallas_call x2, Pallas kernels, weight_products(): pl.pallas_call(weight_kernel, in_specs=[pl.BlockSpec(memory_space=pltpu.S...  11.2 us
  transfers between devices with their start and end apart: 40, of which 18 were waited for; matrix products, arithmetic and copies ran while one was open for 18% of the time, Pallas kernels for 22%

profile of v5, /device:TPU:0, one launch (start us, length us, event | category | flops | bytes accessed | tf_op | source)
XLA Modules:
  0.0 383.7 jit_solution(11133178861928205514)
XLA Ops:
  22.3 5.3 %collective-permute-done.8.refs_2_ = bf16[2,48,384]{2,1,0:T(8,128)(2,1)S(1)} collective-permute-done((bf16[2,48,384]{2,1,0:T(8,128)(2,1)}, bf16[2,48,384]{2,1,0:T(8,128)(2,1)S(1)}, u32[]{:S(2)}, u32[]{:S(2)}) %collective-permute-start.8) | collective-permute-done | bytes 73760 | tf_op jit(solution)/shard_map/ppermute | solution.py:314
  33.7 5.5 %collective-permute-done.10 = bf16[4,2,48,384]{3,2,1,0:T(8,128)(2,1)S(1)} collective-permute-done((bf16[4,2,48,384]{3,2,1,0:T(8,128)(2,1)}, bf16[4,2,48,384]{3,2,1,0:T(8,128)(2,1)S(1)}, u32[]{:S(2)}, u32[]{:S(2)}) %collective-permute-start.10) | collective-permute-done | bytes 294944 | tf_op jit(solution)/shard_map/ppermute | solution.py:314
  51.2 6.4 %collective-permute-done.2.refs_2_ = bf16[2,48,384]{2,1,0:T(8,128)(2,1)S(1)} collective-permute-done((bf16[2,48,384]{2,1,0:T(8,128)(2,1)}, bf16[2,48,384]{2,1,0:T(8,128)(2,1)S(1)}, u32[]{:S(2)}, u32[]{:S(2)}) %collective-permute-start.2) | collective-permute-done | bytes 73760 | tf_op jit(solution)/shard_map/ppermute | solution.py:314
  62.9 19.3 %collective-permute-done.4 = bf16[4,2,48,384]{3,2,1,0:T(8,128)(2,1)S(1)} collective-permute-done((bf16[4,2,48,384]{3,2,1,0:T(8,128)(2,1)}, bf16[4,2,48,384]{3,2,1,0:T(8,128)(2,1)S(1)}, u32[]{:S(2)}, u32[]{:S(2)}) %collective-permute-start.4) | collective-permute-done | bytes 294944 | tf_op jit(solution)/shard_map/ppermute | solution.py:318
  94.2 6.9 %collective-permute-done.5.refs_1_ = bf16[2,4,2,48,384]{4,3,2,1,0:T(8,128)(2,1)S(1)} collective-permute-done((bf16[2,4,2,48,384]{4,3,2,1,0:T(8,128)(2,1)S(1)}, bf16[2,4,2,48,384]{4,3,2,1,0:T(8,128)(2,1)S(1)}, u32[]{:S(2)}, u32[]{:S(2)}) %collective-permute-start.5) | collective-permute-done | bytes 589856 | tf_op jit(solution)/shard_map/ppermute | solution.py:314
  110.3 9.5 %project.1 = (bf16[1024,384]{1,0:T(8,128)(2,1)S(1)}, bf16[1024,384]{1,0:T(8,128)(2,1)S(1)}, bf16[2,1024,384]{2,1,0:T(8,128)(2,1)S(1)}, bf16[2,1024,384]{2,1,0:T(...) custom-call(bf16[1024,768]{1,0:T(8,128)(2,1)S(1)} %copy-done.9, ...), custom_call_target="tpu_custom_call" | custom-call | flops 6039797760 | bytes 16000000 | tf_op jit(solution)/shard_map/project/pallas_call | solution.py:267
  119.9 10.3 %attend_forward.3 = (bf16[1024,384]{1,0:T(8,128)(2,1)S(1)}, f32[4,256,128]{2,1,0:T(8,128)S(1)}) custom-call(s32[4]{0:T(128)S(1)} %copy-done.41, s32[1]{0:T(128)} %bitcast.2.tindex, bf16[1024,384]{1,0:T(8,128)(2,1)S(1)} %get-tuple-element.51.q_ref, bf16[2,1024,384]{2,1,0:T(8,128)(2,1)S(1)} %get-tuple-element.52.k_ref, ...), custom_call_target="tpu_custom_call" | custom-call | flops 8000000000 | bytes 5000000 | tf_op jit(solution)/shard_map/attend_forward/pallas_call | solution.py:121
  131.3 10.3 %attend_forward.2 = (bf16[1024,384]{1,0:T(8,128)(2,1)S(1)}, f32[4,256,128]{2,1,0:T(8,128)S(1)}) custom-call(s32[4]{0:T(128)S(1)} %copy-done.41, s32[1]{0:T(128)} %bitcast.2.tindex, bf16[1024,384]{1,0:T(8,128)(2,1)S(1)} %get-tuple-element.46.q_ref, bf16[2,1024,384]{2,1,0:T(8,128)(2,1)S(1)} %get-tuple-element.47.k_ref, ...), custom_call_target="tpu_custom_call" | custom-call | flops 8000000000 | bytes 5000000 | tf_op jit(solution)/shard_map/attend_forward/pallas_call | solution.py:121
  145.4 10.3 %fusion.5 = (bf16[1024,1536]{1,0:T(8,128)(2,1)}, bf16[1024,1536]{1,0:T(8,128)(2,1)S(1)}) fusion(f32[1536]{0:T(1024)S(1)} %copy-done.86, bf16[1024,768]{1,0:T(8,128)(2,1)} %fusion.13, bf16[2,768,3072]{2,1,0:T(8,128)(2,1)} %bitcast.288), kind=kOutput, calls=%fused_computation.9 | convolution fusion | flops 2456813568 | bytes 10229760 | tf_op jit(solution)/shard_map/dot_general | solution.py:21
  158.4 8.7 %fusion.11 = (bf16[1024,1536]{1,0:T(8,128)(2,1)}, bf16[1024,1536]{1,0:T(8,128)(2,1)S(1)}) fusion(f32[1536]{0:T(1024)S(1)} %copy-done.85, bf16[1024,768]{1,0:T(8,128)(2,1)S(1)} %copy-done.72, bf16[2,768,3072]{2,1,0:T(8,128)(2,1)S(1)} %bitcast.291), kind=kOutput, calls=%fused_computation.15 | convolution fusion | flops 2456813568 | bytes 10231808 | tf_op jit(solution)/shard_map/dot_general | solution.py:21
  188.3 4.3 %fusion.16 = f32[1024,768]{1,0:T(8,128)} fusion(bf16[1024,1536]{1,0:T(8,128)(2,1)S(1)} %get-tuple-element.131, bf16[2,768,3072]{2,1,0:T(8,128)(2,1)S(1)} %bitcast.294), kind=kOutput, calls=%fused_computation.63 | convolution fusion | flops 2415919104 | bytes 8650752 | tf_op jit(solution)/shard_map/dot_general | solution.py:21
  195.3 4.3 %convert_reduce_fusion = (f32[1536]{0:T(1024)S(1)}, bf16[1024,1536]{1,0:T(8,128)(2,1)S(1)}) fusion(bf16[1024,1536]{1,0:T(8,128)(2,1)} %get-tuple-element.83, bf16[1024,768]{1,0:T(8,128)(2,1)S(1)} %convert_element_type.293, bf16[2,768,3072]{2,1,0:T(8,128)(2,1)S(1)} %bitcast.295), kind=kOutput, calls=%fused_computation.16 | convolution fusion | flops 2423781888 | bytes 10229760 | tf_op jit(solution)/shard_map/dot_general | solution.py:21
  207.0 5.4 %multiply_reduce_fusion.1 = (f32[768]{0:T(1024)S(1)}, f32[1024]{0:T(1024)S(1)}, f32[1024]{0:T(1024)S(1)}, f32[768]{0:T(1024)S(1)}, f32[1024,768]{1,0:T(8,128)S(1)}) fusion(f32[1024,768]{1,0:T(8,128)S(1)} %get-tuple-element.126, f32[1024]{0:T(1024)S(1)} %add_rsqrt_fusion.1, f32[1024]{0:T(1024)S(1)} %broadcast_multiply_fusion.4, f32[768]{0:T(1024)S(1)} %copy-done.84, ...), kind=kOutput, calls=%fused_computation.34 | convolution fusion | flops 2424566272 | bytes 18113536 | tf_op jit(solution)/shard_map/dot_general | solution.py:21
  225.1 13.0 %attend_backward.2 = (bf16[1024,384]{1,0:T(8,128)(2,1)S(1)}, bf16[2,1024,384]{2,1,0:T(8,128)(2,1)S(1)}, bf16[2,1024,384]{2,1,0:T(8,128)(2,1)S(1)}, f32[4,2,384]{2,1,0:T(2,128)S(1)}) custom-call(s32[4]{0:T(128)S(1)} %copy-done.41, s32[1]{0:T(128)} %bitcast.2.tindex, bf16[1024,384]{1,0:T(8,128)(2,1)S(1)} %copy-done.53, bf16[2,1024,384]{2,1,0:T(8,128)(2,1)S(1)} %copy-done.47, ...), custom_call_target="tpu_custom_call" | custom-call | flops 17999998976 | bytes 10000000 | tf_op jit(solution)/shard_map/attend_backward/pallas_call | solution.py:140
  238.2 5.1 %weight_products.2 = (bf16[4,8,48,384]{3,2,1,0:T(8,128)(2,1)S(1)}, bf16[4,8,48,384]{3,2,1,0:T(8,128)(2,1)S(1)}) custom-call(s32[1]{0:T(128)} %bitcast.5.core, bf16[1024,768]{1,0:T(8,128)(2,1)S(1)} %copy-done.10, bf16[1024,768]{1,0:T(8,128)(2,1)S(1)} %copy-done.30, bf16[1024,768]{1,0:T(8,128)(2,1)S(1)} %convert_element_type.300.first_ref, ...), custom_call_target="tpu_custom_call" | custom-call | flops 3623878656 | bytes 10000000 | tf_op jit(solution)/shard_map/weight_products/pallas_call | solution.py:233
  243.4 4.3 %collective-permute-done.15 = bf16[1,4,2,48,1536]{4,3,1,2,0:T(8,128)(2,1)} collective-permute-done((bf16[1,4,2,48,1536]{4,3,1,2,0:T(8,128)(2,1)S(1)}, bf16[1,4,2,48,1536]{4,3,1,2,0:T(8,128)(2,1)}, u32[]{:S(2)}, u32[]{:S(2)}) %collective-permute-start.15) | collective-permute-done | bytes 1179680 | tf_op jit(solution)/shard_map/ppermute | solution.py:318
  255.4 12.8 %attend_backward.3 = (bf16[1024,384]{1,0:T(8,128)(2,1)S(1)}, bf16[2,1024,384]{2,1,0:T(8,128)(2,1)S(1)}, bf16[2,1024,384]{2,1,0:T(8,128)(2,1)S(1)}, f32[4,2,384]{2,1,0:T(2,128)S(1)}) custom-call(s32[4]{0:T(128)S(1)} %copy-done.41, s32[1]{0:T(128)} %bitcast.2.tindex, bf16[1024,384]{1,0:T(8,128)(2,1)S(1)} %copy-done.51, bf16[2,1024,384]{2,1,0:T(8,128)(2,1)S(1)} %copy-done.43, ...), custom_call_target="tpu_custom_call" | custom-call | flops 17999998976 | bytes 10000000 | tf_op jit(solution)/shard_map/attend_backward/pallas_call | solution.py:140
  268.3 4.2 %back_product.3.rest_0_ = bf16[1024,768]{1,0:T(8,128)(2,1)S(1)} custom-call(bf16[2,1024,384]{2,1,0:T(8,128)(2,1)S(1)} %get-tuple-element.58.dk_ref.refs_2_.refs_0_, bf16[2,1024,384]{2,1,0:T(8,128)(2,1)S(1)} %get-tuple-element.63.refs_3_.refs_1_.dk_ref, bf16[2,1024,384]{2,1,0:T(8,128)(2,1)S(1)} %get-tuple-element.59.dv_ref.refs_4_.refs_2_, ...), custom_call_target="tpu_custom_call" | custom-call | flops 2415919104 | bytes 8000000 | tf_op jit(solution)/shard_map/back_product/pallas_call | solution.py:182
  274.5 6.1 %weight_products.3 = (bf16[4,8,48,384]{3,2,1,0:T(8,128)(2,1)S(1)}, bf16[4,8,48,384]{3,2,1,0:T(8,128)(2,1)}) custom-call(s32[1]{0:T(128)} %bitcast.5.core, bf16[1024,768]{1,0:T(8,128)(2,1)S(1)} %copy-done.10, bf16[1024,768]{1,0:T(8,128)(2,1)S(1)} %copy-done.30, bf16[1024,768]{1,0:T(8,128)(2,1)S(1)} %convert_element_type.300.first_ref, ...), custom_call_target="tpu_custom_call" | custom-call | flops 3623878656 | bytes 10000000 | tf_op jit(solution)/shard_map/weight_products/pallas_call | solution.py:233
  280.7 3.7 copy.109
  296.9 5.9 %back_product.2 = f32[1024,768]{1,0:T(8,128)S(1)} custom-call(bf16[1024,384]{1,0:T(8,128)(2,1)S(1)} %copy-done.38, bf16[1024,384]{1,0:T(8,128)(2,1)S(1)} %copy-done.40, bf16[2,1024,384]{2,1,0:T(8,128)(2,1)S(1)} %copy-done.14, bf16[2,1024,384]{2,1,0:T(8,128)(2,1)S(1)} %copy-done.18, bf16[2,1024,384]{2,1,0:T(8,128)(2,1)S(1)} %copy-done.16, ...), custom_call_target="tpu_custom_call" | custom-call | flops 3623878656 | bytes 8000000 | tf_op jit(solution)/shard_map/back_product/pallas_call | solution.py:182
  302.9 11.6 %collective-permute-done.23 = bf16[4,4,48,384]{3,2,1,0:T(8,128)(2,1)S(1)} collective-permute-done((bf16[4,4,48,384]{3,2,1,0:T(8,128)(2,1)S(1)}, bf16[4,4,48,384]{3,2,1,0:T(8,128)(2,1)S(1)}, u32[]{:S(2)}, u32[]{:S(2)}) %collective-permute-start.23) | collective-permute-done | bytes 589856 | tf_op jit(solution)/shard_map/ppermute | solution.py:314
  322.5 11.8 %collective-permute-done.24 = bf16[4,4,48,384]{3,2,1,0:T(8,128)(2,1)S(1)} collective-permute-done((bf16[4,4,48,384]{3,2,1,0:T(8,128)(2,1)S(1)}, bf16[4,4,48,384]{3,2,1,0:T(8,128)(2,1)S(1)}, u32[]{:S(2)}, u32[]{:S(2)}) %collective-permute-start.24) | collective-permute-done | bytes 589856 | tf_op jit(solution)/shard_map/ppermute | solution.py:318
  346.4 4.9 %collective-permute-done.34 = bf16[1,48,1536]{2,1,0:T(8,128)(2,1)S(1)} collective-permute-done((bf16[1,48,1536]{2,1,0:T(8,128)(2,1)}, bf16[1,48,1536]{2,1,0:T(8,128)(2,1)S(1)}, u32[]{:S(2)}, u32[]{:S(2)}) %collective-permute-start.34) | collective-permute-done | bytes 147488 | tf_op jit(solution)/shard_map/ppermute | solution.py:314
  (386 shorter events, 177.7 us)
Async XLA Ops:
  7.2 138.2 %all-gather.2.cloned.1.call-start = ((), (), s32[]{:S(2)}) async-start(), calls=%async_computation | async-start | bytes 9732096 | tf_op jit(solution)/shard_map/all_gather | solution.py:438
  13.3 45.8 %collective-permute-start = (bf16[1024,768]{1,0:T(8,128)(2,1)S(1)}, bf16[1024,768]{1,0:T(8,128)(2,1)S(1)}, u32[]{:S(2)}, u32[]{:S(2)}) collective-permute-start(bf16[1024,768]{1,0:T(8,128)(2,1)S(1)} %bitcast_convert_fusion.refs_2_.own_ref), channel_id=1, source_target_pairs={{0,1},{1,0},{2,3},{3,2},{4,5},{5,4},{6,7},{7,6},{8,9},{9,8},{10,11... | collective-permute-start | bytes 4718600 | tf_op jit(solution)/shard_map/ppermute | solution.py:318
  41.2 43.3 %collective-permute-start.11 = (bf16[2,4,2,48,384]{4,3,2,1,0:T(8,128)(2,1)}, bf16[2,4,2,48,384]{4,3,2,1,0:T(8,128)(2,1)}, u32[]{:S(2)}, u32[]{:S(2)}) collective-permute-start(bf16[2,4,2,48,384]{4,3,2,1,0:T(8,128)(2,1)} %get-tuple-element.108), channel_id=1, source_target_pairs={{0,1},{1,0},{2,3},{3,2},{4,5},{5,4},{6,7},{7,6},{8,9},{9,8},{10,11... | collective-permute-start | bytes 1769480 | tf_op jit(solution)/shard_map/ppermute | solution.py:318
  62.6 19.5 %collective-permute-start.4 = (bf16[4,2,48,384]{3,2,1,0:T(8,128)(2,1)}, bf16[4,2,48,384]{3,2,1,0:T(8,128)(2,1)S(1)}, u32[]{:S(2)}, u32[]{:S(2)}) collective-permute-start(bf16[4,2,48,384]{3,2,1,0:T(8,128)(2,1)} %pack_shards.7), channel_id=1, source_target_pairs={{0,1},{1,0},{2,3},{3,2},{4,5},{5,4},{6,7},{7,6},{8,9},{9,8},{10,11... | collective-permute-start | bytes 884744 | tf_op jit(solution)/shard_map/ppermute | solution.py:318
  83.2 18.0 %collective-permute-start.5 = (bf16[2,4,2,48,384]{4,3,2,1,0:T(8,128)(2,1)S(1)}, bf16[2,4,2,48,384]{4,3,2,1,0:T(8,128)(2,1)S(1)}, u32[]{:S(2)}, u32[]{:S(2)}) collective-permute-start(bf16[2,4,2,48,384]{4,3,2,1,0:T(8,128)(2,1)S(1)} %pad_maximum_fusion.3.refs_0_), channel_id=1, source_target_pairs={{0,4},{2,6},{4,0},{6,2},{8,12},{10,14},{12,8},{14,10},{16,20},{18,... | collective-permute-start | bytes 1769480 | tf_op jit(solution)/shard_map/ppermute | solution.py:314
  85.9 20.9 %collective-permute-start.12 = (bf16[2,2,4,2,48,384]{5,4,3,2,1,0:T(8,128)(2,1)S(1)}, bf16[2,2,4,2,48,384]{5,4,3,2,1,0:T(8,128)(2,1)S(1)}, u32[]{:S(2)}, u32[]{:S(2)}) collective-permute-start(bf16[2,2,4,2,48,384]{5,4,3,2,1,0:T(8,128)(2,1)S(1)} %pad_maximum_fusion.2.mine_ref), channel_id=1, source_target_pairs={{0,2},{2,0},{4,6},{6,4},{8,10},{10,8},{12,14},{14,12},{16,18},{18,... | collective-permute-start | bytes 3538952 | tf_op jit(solution)/shard_map/ppermute | solution.py:314
  194.9 23.7 %collective-permute-start.13 = (bf16[2,1,4,2,48,1536]{5,4,2,3,1,0:T(8,128)(2,1)}, bf16[2,1,4,2,48,1536]{5,4,2,3,1,0:T(8,128)(2,1)S(1)}, u32[]{:S(2)}, u32[]{:S(2)}) collective-permute-start(bf16[2,1,4,2,48,1536]{5,4,2,3,1,0:T(8,128)(2,1)} %pad_maximum_fusion), channel_id=1, source_target_pairs={{0,2},{2,0},{4,6},{6,4},{8,10},{10,8},{12,14},{14,12},{16,18},{18,... | collective-permute-start | bytes 7077896 | tf_op jit(solution)/shard_map/ppermute | solution.py:314
  205.1 16.0 %collective-permute-start.14 = (bf16[2,1,4,2,48,1536]{5,4,2,0,3,1:T(8,128)(2,1)}, bf16[2,1,4,2,48,1536]{5,4,2,0,3,1:T(8,128)(2,1)S(1)}, u32[]{:S(2)}, u32[]{:S(2)}) collective-permute-start(bf16[2,1,4,2,48,1536]{5,4,2,0,3,1:T(8,128)(2,1)} %pad_maximum_fusion.1), channel_id=1, source_target_pairs={{0,2},{2,0},{4,6},{6,4},{8,10},{10,8},{12,14},{14,12},{16,18},{18,... | collective-permute-start | bytes 7077896 | tf_op jit(solution)/shard_map/ppermute | solution.py:314
  219.6 28.1 %collective-permute-start.15 = (bf16[1,4,2,48,1536]{4,3,1,2,0:T(8,128)(2,1)S(1)}, bf16[1,4,2,48,1536]{4,3,1,2,0:T(8,128)(2,1)}, u32[]{:S(2)}, u32[]{:S(2)}) collective-permute-start(bf16[1,4,2,48,1536]{4,3,1,2,0:T(8,128)(2,1)S(1)} %dynamic-slice_bitcast_fusion.1), channel_id=1, source_target_pairs={{0,1},{1,0},{2,3},{3,2},{4,5},{5,4},{6,7},{7,6},{8,9},{9,8},{10,11... | collective-permute-start | bytes 3538952 | tf_op jit(solution)/shard_map/ppermute | solution.py:318
  223.2 27.8 %collective-permute-start.16 = (bf16[2,1,4,48,1536]{4,3,2,1,0:T(8,128)(2,1)S(1)}, bf16[2,1,4,48,1536]{4,3,2,1,0:T(8,128)(2,1)}, u32[]{:S(2)}, u32[]{:S(2)}) collective-permute-start(bf16[2,1,4,48,1536]{4,3,2,1,0:T(8,128)(2,1)S(1)} %dynamic-slice_bitcast_fusion), channel_id=1, source_target_pairs={{0,4},{2,6},{4,0},{6,2},{8,12},{10,14},{12,8},{14,10},{16,20},{18,... | collective-permute-start | bytes 3538952 | tf_op jit(solution)/shard_map/ppermute | solution.py:314
  249.4 23.1 %collective-permute-start.20 = (bf16[1,4,48,1536]{3,2,1,0:T(8,128)(2,1)S(1)}, bf16[1,4,48,1536]{3,2,1,0:T(8,128)(2,1)}, u32[]{:S(2)}, u32[]{:S(2)}) collective-permute-start(bf16[1,4,48,1536]{3,2,1,0:T(8,128)(2,1)S(1)} %dynamic-slice_bitcast_fusion.4), channel_id=1, source_target_pairs={{0,4},{2,6},{4,0},{6,2},{8,12},{10,14},{12,8},{14,10},{16,20},{18,... | collective-permute-start | bytes 1769480 | tf_op jit(solution)/shard_map/ppermute | solution.py:314
  252.7 21.5 %collective-permute-start.21 = (bf16[1,4,48,1536]{3,2,1,0:T(8,128)(2,1)S(1)}, bf16[1,4,48,1536]{3,2,1,0:T(8,128)(2,1)S(1)}, u32[]{:S(2)}, u32[]{:S(2)}) collective-permute-start(bf16[1,4,48,1536]{3,2,1,0:T(8,128)(2,1)S(1)} %dynamic-slice_bitcast_fusion.3), channel_id=1, source_target_pairs={{0,1},{1,0},{2,3},{3,2},{4,5},{5,4},{6,7},{7,6},{8,9},{9,8},{10,11... | collective-permute-start | bytes 1769480 | tf_op jit(solution)/shard_map/ppermute | solution.py:318
  284.6 77.0 %collective-permute-start.18 = (bf16[1024,768]{1,0:T(8,128)(2,1)}, bf16[1024,768]{1,0:T(8,128)(2,1)}, u32[]{:S(2)}, u32[]{:S(2)}) collective-permute-start(bf16[1024,768]{1,0:T(8,128)(2,1)} %copy-done.31), channel_id=1, source_target_pairs={{0,1},{1,0},{2,3},{3,2},{4,5},{5,4},{6,7},{7,6},{8,9},{9,8},{10,11... | collective-permute-start | bytes 4718600 | tf_op jit(solution)/shard_map/ppermute | solution.py:318
  286.2 16.7 %collective-permute-start.19 = (bf16[4,4,48,384]{3,2,1,0:T(8,128)(2,1)S(1)}, bf16[4,4,48,384]{3,2,1,0:T(8,128)(2,1)S(1)}, u32[]{:S(2)}, u32[]{:S(2)}) collective-permute-start(bf16[4,4,48,384]{3,2,1,0:T(8,128)(2,1)S(1)} %dynamic-slice_bitcast_fusion.5), channel_id=1, source_target_pairs={{0,4},{2,6},{4,0},{6,2},{8,12},{10,14},{12,8},{14,10},{16,20},{18,... | collective-permute-start | bytes 1769480 | tf_op jit(solution)/shard_map/ppermute | solution.py:314
  290.0 24.4 %collective-permute-start.23 = (bf16[4,4,48,384]{3,2,1,0:T(8,128)(2,1)S(1)}, bf16[4,4,48,384]{3,2,1,0:T(8,128)(2,1)S(1)}, u32[]{:S(2)}, u32[]{:S(2)}) collective-permute-start(bf16[4,4,48,384]{3,2,1,0:T(8,128)(2,1)S(1)} %dynamic-slice_bitcast_fusion.2), channel_id=1, source_target_pairs={{0,4},{2,6},{4,0},{6,2},{8,12},{10,14},{12,8},{14,10},{16,20},{18,... | collective-permute-start | bytes 1769480 | tf_op jit(solution)/shard_map/ppermute | solution.py:314
  314.7 19.5 %collective-permute-start.24 = (bf16[4,4,48,384]{3,2,1,0:T(8,128)(2,1)S(1)}, bf16[4,4,48,384]{3,2,1,0:T(8,128)(2,1)S(1)}, u32[]{:S(2)}, u32[]{:S(2)}) collective-permute-start(bf16[4,4,48,384]{3,2,1,0:T(8,128)(2,1)S(1)} %broadcast_select_fusion), channel_id=1, source_target_pairs={{0,1},{1,0},{2,3},{3,2},{4,5},{5,4},{6,7},{7,6},{8,9},{9,8},{10,11... | collective-permute-start | bytes 1769480 | tf_op jit(solution)/shard_map/ppermute | solution.py:318
  317.3 21.1 %collective-permute-start.36 = (bf16[1,48,1536]{2,1,0:T(8,128)(2,1)}, bf16[1,48,1536]{2,1,0:T(8,128)(2,1)S(1)}, u32[]{:S(2)}, u32[]{:S(2)}) collective-permute-start(bf16[1,48,1536]{2,1,0:T(8,128)(2,1)} %get-tuple-element.98), channel_id=1, source_target_pairs={{0,8},{2,10},{4,12},{6,14},{8,0},{10,2},{12,4},{14,6},{16,24},{18,... | collective-permute-start | bytes 442376 | tf_op jit(solution)/shard_map/ppermute | solution.py:314
  318.7 22.1 %collective-permute-start.37 = (bf16[1,48,1536]{2,1,0:T(8,128)(2,1)}, bf16[1,48,1536]{2,1,0:T(8,128)(2,1)}, u32[]{:S(2)}, u32[]{:S(2)}) collective-permute-start(bf16[1,48,1536]{2,1,0:T(8,128)(2,1)} %get-tuple-element.100), channel_id=1, source_target_pairs={{0,16},{2,18},{4,20},{6,22},{8,24},{10,26},{12,28},{14,30},{16,0},... | collective-permute-start | bytes 442376 | tf_op jit(solution)/shard_map/ppermute | solution.py:314
  321.1 20.3 %collective-permute-start.38 = (bf16[1,48,1536]{2,1,0:T(8,128)(2,1)}, bf16[1,48,1536]{2,1,0:T(8,128)(2,1)}, u32[]{:S(2)}, u32[]{:S(2)}) collective-permute-start(bf16[1,48,1536]{2,1,0:T(8,128)(2,1)} %get-tuple-element.99), channel_id=1, source_target_pairs={{0,24},{2,26},{4,28},{6,30},{8,16},{10,18},{12,20},{14,22},{16,8},... | collective-permute-start | bytes 442376 | tf_op jit(solution)/shard_map/ppermute | solution.py:314
  334.3 12.1 %collective-permute-start.33 = (bf16[1,48,1536]{2,1,0:T(8,128)(2,1)}, bf16[1,48,1536]{2,1,0:T(8,128)(2,1)S(1)}, u32[]{:S(2)}, u32[]{:S(2)}) collective-permute-start(bf16[1,48,1536]{2,1,0:T(8,128)(2,1)} %get-tuple-element.101), channel_id=1, source_target_pairs={{0,8},{2,10},{4,12},{6,14},{8,0},{10,2},{12,4},{14,6},{16,24},{18,... | collective-permute-start | bytes 442376 | tf_op jit(solution)/shard_map/ppermute | solution.py:314
  338.4 12.8 %collective-permute-start.34 = (bf16[1,48,1536]{2,1,0:T(8,128)(2,1)}, bf16[1,48,1536]{2,1,0:T(8,128)(2,1)S(1)}, u32[]{:S(2)}, u32[]{:S(2)}) collective-permute-start(bf16[1,48,1536]{2,1,0:T(8,128)(2,1)} %get-tuple-element.103), channel_id=1, source_target_pairs={{0,16},{2,18},{4,20},{6,22},{8,24},{10,26},{12,28},{14,30},{16,0},... | collective-permute-start | bytes 442376 | tf_op jit(solution)/shard_map/ppermute | solution.py:314
  354.4 16.1 %collective-permute-start.25 = (bf16[4,48,384]{2,1,0:T(8,128)(2,1)S(1)}, bf16[4,48,384]{2,1,0:T(8,128)(2,1)S(1)}, u32[]{:S(2)}, u32[]{:S(2)}) collective-permute-start(bf16[4,48,384]{2,1,0:T(8,128)(2,1)S(1)} %get-tuple-element.104), channel_id=1, source_target_pairs={{0,8},{2,10},{4,12},{6,14},{8,0},{10,2},{12,4},{14,6},{16,24},{18,... | collective-permute-start | bytes 442376 | tf_op jit(solution)/shard_map/ppermute | solution.py:314
  358.0 13.0 %collective-permute-start.26 = (bf16[4,48,384]{2,1,0:T(8,128)(2,1)S(1)}, bf16[4,48,384]{2,1,0:T(8,128)(2,1)S(1)}, u32[]{:S(2)}, u32[]{:S(2)}) collective-permute-start(bf16[4,48,384]{2,1,0:T(8,128)(2,1)S(1)} %get-tuple-element.106), channel_id=1, source_target_pairs={{0,16},{2,18},{4,20},{6,22},{8,24},{10,26},{12,28},{14,30},{16,0},... | collective-permute-start | bytes 442376 | tf_op jit(solution)/shard_map/ppermute | solution.py:314
  359.0 12.1 %collective-permute-start.27 = (bf16[4,48,384]{2,1,0:T(8,128)(2,1)S(1)}, bf16[4,48,384]{2,1,0:T(8,128)(2,1)S(1)}, u32[]{:S(2)}, u32[]{:S(2)}) collective-permute-start(bf16[4,48,384]{2,1,0:T(8,128)(2,1)S(1)} %get-tuple-element.105), channel_id=1, source_target_pairs={{0,24},{2,26},{4,28},{6,30},{8,16},{10,18},{12,20},{14,22},{16,8},... | collective-permute-start | bytes 442376 | tf_op jit(solution)/shard_map/ppermute | solution.py:314
  (116 other events, 941.4 us)
Sparse Core Ops, SparseCore 0:
  11.5 96.8 all-gather.1
